TPU v7x, 32 devices: a whole 2x2x4 slice. The times are simulated.
32 devices in a mesh: fsdp: 32 (over z, y, x, core).
Axes of the slice: x: 2, y: 2, z: 4, core: 2. Of those that a mesh axis runs over, the one named last changes fastest.
Arguments:
- patches: bfloat16 [64, 197, 768], P('fsdp'), may hold values from -6 to 6
- live_count: int32 [32], P('fsdp'), may hold values from 1 to 2, 48 in all
- expert_ids: int32 [12608, 2], P('fsdp'), may hold values from 0 to 3, all different within a row; in each aligned block of 394 rows (0 to 393, 394 to 787, ...) at most 247 rows name the same one
- attn_gain: bfloat16 [768, 2], P('fsdp'), may hold values from 0.099609375 to 1.8984375
- attn_qkv: bfloat16 [768, 2, 2304], P('fsdp'), may hold values from -0.21875 to 0.21875
- attn_out: bfloat16 [768, 2, 768], P('fsdp'), may hold values from -1.25 to 1.25
- mlp_gain: bfloat16 [768], P('fsdp'), may hold values from 0.099609375 to 1.8984375
- mlp_in: bfloat16 [768, 3072], P('fsdp'), may hold values from -0.21875 to 0.21875
- mlp_out: bfloat16 [3072, 768], P('fsdp'), may hold values from -0.15625 to 0.15625
- moe_gain: bfloat16 [768], P('fsdp'), may hold values from 0.099609375 to 1.8984375
- router: bfloat16 [768, 4], P('fsdp'), may hold values from -0.15625 to 0.15625
- expert_in: bfloat16 [768, 4, 3072], P('fsdp'), may hold values from -0.21875 to 0.21875
- expert_out: bfloat16 [3072, 4, 768], P('fsdp'), may hold values from -0.21875 to 0.21875
- cotangent: bfloat16 [64, 197, 768], P('fsdp'), may hold values from -6 to 6
Outputs:
- block_out: bfloat16 [64, 197, 768], P('fsdp')
- input_grad: float32 [64, 197, 768], P('fsdp')
- grad_attn_gain: float32 [768, 2], P('fsdp')
- grad_attn_qkv: float32 [768, 2, 2304], P('fsdp')
- grad_attn_out: float32 [768, 2, 768], P('fsdp')
- grad_mlp_gain: float32 [768], P('fsdp')
- grad_mlp_in: float32 [768, 3072], P('fsdp')
- grad_mlp_out: float32 [3072, 768], P('fsdp')
- grad_moe_gain: float32 [768], P('fsdp')
- grad_router: float32 [768, 4], P('fsdp')
- grad_expert_in: float32 [768, 4, 3072], P('fsdp')
- grad_expert_out: float32 [3072, 4, 768], P('fsdp')
Inputs may be any that keep to these rules, and one draw needn't show every extreme that they name: `live_count`: each device holds 1 to 2 live images in its first slots, 48 in all, and some device holds 2. `expert_ids`: each token names 2 different experts; of the 394 tokens of one device at most 247 name the same expert, and some device reaches 247.
All inputs are finite; a program needn't handle non-finite values.
Results may differ from a plain program's by a relative error of at most 0.023.
Values may be sent and summed in bfloat16 or wider, within the bound.
A program may use at most 384 MiB of HBM per device.

v0:
```python
import jax
import jax.numpy as jnp
from jax import lax
from jax.sharding import PartitionSpec as P

HEADS = 12
HEAD_DIM = 64
EXPERTS = 4
CAP = 247


NORM_EPSILON = 1e-06


def from_partner(array, axis, apart):
    return lax.ppermute(array, axis, [(i, i ^ 1 << apart) for i in range(lax.axis_size(axis))])


def from_behind(value, axis, steps):
    count = lax.axis_size(axis)
    pairs = [(source, (source + steps) % count) for source in range(count)]
    return lax.ppermute(value, axis, pairs)


def layer_norm(residual, norm_gain):
    center = residual - jnp.mean(residual, -1, keepdims=True)
    spread = jnp.mean(center * center, -1, keepdims=True)
    return center * lax.rsqrt(spread + NORM_EPSILON) * norm_gain


def gelu_tanh(values):
    return jax.nn.gelu(values, approximate=True)


def router_softmax(values):
    return jax.nn.softmax(values, axis=-1)


def cross_rows(left, right):
    return jnp.einsum("rd,re->de", left, right, preferred_element_type=jnp.float32)


def halve_sum(flat):
    device_total = lax.axis_size("fsdp")
    device_id = lax.axis_index("fsdp")
    held = flat
    for bit in reversed(range(device_total.bit_length() - 1)):
        half = 1 << bit
        lower_part = held[:half]
        upper_part = held[half:]
        upper = device_id // half % 2 == 1
        sent = jnp.where(upper, lower_part, upper_part)
        staying = jnp.where(upper, upper_part, lower_part)
        held = staying + from_partner(sent.astype(jnp.bfloat16), "fsdp", bit).astype(sent.dtype)
    return held[0]


def reduce_owned(grads):
    device_total = lax.axis_size("fsdp")
    flats = [grad.reshape(device_total, -1) for grad in grads]
    owned = halve_sum(jnp.concatenate(flats, 1))
    results = []
    begin_at = 0
    for grad, flat in zip(grads, flats):
        length = flat.shape[1]
        results.append(
            owned[begin_at : begin_at + length].reshape(
                (grad.shape[0] // device_total,) + grad.shape[1:]
            )
        )
        begin_at = begin_at + length
    return results


def fetch_attention(attn_gain, attn_qkv, attn_out, which_layer):
    return (
        lax.all_gather(attn_gain[:, which_layer], "fsdp", axis=0, tiled=True),
        lax.all_gather(attn_qkv[:, which_layer], "fsdp", axis=0, tiled=True),
        lax.all_gather(attn_out[:, which_layer], "fsdp", axis=0, tiled=True),
    )


def refetch_attention(attn_gain, attn_qkv, attn_out, which_layer):
    return (
        lax.all_gather(attn_gain[:, which_layer], "fsdp", axis=0, tiled=True),
        lax.all_gather(attn_qkv[:, which_layer], "fsdp", axis=0, tiled=True),
        lax.all_gather(attn_out[:, which_layer], "fsdp", axis=0, tiled=True),
    )


def narrow_shift(values, offset):
    return from_behind(values, "fsdp", offset)


def wide_shift(values, offset):
    return from_behind(values.astype(jnp.bfloat16), "fsdp", offset).astype(values.dtype)


def order_by_group(stacked, group_id):
    index = (group_id - jnp.arange(EXPERTS, dtype=jnp.int32)) % EXPERTS
    return jnp.take(stacked, index, axis=0)


def expert_piece(weight, offset, group_id):
    return lax.dynamic_index_in_dim(
        weight, (group_id + offset) % EXPERTS, 1, keepdims=False
    ).reshape(-1)


def collect_expert(w_in, w_out, group_id, rank_id, group_size):
    pieces = []
    for offset in range(EXPERTS):
        piece = jnp.stack(
            [expert_piece(w_in, offset, group_id), expert_piece(w_out, offset, group_id)]
        )
        if offset > 0:
            piece = narrow_shift(piece, offset * group_size)
        pieces.append(piece)
    held = order_by_group(jnp.stack(pieces), group_id)[:, None]
    for bit in range(group_size.bit_length() - 1):
        other = from_partner(held, "fsdp", bit)
        upper = rank_id // (1 << bit) % 2 == 1
        held = jnp.where(
            upper, jnp.concatenate([other, held], 1), jnp.concatenate([held, other], 1)
        )
    flat = jnp.moveaxis(held, 2, 0).reshape(2, -1)
    return (flat[0].reshape(-1, w_in.shape[2]), flat[1].reshape(-1, w_out.shape[2]))


def reduce_expert(grad_inner, grad_outer, group_id, rank_id, group_size, in_shape, out_shape):
    flat = jnp.stack([grad_inner.reshape(-1), grad_outer.reshape(-1)])
    held = jnp.moveaxis(flat.reshape(2, EXPERTS, group_size, -1), 0, 2)
    for bit in reversed(range(group_size.bit_length() - 1)):
        half = 1 << bit
        lower_part = held[:, :half]
        upper_part = held[:, half:]
        upper = rank_id // half % 2 == 1
        sent = jnp.where(upper, lower_part, upper_part)
        staying = jnp.where(upper, upper_part, lower_part)
        held = staying + from_partner(sent.astype(jnp.bfloat16), "fsdp", bit).astype(sent.dtype)
    owned = held[:, 0]
    pieces = []
    for offset in range(EXPERTS):
        piece = lax.dynamic_index_in_dim(owned, (group_id + offset) % EXPERTS, 0, keepdims=False)
        if offset > 0:
            piece = wide_shift(piece, offset * group_size)
        pieces.append(piece)
    result = order_by_group(jnp.stack(pieces), group_id)
    grad_in_shard = result[:, 0].reshape(EXPERTS, in_shape[0], in_shape[2]).transpose(1, 0, 2)
    grad_out_shard = result[:, 1].reshape(EXPERTS, out_shape[0], out_shape[2]).transpose(1, 0, 2)
    return (grad_in_shard, grad_out_shard)


def spread_rows(rows, group_id, group_size):
    buffers = []
    for offset in range(EXPERTS):
        buffer = lax.dynamic_index_in_dim(rows, (group_id + offset) % EXPERTS, 0, keepdims=False)
        if offset > 0:
            buffer = narrow_shift(buffer, offset * group_size)
        buffers.append(buffer)
    return jnp.stack(buffers)


def return_rows(results, group_id, group_size, mover):
    buffers = []
    for offset in range(EXPERTS):
        buffer = results[offset]
        if offset > 0:
            buffer = mover(buffer, (EXPERTS - offset) * group_size)
        buffers.append(buffer)
    index = (jnp.arange(EXPERTS, dtype=jnp.int32) - group_id) % EXPERTS
    return jnp.take(jnp.stack(buffers), index, axis=0)


def split_heads(mixed_qkv, slot_count):
    split_qkv = mixed_qkv.reshape(slot_count, -1, 3, HEADS, HEAD_DIM)
    return (split_qkv[:, :, 0], split_qkv[:, :, 1], split_qkv[:, :, 2])


def head_scores(queries, key_rows):
    return jnp.einsum(
        "bqhd,bkhd->bhqk", queries, key_rows, preferred_element_type=jnp.float32
    ) * HEAD_DIM ** (-0.5)


def attention_forward(residual, weights, slot_count):
    norm_gain, w_qkv, w_out = weights
    normed = layer_norm(residual, norm_gain.astype(jnp.float32)).astype(jnp.bfloat16)
    mixed_qkv = jnp.dot(normed, w_qkv, preferred_element_type=jnp.float32).astype(jnp.bfloat16)
    queries, key_rows, value_rows = split_heads(mixed_qkv, slot_count)
    scores = head_scores(queries, key_rows)
    top_score = jnp.max(scores, -1, keepdims=True)
    log_total = top_score + jnp.log(jnp.sum(jnp.exp(scores - top_score), -1, keepdims=True))
    probs_low = jnp.exp(scores - log_total).astype(jnp.bfloat16)
    context = jnp.einsum(
        "bhqk,bkhd->bqhd", probs_low, value_rows, preferred_element_type=jnp.float32
    )
    context = context.reshape(residual.shape).astype(jnp.bfloat16)
    branch = jnp.dot(context, w_out, preferred_element_type=jnp.float32)
    return (branch, (normed, mixed_qkv, log_total, context))


def attention_backward(upstream, residual, weights, kept_forward, slot_count):
    norm_gain, w_qkv, w_out = weights
    normed, mixed_qkv, log_total, context = kept_forward
    upstream_low = upstream.astype(jnp.bfloat16)
    grad_outer = cross_rows(context, upstream_low)
    grad_context = jnp.dot(upstream_low, w_out.T, preferred_element_type=jnp.float32).astype(
        jnp.bfloat16
    )
    grad_context = grad_context.reshape(slot_count, -1, HEADS, HEAD_DIM)
    queries, key_rows, value_rows = split_heads(mixed_qkv, slot_count)
    attn_probs = jnp.exp(head_scores(queries, key_rows) - log_total)
    grad_probs = jnp.einsum(
        "bqhd,bkhd->bhqk", grad_context, value_rows, preferred_element_type=jnp.float32
    )
    grad_values = jnp.einsum(
        "bhqk,bqhd->bkhd",
        attn_probs.astype(jnp.bfloat16),
        grad_context,
        preferred_element_type=jnp.float32,
    )
    row_inner = jnp.sum(grad_probs * attn_probs, -1, keepdims=True)
    grad_scores = (attn_probs * (grad_probs - row_inner)).astype(jnp.bfloat16)
    grad_queries = jnp.einsum(
        "bhqk,bkhd->bqhd", grad_scores, key_rows, preferred_element_type=jnp.float32
    ) * HEAD_DIM ** (-0.5)
    grad_keys = jnp.einsum(
        "bhqk,bqhd->bkhd", grad_scores, queries, preferred_element_type=jnp.float32
    ) * HEAD_DIM ** (-0.5)
    grad_mixed = (
        jnp.stack([grad_queries, grad_keys, grad_values], axis=2)
        .reshape(residual.shape[0], -1)
        .astype(jnp.bfloat16)
    )
    grad_qkv = cross_rows(normed, grad_mixed)
    grad_normed = jnp.dot(grad_mixed, w_qkv.T, preferred_element_type=jnp.float32)
    _, norm_pull = jax.vjp(layer_norm, residual, norm_gain.astype(jnp.float32))
    grad_resid, grad_gain = norm_pull(grad_normed)
    return (upstream + grad_resid, (grad_gain, grad_qkv, grad_outer))


def mlp_forward(residual, weights):
    norm_gain, w_in, w_out = weights
    normed = layer_norm(residual, norm_gain.astype(jnp.float32)).astype(jnp.bfloat16)
    hidden = jnp.dot(normed, w_in, preferred_element_type=jnp.float32)
    active = gelu_tanh(hidden).astype(jnp.bfloat16)
    branch = jnp.dot(active, w_out, preferred_element_type=jnp.float32)
    return (branch, (normed, hidden, active))


def mlp_backward(upstream, residual, weights, kept_forward):
    norm_gain, w_in, w_out = weights
    normed, hidden, active = kept_forward
    upstream_low = upstream.astype(jnp.bfloat16)
    grad_outer = cross_rows(active, upstream_low)
    grad_active = jnp.dot(upstream_low, w_out.T, preferred_element_type=jnp.float32)
    _, gelu_pull = jax.vjp(gelu_tanh, hidden)
    grad_hidden = gelu_pull(grad_active)[0].astype(jnp.bfloat16)
    grad_inner = cross_rows(normed, grad_hidden)
    grad_normed = jnp.dot(grad_hidden, w_in.T, preferred_element_type=jnp.float32)
    _, norm_pull = jax.vjp(layer_norm, residual, norm_gain.astype(jnp.float32))
    grad_resid, grad_gain = norm_pull(grad_normed)
    return (upstream + grad_resid, (grad_gain, grad_inner, grad_outer))


def one_expert_forward(expert_rows, w_in_one, w_out_one, group_id, group_size):
    received = spread_rows(expert_rows, group_id, group_size)
    flat_rows = received.reshape(-1, received.shape[2])
    hidden = jnp.dot(flat_rows, w_in_one, preferred_element_type=jnp.float32)
    active = gelu_tanh(hidden).astype(jnp.bfloat16)
    produced = jnp.dot(active, w_out_one, preferred_element_type=jnp.float32).astype(jnp.bfloat16)
    returned = return_rows(produced.reshape(received.shape), group_id, group_size, narrow_shift)
    return (returned, (flat_rows, hidden, active))


def one_expert_backward(grad_produced, kept_experts, w_in_one, w_out_one, group_id, group_size):
    flat_rows, hidden, active = kept_experts
    received = spread_rows(grad_produced, group_id, group_size)
    grad_flat = received.reshape(-1, received.shape[2])
    grad_outer = cross_rows(active, grad_flat)
    grad_active = jnp.dot(grad_flat, w_out_one.T, preferred_element_type=jnp.float32)
    _, gelu_pull = jax.vjp(gelu_tanh, hidden)
    grad_hidden = gelu_pull(grad_active)[0].astype(jnp.bfloat16)
    grad_inner = cross_rows(flat_rows, grad_hidden)
    grad_rows = jnp.dot(grad_hidden, w_in_one.T, preferred_element_type=jnp.float32).reshape(
        received.shape
    )
    grad_rows = return_rows(grad_rows, group_id, group_size, wide_shift)
    return (grad_rows, (grad_inner, grad_outer))


def moe_forward(residual, expert_ids, small_weights, run_experts):
    norm_gain, router = small_weights
    normed = layer_norm(residual, norm_gain.astype(jnp.float32)).astype(jnp.bfloat16)
    logits = jnp.dot(normed, router, preferred_element_type=jnp.float32)
    chances = router_softmax(logits)
    expert_range = jnp.arange(EXPERTS, dtype=jnp.int32)
    chosen_int = (expert_ids[:, :, None] == expert_range).astype(jnp.int32)
    chosen = chosen_int.astype(jnp.float32)
    gate_values = jnp.sum(chances[:, None, :] * chosen, -1)
    per_token = jnp.sum(chosen_int, 1)
    earlier = jnp.cumsum(per_token, 0) - per_token
    placed = jnp.sum(chosen_int * earlier[:, None, :], -1)
    slot_of = expert_ids * CAP + placed
    slot_range = jnp.arange(EXPERTS * CAP, dtype=jnp.int32)
    dispatch = jnp.any(slot_of[None, :, :] == slot_range[:, None, None], -1).astype(jnp.bfloat16)
    expert_rows = jnp.dot(dispatch, normed, preferred_element_type=jnp.float32).astype(jnp.bfloat16)
    expert_rows = expert_rows.reshape(EXPERTS, CAP, -1)
    produced, kept_experts = run_experts(expert_rows)
    produced = produced.reshape(EXPERTS * CAP, -1)
    picked = jnp.take(produced, slot_of, axis=0)
    branch = jnp.sum(gate_values[:, :, None] * picked.astype(jnp.float32), 1)
    return (branch, (normed, logits, chosen, gate_values, slot_of, picked, kept_experts))


def moe_backward(upstream, residual, small_weights, kept_forward, back_experts):
    norm_gain, router = small_weights
    normed, logits, chosen, gate_values, slot_of, picked, kept_experts = kept_forward
    grad_gates = jnp.sum(upstream[:, None, :] * picked.astype(jnp.float32), -1)
    grad_chances = jnp.sum(grad_gates[:, :, None] * chosen, 1)
    _, soft_pull = jax.vjp(router_softmax, logits)
    grad_logits = soft_pull(grad_chances)[0].astype(jnp.bfloat16)
    grad_router = cross_rows(normed, grad_logits)
    scaled = (gate_values[:, :, None] * upstream[:, None, :]).astype(jnp.bfloat16)
    slot_range = jnp.arange(EXPERTS * CAP, dtype=jnp.int32)
    selector = (slot_of[:, :, None] == slot_range).astype(jnp.bfloat16)
    grad_produced = jnp.einsum(
        "rks,rkd->sd", selector, scaled, preferred_element_type=jnp.float32
    ).astype(jnp.bfloat16)
    grad_produced = grad_produced.reshape(EXPERTS, CAP, -1)
    grad_rows, large_grads = back_experts(grad_produced, kept_experts)
    grad_rows = grad_rows.reshape(EXPERTS * CAP, -1)
    grad_normed = jnp.sum(jnp.take(grad_rows, slot_of, axis=0), 1)
    grad_normed = grad_normed + jnp.dot(grad_logits, router.T, preferred_element_type=jnp.float32)
    _, norm_pull = jax.vjp(layer_norm, residual, norm_gain.astype(jnp.float32))
    grad_resid, grad_gain = norm_pull(grad_normed)
    return (upstream + grad_resid, (grad_gain, grad_router), large_grads)


def local(
    patches,
    live_count,
    expert_ids,
    attn_gain,
    attn_qkv,
    attn_out,
    mlp_gain,
    mlp_in,
    mlp_out,
    moe_gain,
    router,
    expert_in,
    expert_out,
    cotangent,
):
    slot_count, seq_len, width = patches.shape
    row_count = slot_count * seq_len
    device_total = lax.axis_size("fsdp")
    group_size = device_total // EXPERTS
    device_id = lax.axis_index("fsdp")
    group_id = device_id // group_size
    rank_id = device_id % group_size
    alive_slots = (jnp.arange(slot_count, dtype=jnp.int32) < live_count[0]).astype(jnp.float32)
    alive_rows = jnp.repeat(alive_slots, seq_len)[:, None]
    resid_zero = patches.astype(jnp.float32).reshape(row_count, width)
    first_attn = fetch_attention(attn_gain, attn_qkv, attn_out, 0)
    branch_one, kept_one = attention_forward(resid_zero, first_attn, slot_count)
    resid_one = resid_zero + branch_one
    gathered_mlp = (
        lax.all_gather(mlp_gain, "fsdp", axis=0, tiled=True),
        lax.all_gather(mlp_in, "fsdp", axis=0, tiled=True),
        lax.all_gather(mlp_out, "fsdp", axis=0, tiled=True),
        lax.all_gather(moe_gain, "fsdp", axis=0, tiled=True),
        lax.all_gather(router, "fsdp", axis=0, tiled=True),
    )
    mlp_weights = (gathered_mlp[0], gathered_mlp[1], gathered_mlp[2])
    small_moe = (gathered_mlp[3], gathered_mlp[4])
    branch_two, kept_two = mlp_forward(resid_one, mlp_weights)
    resid_two = resid_one + branch_two
    second_attn = fetch_attention(attn_gain, attn_qkv, attn_out, 1)
    branch_three, kept_three = attention_forward(resid_two, second_attn, slot_count)
    resid_three = resid_two + branch_three
    expert_weights = collect_expert(expert_in, expert_out, group_id, rank_id, group_size)

    def run_experts(rows):
        return one_expert_forward(rows, expert_weights[0], expert_weights[1], group_id, group_size)

    branch_four, kept_four = moe_forward(resid_three, expert_ids, small_moe, run_experts)
    resid_four = resid_three + branch_four
    block_out = (resid_four * alive_rows).astype(jnp.bfloat16).reshape(patches.shape)
    upstream = cotangent.astype(jnp.float32).reshape(row_count, width) * alive_rows
    back_weights = collect_expert(expert_in, expert_out, group_id, rank_id, group_size)

    def back_experts(grad_produced, kept_experts):
        return one_expert_backward(
            grad_produced, kept_experts, back_weights[0], back_weights[1], group_id, group_size
        )

    upstream, moe_small_grads, large_grads = moe_backward(
        upstream, resid_three, small_moe, kept_four, back_experts
    )
    expert_shards = reduce_expert(
        large_grads[0],
        large_grads[1],
        group_id,
        rank_id,
        group_size,
        expert_in.shape,
        expert_out.shape,
    )
    second_back = refetch_attention(attn_gain, attn_qkv, attn_out, 1)
    upstream, second_grads = attention_backward(
        upstream, resid_two, second_back, kept_three, slot_count
    )
    second_shards = reduce_owned([second_grads[0], second_grads[1], second_grads[2]])
    mlp_back = (
        lax.all_gather(mlp_gain, "fsdp", axis=0, tiled=True),
        lax.all_gather(mlp_in, "fsdp", axis=0, tiled=True),
        lax.all_gather(mlp_out, "fsdp", axis=0, tiled=True),
    )
    upstream, mlp_grads = mlp_backward(upstream, resid_one, mlp_back, kept_two)
    mlp_shards = reduce_owned(
        [mlp_grads[0], mlp_grads[1], mlp_grads[2], moe_small_grads[0], moe_small_grads[1]]
    )
    first_back = refetch_attention(attn_gain, attn_qkv, attn_out, 0)
    upstream, first_grads = attention_backward(
        upstream, resid_zero, first_back, kept_one, slot_count
    )
    first_shards = reduce_owned([first_grads[0], first_grads[1], first_grads[2]])
    input_grad = upstream.reshape(patches.shape)
    grad_attn_gain = jnp.stack([first_shards[0], second_shards[0]], axis=1)
    grad_attn_qkv = jnp.stack([first_shards[1], second_shards[1]], axis=1)
    grad_attn_out = jnp.stack([first_shards[2], second_shards[2]], axis=1)
    return (
        block_out,
        input_grad,
        grad_attn_gain,
        grad_attn_qkv,
        grad_attn_out,
        mlp_shards[0],
        mlp_shards[1],
        mlp_shards[2],
        mlp_shards[3],
        mlp_shards[4],
        expert_shards[0],
        expert_shards[1],
    )


def solution(mesh):
    placed = (
        P("fsdp", None, None),
        P("fsdp"),
        P("fsdp", None),
        P("fsdp", None),
        P("fsdp", None, None),
        P("fsdp", None, None),
        P("fsdp"),
        P("fsdp", None),
        P("fsdp", None),
        P("fsdp"),
        P("fsdp", None),
        P("fsdp", None, None),
        P("fsdp", None, None),
        P("fsdp", None, None),
    )
    return jax.shard_map(
        local,
        mesh=mesh,
        in_specs=placed,
        out_specs=(
            P("fsdp", None, None),
            P("fsdp", None, None),
            P("fsdp", None),
            P("fsdp", None, None),
            P("fsdp", None, None),
            P("fsdp"),
            P("fsdp", None),
            P("fsdp", None),
            P("fsdp"),
            P("fsdp", None),
            P("fsdp", None, None),
            P("fsdp", None, None),
        ),
        check_vma=False,
    )
```

profile of v0, /device:TPU:0, one launch (start us, length us, event | category | flops | bytes accessed | tf_op | source)
XLA Modules:
  0.0 1501.0 jit_solution(920239332049394024)
XLA Ops:
  15.3 5.1 collective-permute-start.5
  29.2 18.6 %collective-permute-done.4 = bf16[2,73728]{1,0:T(2,128)(2,1)S(1)} collective-permute-done((bf16[2,73728]{1,0:T(2,128)(2,1)S(1)}, bf16[2,73728]{1,0:T(2,128)(2,1)S(1)}, u32[]{:S(2)}, u32[]{:S(2)}) %collective-permute-start.4) | collective-permute-done | bytes 294944 | tf_op jit(solution)/shard_map/ppermute | solution.py:22
  64.3 92.0 %all-reduce.5 = (bf16[768]{0:T(1024)(128)(2,1)S(1)}, bf16[768]{0:T(1024)(128)(2,1)S(1)}, bf16[768]{0:T(1024)(128)(2,1)S(1)}, bf16[768]{0:T(1024)(128)(2,1)S(1)}) all-reduce(bf16[768]{0:T(1024)(128)(2,1)S(1)} %dynamic-update-slice, bf16[768]{0:T(1024)(128)(2,1)S(1)} %dynamic-update-slice.1, ...), channel_id=2, replica_groups=mesh['fsdp'=32] {'fsdp'}, use_global_device_ids=true, to_apply=%add.1 | all-reduce | flops 3072 | bytes 12288
  165.6 12.7 broadcast_select_fusion.1
  182.5 39.9 %all-gather.6 = bf16[32,24,4]{1,2,0:T(4,128)(2,1)S(1)} all-gather(bf16[1,24,4]{1,2,0:T(4,128)(2,1)S(1)} %bitcast.307), channel_id=1, replica_groups=mesh['fsdp'=32] {'fsdp'}, dimensions={0}, use_global_device_ids=true | all-gather | bytes 6336 | tf_op jit(solution)/shard_map/all_gather | solution.py:375
  227.7 5.5 compare_reduce_fusion
  264.5 37.0 %collective-permute-done.8 = bf16[4,4,2,73728]{3,2,0,1:T(2,128)(2,1)} collective-permute-done((bf16[4,4,2,73728]{3,2,0,1:T(2,128)(2,1)}, bf16[4,4,2,73728]{3,2,0,1:T(2,128)(2,1)}, u32[]{:S(2)}, u32[]{:S(2)}) %collective-permute-start.8) | collective-permute-done | bytes 4718624 | tf_op jit(solution)/shard_map/ppermute | solution.py:16
  301.5 23.7 %fusion.7 = bf16[2,4,8,73728]{3,0,1,2:T(2,128)(2,1)} fusion(pred[]{:T(512)S(6)} %eq.145, bf16[4,4,2,73728]{3,2,0,1:T(2,128)(2,1)} %broadcast_select_fusion.1, bf16[4,4,2,73728]{3,2,0,1:T(2,128)(2,1)} %collective-permute-done.8), kind=kLoop, calls=%fused_computation.20 | loop fusion | flops 14155776 | bytes 18874368 | tf_op jit(solution)/shard_map/transpose | solution.py:126
  325.4 6.8 fusion.104
  332.2 6.9 fusion.118
  339.4 18.9 %all-gather.22.cloned.1.call-done = bf16[768,1,2304]{2,0,1:T(8,128)(2,1)} async-done(((bf16[24,1,2304]{2,0,1:T(8,128)(2,1)}), bf16[768,1,2304]{2,0,1:T(8,128)(2,1)}) %all-gather.22.cloned.1.call-update) | async-done | bytes 3538960 | tf_op jit(solution)/shard_map/all_gather | solution.py:78
  366.9 5.1 fusion.112
  386.9 27.6 %all-gather.24.cloned.1.call-done = bf16[768,1,768]{2,0,1:T(8,128)(2,1)} async-done(((bf16[24,1,768]{2,0,1:T(8,128)(2,1)}), bf16[768,1,768]{2,0,1:T(8,128)(2,1)}) %all-gather.24.cloned.1.call-update) | async-done | bytes 1179664 | tf_op jit(solution)/shard_map/all_gather | solution.py:79
  435.6 16.2 %collective-permute-start.12 = (bf16[247,768]{1,0:T(8,128)(2,1)}, bf16[247,768]{1,0:T(8,128)(2,1)S(1)}, u32[]{:S(2)}, u32[]{:S(2)}) collective-permute-start(bf16[247,768]{1,0:T(8,128)(2,1)} %get-tuple-element.131), channel_id=1, source_target_pairs={{0,8},{1,9},{2,10},{3,11},{4,12},{5,13},{6,14},{7,15},{8,16},{9,17... | collective-permute-start | bytes 1138184 | tf_op jit(solution)/shard_map/ppermute | solution.py:22
  451.8 24.2 %fusion.111 = (bf16[1,4,8,73728]{3,0,1,2:T(2,128)(2,1)}, bf16[1,4,8,73728]{3,0,1,2:T(2,128)(2,1)S(1)}) fusion(bf16[2,4,8,73728]{3,0,1,2:T(2,128)(2,1)} %fusion.7), kind=kLoop, calls=%fused_computation.338 | loop fusion | bytes 18874368 | tf_op jit(solution)/shard_map/slice | solution.py:127
  476.0 7.3 copy.290
  483.3 6.2 reshape_squeeze.15
  489.5 11.0 copy.289
  500.5 6.1 reshape_squeeze.14
  511.3 12.3 fusion.123
  523.6 10.3 convolution_convert_fusion.2
  534.0 13.1 fusion.6
  547.1 12.6 fusion.106
  559.7 6.6 fusion.121
  566.3 7.7 fusion.125
  582.1 23.7 %stack.225 = f32[1,4,8,73728]{3,0,2,1:T(1,128)} reshape(f32[3072,768]{1,0:T(8,128)} %fusion.106) | data formatting | bytes 18874368 | tf_op jit(solution)/shard_map/stack | solution.py:131
  605.8 24.3 %stack.224 = f32[1,4,8,73728]{3,0,2,1:T(1,128)} reshape(f32[768,3072]{1,0:T(8,128)} %fusion.125) | data formatting | bytes 18874368 | tf_op jit(solution)/shard_map/stack | solution.py:131
  630.1 18.8 %maximum_bitcast_fusion = f32[4,8,2,73728]{3,2,1,0:T(2,128)S(1)} fusion(f32[1,4,8,73728]{3,0,2,1:T(1,128)} %stack.225, f32[1,4,8,73728]{3,0,2,1:T(1,128)} %stack.224), kind=kLoop, calls=%fused_computation.6 | loop fusion | flops 4718592 | bytes 37748736 | tf_op jit(solution)/shard_map/transpose | solution.py:132
  648.9 7.8 select_convert_fusion.1
  721.2 6.6 convert_element_type.322
  727.9 5.0 multiply_reduce_fusion.6
  733.7 9.2 fusion.14
  765.4 5.2 fusion.105
  775.7 5.3 fusion.103
  781.0 5.6 fusion.68
  797.9 6.6 convert_element_type.329
  812.2 6.7 reshape.548
  821.9 20.7 %dynamic-update-slice.10 = f32[32,73752]{1,0:T(8,128)} dynamic-update-slice(f32[32,73752]{1,0:T(8,128)} %dynamic-update-slice.9, f32[32,55296]{1,0:T(8,128)} %reshape.548, s32[]{} %constant.526, s32[]{} %constant.527) | dynamic-update-slice | bytes 14155780
  842.5 8.8 dynamic-update-slice.11
  851.4 5.8 select_convert_fusion.3
  863.1 6.8 reshape.545
  872.9 20.7 %dynamic-update-slice.13 = f32[32,73752]{1,0:T(8,128)} dynamic-update-slice(f32[32,73752]{1,0:T(8,128)} %dynamic-update-slice.12, f32[32,55296]{1,0:T(8,128)} %reshape.545, s32[]{} %constant.526, s32[]{} %constant.527) | dynamic-update-slice | bytes 14155780
  893.6 8.6 dynamic-update-slice.14
  902.2 5.7 select_convert_fusion.4
  910.0 8.1 reshape.551
  918.1 8.2 reshape.552
  927.9 28.8 %dynamic-update-slice.5 = f32[32,147600]{1,0:T(8,128)} dynamic-update-slice(f32[32,147600]{1,0:T(8,128)} %dynamic-update-slice.4, f32[32,73728]{1,0:T(8,128)} %reshape.551, s32[]{} %constant.526, s32[]{} %constant.527) | dynamic-update-slice | bytes 18874372
  956.6 28.4 %dynamic-update-slice.6 = f32[32,147600]{1,0:T(8,128)} dynamic-update-slice(f32[32,147600]{1,0:T(8,128)} %dynamic-update-slice.5, f32[32,73728]{1,0:T(8,128)} %reshape.552, s32[]{} %constant.526, s32[]{} %constant.528) | dynamic-update-slice | bytes 18874372
  988.0 9.6 select_convert_fusion
  998.6 98.8 %collective-permute-done.23 = bf16[16,73752]{1,0:T(8,128)(2,1)} collective-permute-done((bf16[16,73752]{1,0:T(8,128)(2,1)}, bf16[16,73752]{1,0:T(8,128)(2,1)}, u32[]{:S(2)}, u32[]{:S(2)}) %collective-permute-start.23) | collective-permute-done | bytes 2360096 | tf_op jit(solution)/shard_map/ppermute | solution.py:16
  1097.5 5.0 convert_add_fusion.3
  1102.8 45.3 %collective-permute-done.18 = bf16[16,73752]{1,0:T(8,128)(2,1)S(1)} collective-permute-done((bf16[16,73752]{1,0:T(8,128)(2,1)}, bf16[16,73752]{1,0:T(8,128)(2,1)S(1)}, u32[]{:S(2)}, u32[]{:S(2)}) %collective-permute-start.18) | collective-permute-done | bytes 2360096 | tf_op jit(solution)/shard_map/ppermute | solution.py:16
  1152.9 121.6 %collective-permute-done.24 = bf16[8,73752]{1,0:T(8,128)(2,1)S(1)} collective-permute-done((bf16[8,73752]{1,0:T(8,128)(2,1)S(1)}, bf16[8,73752]{1,0:T(8,128)(2,1)S(1)}, u32[]{:S(2)}, u32[]{:S(2)}) %collective-permute-start.24) | collective-permute-done | bytes 1180064 | tf_op jit(solution)/shard_map/ppermute | solution.py:16
  1275.9 23.9 %collective-permute-done.19 = bf16[8,73752]{1,0:T(8,128)(2,1)S(1)} collective-permute-done((bf16[8,73752]{1,0:T(8,128)(2,1)S(1)}, bf16[8,73752]{1,0:T(8,128)(2,1)S(1)}, u32[]{:S(2)}, u32[]{:S(2)}) %collective-permute-start.19) | collective-permute-done | bytes 1180064 | tf_op jit(solution)/shard_map/ppermute | solution.py:16
  1303.5 12.4 collective-permute-done.20
  1317.9 8.4 convert_add_fusion.1
  1340.4 8.5 convert_add_fusion
  1354.8 26.3 %collective-permute-done.34 = bf16[4,2,2,73728]{3,2,1,0:T(2,128)(2,1)} collective-permute-done((bf16[4,2,2,73728]{3,2,1,0:T(2,128)(2,1)S(1)}, bf16[4,2,2,73728]{3,2,1,0:T(2,128)(2,1)}, u32[]{:S(2)}, u32[]{:S(2)}) %collective-permute-start.34) | collective-permute-done | bytes 2359328 | tf_op jit(solution)/shard_map/ppermute | solution.py:16
  1381.1 7.6 convert_add_fusion.5
  1390.0 18.7 %collective-permute-done.29 = bf16[8,147600]{1,0:T(8,128)(2,1)} collective-permute-done((bf16[8,147600]{1,0:T(8,128)(2,1)}, bf16[8,147600]{1,0:T(8,128)(2,1)}, u32[]{:S(2)}, u32[]{:S(2)}) %collective-permute-start.29) | collective-permute-done | bytes 2361632 | tf_op jit(solution)/shard_map/ppermute | solution.py:16
  1422.4 6.2 collective-permute-done.38
  1428.8 18.5 %collective-permute-done.37 = bf16[2,73728]{1,0:T(2,128)(2,1)S(1)} collective-permute-done((bf16[2,73728]{1,0:T(2,128)(2,1)S(1)}, bf16[2,73728]{1,0:T(2,128)(2,1)S(1)}, u32[]{:S(2)}, u32[]{:S(2)}) %collective-permute-start.37) | collective-permute-done | bytes 294944 | tf_op jit(solution)/shard_map/ppermute | solution.py:22
  1463.6 11.3 collective-permute-done.31
  1477.1 6.7 slice_reduce_fusion
  (621 shorter events, 345.4 us)
Async XLA Ops:
  7.2 226.0 %all-gather.18.cloned.1.call-start = ((), (), s32[]{:S(2)}) async-start(), calls=%async_computation.2 | async-start | bytes 3649536 | tf_op jit(solution)/shard_map/all_gather | solution.py:78
  9.4 252.4 %all-gather.20.cloned.1.call-start = ((), (), s32[]{:S(2)}) async-start(), calls=%async_computation.3 | async-start | bytes 1216512 | tf_op jit(solution)/shard_map/all_gather | solution.py:79
  11.2 314.1 %all-gather.14.cloned.1.call-start = ((), (), s32[]{:S(2)}) async-start(), calls=%async_computation | async-start | bytes 4866048 | tf_op jit(solution)/shard_map/all_gather | solution.py:372
  12.0 320.2 %all-gather.16.cloned.1.call-start = ((), (), s32[]{:S(2)}) async-start(), calls=%async_computation.1 | async-start | bytes 4866048 | tf_op jit(solution)/shard_map/all_gather | solution.py:373
  15.3 14.0 collective-permute-start.5
  20.4 337.9 %all-gather.22.cloned.1.call-start = ((), (), s32[]{:S(2)}) async-start(), calls=%async_computation.4 | async-start | bytes 3649536 | tf_op jit(solution)/shard_map/all_gather | solution.py:78
  21.1 26.7 %collective-permute-start.4 = (bf16[2,73728]{1,0:T(2,128)(2,1)S(1)}, bf16[2,73728]{1,0:T(2,128)(2,1)S(1)}, u32[]{:S(2)}, u32[]{:S(2)}) collective-permute-start(bf16[2,73728]{1,0:T(2,128)(2,1)S(1)} %pad_maximum_fusion.9), channel_id=1, source_target_pairs={{0,16},{1,17},{2,18},{3,19},{4,20},{5,21},{6,22},{7,23},{8,24},{9,... | collective-permute-start | bytes 884744 | tf_op jit(solution)/shard_map/ppermute | solution.py:22
  21.9 26.0 %collective-permute-start.3 = (bf16[2,73728]{1,0:T(2,128)(2,1)S(1)}, bf16[2,73728]{1,0:T(2,128)(2,1)S(1)}, u32[]{:S(2)}, u32[]{:S(2)}) collective-permute-start(bf16[2,73728]{1,0:T(2,128)(2,1)S(1)} %pad_maximum_fusion.8), channel_id=1, source_target_pairs={{0,8},{1,9},{2,10},{3,11},{4,12},{5,13},{6,14},{7,15},{8,16},{9,17... | collective-permute-start | bytes 884744 | tf_op jit(solution)/shard_map/ppermute | solution.py:22
  23.6 390.8 %all-gather.24.cloned.1.call-start = ((), (), s32[]{:S(2)}) async-start(), calls=%async_computation.5 | async-start | bytes 1216512 | tf_op jit(solution)/shard_map/all_gather | solution.py:79
  54.1 2.9 collective-permute-start.6
  61.5 104.1 %collective-permute-start.7 = (bf16[4,2,2,73728]{3,2,0,1:T(2,128)(2,1)}, bf16[4,2,2,73728]{3,2,0,1:T(2,128)(2,1)}, u32[]{:S(2)}, u32[]{:S(2)}) collective-permute-start(bf16[4,2,2,73728]{3,2,0,1:T(2,128)(2,1)} %broadcast_select_fusion.2), channel_id=1, source_target_pairs={{0,2},{1,3},{2,0},{3,1},{4,6},{5,7},{6,4},{7,5},{8,10},{9,11},{10,... | collective-permute-start | bytes 7077896 | tf_op jit(solution)/shard_map/ppermute | solution.py:16
  63.3 198.5 %copy-start.9 = (f32[394,768]{1,0:T(8,128)}, f32[394,768]{1,0:T(8,128)S(1)}, u32[]{:S(2)}) copy-start(f32[394,768]{1,0:T(8,128)S(1)} %reshape.529) | copy-start | bytes 3631108
  63.3 95.6 %copy-start.60 = (bf16[2,197,768]{2,0,1:T(2,128)(2,1)S(1)}, bf16[2,197,768]{2,0,1:T(2,128)(2,1)}, u32[]{:S(2)}) copy-start(bf16[2,197,768]{2,0,1:T(2,128)(2,1)} %param.29) | copy-start | bytes 1815556
  156.3 76.9 %copy-start.74 = (f32[768]{0:T(1024)}, f32[768]{0:T(1024)S(1)}, u32[]{:S(2)}) copy-start(f32[768]{0:T(1024)S(1)} %convert_element_type.376) | copy-start | bytes 9220
  158.2 74.9 %copy-start.100 = (f32[394]{0:T(512)}, f32[394]{0:T(512)S(1)}, u32[]{:S(2)}) copy-start(f32[394]{0:T(512)S(1)} %rsqrt.47) | copy-start | bytes 4732
  158.3 74.8 %copy-start.102 = (f32[394]{0:T(512)}, f32[394]{0:T(512)S(1)}, u32[]{:S(2)}) copy-start(f32[394]{0:T(512)S(1)} %div.167) | copy-start | bytes 4732
  158.4 167.0 %copy-start.94 = (f32[768]{0:T(1024)}, f32[768]{0:T(1024)S(1)}, u32[]{:S(2)}) copy-start(f32[768]{0:T(1024)S(1)} %convert_element_type.295) | copy-start | bytes 9220
  158.8 199.4 %copy-start.96 = (f32[768]{0:T(1024)}, f32[768]{0:T(1024)S(1)}, u32[]{:S(2)}) copy-start(f32[768]{0:T(1024)S(1)} %convert_element_type.377) | copy-start | bytes 9220
  158.9 258.0 %copy-start.68 = (f32[768]{0:T(1024)}, f32[768]{0:T(1024)S(1)}, u32[]{:S(2)}) copy-start(f32[768]{0:T(1024)S(1)} %convert_element_type.305) | copy-start | bytes 9220
  161.5 65.1 %copy-start.11 = (f32[394,768]{1,0:T(8,128)}, f32[394,768]{1,0:T(8,128)S(1)}, u32[]{:S(2)}) copy-start(f32[394,768]{1,0:T(8,128)S(1)} %reshape.559) | copy-start | bytes 3631108
  162.3 64.3 %copy-start.78 = (f32[394]{0:T(512)}, f32[394]{0:T(512)S(1)}, u32[]{:S(2)}) copy-start(f32[394]{0:T(512)S(1)} %mul.516) | copy-start | bytes 4732
  178.3 123.3 %collective-permute-start.8 = (bf16[4,4,2,73728]{3,2,0,1:T(2,128)(2,1)}, bf16[4,4,2,73728]{3,2,0,1:T(2,128)(2,1)}, u32[]{:S(2)}, u32[]{:S(2)}) collective-permute-start(bf16[4,4,2,73728]{3,2,0,1:T(2,128)(2,1)} %broadcast_select_fusion.1), channel_id=1, source_target_pairs={{0,4},{1,5},{2,6},{3,7},{4,0},{5,1},{6,2},{7,3},{8,12},{9,13},{10,... | collective-permute-start | bytes 14155784 | tf_op jit(solution)/shard_map/ppermute | solution.py:16
  222.5 204.0 %copy-start.70 = (bf16[768,4]{0,1:T(4,128)(2,1)}, bf16[768,4]{0,1:T(4,128)(2,1)S(1)}, u32[]{:S(2)}) copy-start(bf16[768,4]{0,1:T(4,128)(2,1)S(1)} %reshape.636) | copy-start | bytes 18436
  264.2 68.0 %copy-start.13 = (f32[394,768]{1,0:T(8,128)}, f32[394,768]{1,0:T(8,128)S(1)}, u32[]{:S(2)}) copy-start(f32[394,768]{1,0:T(8,128)S(1)} %get-tuple-element.162) | copy-start | bytes 3631108
  264.2 61.2 %copy-start.80 = (f32[394]{0:T(512)}, f32[394]{0:T(512)S(1)}, u32[]{:S(2)}) copy-start(f32[394]{0:T(512)S(1)} %broadcast_multiply_fusion.4) | copy-start | bytes 4732
  264.5 60.8 %copy-start.84 = (f32[394]{0:T(512)}, f32[394]{0:T(512)S(1)}, u32[]{:S(2)}) copy-start(f32[394]{0:T(512)S(1)} %multiply_reduce_fusion.14) | copy-start | bytes 4732
  264.5 60.9 %copy-start.104 = (f32[394]{0:T(512)}, f32[394]{0:T(512)S(1)}, u32[]{:S(2)}) copy-start(f32[394]{0:T(512)S(1)} %fusion.88) | copy-start | bytes 4732
  339.0 75.4 %copy-start.16 = (f32[394,768]{1,0:T(8,128)}, f32[394,768]{1,0:T(8,128)S(1)}, u32[]{:S(2)}) copy-start(f32[394,768]{1,0:T(8,128)S(1)} %get-tuple-element.164) | copy-start | bytes 3631108
  423.5 12.2 collective-permute-start.2
  425.7 80.8 %collective-permute-start.1 = (bf16[247,768]{1,0:T(8,128)(2,1)}, bf16[247,768]{1,0:T(8,128)(2,1)}, u32[]{:S(2)}, u32[]{:S(2)}) collective-permute-start(bf16[247,768]{1,0:T(8,128)(2,1)} %get-tuple-element.138), channel_id=1, source_target_pairs={{0,16},{1,17},{2,18},{3,19},{4,20},{5,21},{6,22},{7,23},{8,24},{9,... | collective-permute-start | bytes 1138184 | tf_op jit(solution)/shard_map/ppermute | solution.py:22
  425.7 80.8 %collective-permute-start = (bf16[247,768]{1,0:T(8,128)(2,1)}, bf16[247,768]{1,0:T(8,128)(2,1)}, u32[]{:S(2)}, u32[]{:S(2)}) collective-permute-start(bf16[247,768]{1,0:T(8,128)(2,1)} %get-tuple-element.139), channel_id=1, source_target_pairs={{0,8},{1,9},{2,10},{3,11},{4,12},{5,13},{6,14},{7,15},{8,16},{9,17... | collective-permute-start | bytes 1138184 | tf_op jit(solution)/shard_map/ppermute | solution.py:22
  431.4 78.1 %collective-permute-start.14 = (bf16[247,768]{1,0:T(8,128)(2,1)}, bf16[247,768]{1,0:T(8,128)(2,1)S(1)}, u32[]{:S(2)}, u32[]{:S(2)}) collective-permute-start(bf16[247,768]{1,0:T(8,128)(2,1)} %get-tuple-element.129), channel_id=1, source_target_pairs={{0,24},{1,25},{2,26},{3,27},{4,28},{5,29},{6,30},{7,31},{8,0},{9,1... | collective-permute-start | bytes 1138184 | tf_op jit(solution)/shard_map/ppermute | solution.py:22
  434.5 75.1 %collective-permute-start.13 = (bf16[247,768]{1,0:T(8,128)(2,1)}, bf16[247,768]{1,0:T(8,128)(2,1)S(1)}, u32[]{:S(2)}, u32[]{:S(2)}) collective-permute-start(bf16[247,768]{1,0:T(8,128)(2,1)} %get-tuple-element.130), channel_id=1, source_target_pairs={{0,16},{1,17},{2,18},{3,19},{4,20},{5,21},{6,22},{7,23},{8,24},{9,... | collective-permute-start | bytes 1138184 | tf_op jit(solution)/shard_map/ppermute | solution.py:22
  435.6 73.9 %collective-permute-start.12 = (bf16[247,768]{1,0:T(8,128)(2,1)}, bf16[247,768]{1,0:T(8,128)(2,1)S(1)}, u32[]{:S(2)}, u32[]{:S(2)}) collective-permute-start(bf16[247,768]{1,0:T(8,128)(2,1)} %get-tuple-element.131), channel_id=1, source_target_pairs={{0,8},{1,9},{2,10},{3,11},{4,12},{5,13},{6,14},{7,15},{8,16},{9,17... | collective-permute-start | bytes 1138184 | tf_op jit(solution)/shard_map/ppermute | solution.py:22
  575.1 83.7 %collective-permute-start.11 = (bf16[247,768]{1,0:T(8,128)(2,1)}, bf16[247,768]{1,0:T(8,128)(2,1)S(1)}, u32[]{:S(2)}, u32[]{:S(2)}) collective-permute-start(bf16[247,768]{1,0:T(8,128)(2,1)} %get-tuple-element.133), channel_id=1, source_target_pairs={{0,8},{1,9},{2,10},{3,11},{4,12},{5,13},{6,14},{7,15},{8,16},{9,17... | collective-permute-start | bytes 1138184 | tf_op jit(solution)/shard_map/ppermute | solution.py:22
  575.1 86.6 %collective-permute-start.10 = (bf16[247,768]{1,0:T(8,128)(2,1)}, bf16[247,768]{1,0:T(8,128)(2,1)S(1)}, u32[]{:S(2)}, u32[]{:S(2)}) collective-permute-start(bf16[247,768]{1,0:T(8,128)(2,1)} %get-tuple-element.134), channel_id=1, source_target_pairs={{0,16},{1,17},{2,18},{3,19},{4,20},{5,21},{6,22},{7,23},{8,24},{9,... | collective-permute-start | bytes 1138184 | tf_op jit(solution)/shard_map/ppermute | solution.py:22
  575.1 88.1 %collective-permute-start.9 = (bf16[247,768]{1,0:T(8,128)(2,1)S(1)}, bf16[247,768]{1,0:T(8,128)(2,1)}, u32[]{:S(2)}, u32[]{:S(2)}) collective-permute-start(bf16[247,768]{1,0:T(8,128)(2,1)S(1)} %get-tuple-element.135), channel_id=1, source_target_pairs={{0,24},{1,25},{2,26},{3,27},{4,28},{5,29},{6,30},{7,31},{8,0},{9,1... | collective-permute-start | bytes 1138184 | tf_op jit(solution)/shard_map/ppermute | solution.py:22
  580.1 88.4 %collective-permute-start.17 = (bf16[247,768]{1,0:T(8,128)(2,1)}, bf16[247,768]{1,0:T(8,128)(2,1)}, u32[]{:S(2)}, u32[]{:S(2)}) collective-permute-start(bf16[247,768]{1,0:T(8,128)(2,1)} %get-tuple-element.126), channel_id=1, source_target_pairs={{0,8},{1,9},{2,10},{3,11},{4,12},{5,13},{6,14},{7,15},{8,16},{9,17... | collective-permute-start | bytes 1138184 | tf_op jit(solution)/shard_map/ppermute | solution.py:22
  580.6 95.6 %collective-permute-start.16 = (bf16[247,768]{1,0:T(8,128)(2,1)}, bf16[247,768]{1,0:T(8,128)(2,1)}, u32[]{:S(2)}, u32[]{:S(2)}) collective-permute-start(bf16[247,768]{1,0:T(8,128)(2,1)} %get-tuple-element.127), channel_id=1, source_target_pairs={{0,16},{1,17},{2,18},{3,19},{4,20},{5,21},{6,22},{7,23},{8,24},{9,... | collective-permute-start | bytes 1138184 | tf_op jit(solution)/shard_map/ppermute | solution.py:22
  658.8 18.6 %collective-permute-start.15 = (bf16[247,768]{1,0:T(8,128)(2,1)S(1)}, bf16[247,768]{1,0:T(8,128)(2,1)}, u32[]{:S(2)}, u32[]{:S(2)}) collective-permute-start(bf16[247,768]{1,0:T(8,128)(2,1)S(1)} %get-tuple-element.125), channel_id=1, source_target_pairs={{0,24},{1,25},{2,26},{3,27},{4,28},{5,29},{6,30},{7,31},{8,0},{9,1... | collective-permute-start | bytes 1138184 | tf_op jit(solution)/shard_map/ppermute | solution.py:22
  661.7 656.2 %collective-permute-start.33 = (bf16[4,4,2,73728]{3,2,1,0:T(2,128)(2,1)}, bf16[4,4,2,73728]{3,2,1,0:T(2,128)(2,1)}, u32[]{:S(2)}, u32[]{:S(2)}) collective-permute-start(bf16[4,4,2,73728]{3,2,1,0:T(2,128)(2,1)} %select_convert_fusion.1), channel_id=1, source_target_pairs={{0,4},{1,5},{2,6},{3,7},{4,0},{5,1},{6,2},{7,3},{8,12},{9,13},{10,... | collective-permute-start | bytes 14155784 | tf_op jit(solution)/shard_map/ppermute | solution.py:16
  857.1 240.3 %collective-permute-start.23 = (bf16[16,73752]{1,0:T(8,128)(2,1)}, bf16[16,73752]{1,0:T(8,128)(2,1)}, u32[]{:S(2)}, u32[]{:S(2)}) collective-permute-start(bf16[16,73752]{1,0:T(8,128)(2,1)} %select_convert_fusion.3), channel_id=1, source_target_pairs={{0,16},{1,17},{2,18},{3,19},{4,20},{5,21},{6,22},{7,23},{8,24},{9,... | collective-permute-start | bytes 7080200 | tf_op jit(solution)/shard_map/ppermute | solution.py:16
  907.9 240.2 %collective-permute-start.18 = (bf16[16,73752]{1,0:T(8,128)(2,1)}, bf16[16,73752]{1,0:T(8,128)(2,1)S(1)}, u32[]{:S(2)}, u32[]{:S(2)}) collective-permute-start(bf16[16,73752]{1,0:T(8,128)(2,1)} %select_convert_fusion.4), channel_id=1, source_target_pairs={{0,16},{1,17},{2,18},{3,19},{4,20},{5,21},{6,22},{7,23},{8,24},{9,... | collective-permute-start | bytes 7080200 | tf_op jit(solution)/shard_map/ppermute | solution.py:16
  997.6 342.8 %collective-permute-start.28 = (bf16[16,147600]{1,0:T(8,128)(2,1)}, bf16[16,147600]{1,0:T(8,128)(2,1)}, u32[]{:S(2)}, u32[]{:S(2)}) collective-permute-start(bf16[16,147600]{1,0:T(8,128)(2,1)} %select_convert_fusion), channel_id=1, source_target_pairs={{0,16},{1,17},{2,18},{3,19},{4,20},{5,21},{6,22},{7,23},{8,24},{9,... | collective-permute-start | bytes 14169608 | tf_op jit(solution)/shard_map/ppermute | solution.py:16
  1102.7 171.8 %collective-permute-start.24 = (bf16[8,73752]{1,0:T(8,128)(2,1)S(1)}, bf16[8,73752]{1,0:T(8,128)(2,1)S(1)}, u32[]{:S(2)}, u32[]{:S(2)}) collective-permute-start(bf16[8,73752]{1,0:T(8,128)(2,1)S(1)} %select_convert_fusion.7), channel_id=1, source_target_pairs={{0,8},{1,9},{2,10},{3,11},{4,12},{5,13},{6,14},{7,15},{8,0},{9,1},... | collective-permute-start | bytes 3540104 | tf_op jit(solution)/shard_map/ppermute | solution.py:16
  1148.1 169.8 %slice-start.4 = ((s8[18874368]{0:T(1024)(128)(4,1)}), s8[4194304]{0:T(1024)(128)(4,1)S(1)}, s32[]{:S(2)}) async-start(s8[18874368]{0:T(1024)(128)(4,1)} %bitcast.274), calls=%async_computation.10 | async-start | bytes 8388608
  1148.1 169.8 %slice-start.5 = ((s8[18874368]{0:T(1024)(128)(4,1)}), s8[2097152]{0:T(1024)(128)(4,1)S(1)}, s32[]{:S(2)}) async-start(s8[18874368]{0:T(1024)(128)(4,1)} %bitcast.274), calls=%async_computation.11 | async-start | bytes 4194304
  1152.8 165.1 %slice-start.6 = ((s8[18874368]{0:T(1024)(128)(4,1)}), s8[4194304]{0:T(1024)(128)(4,1)S(1)}, s32[]{:S(2)}) async-start(s8[18874368]{0:T(1024)(128)(4,1)} %bitcast.274), calls=%async_computation.12 | async-start | bytes 8388608
  1152.8 147.0 %collective-permute-start.19 = (bf16[8,73752]{1,0:T(8,128)(2,1)S(1)}, bf16[8,73752]{1,0:T(8,128)(2,1)S(1)}, u32[]{:S(2)}, u32[]{:S(2)}) collective-permute-start(bf16[8,73752]{1,0:T(8,128)(2,1)S(1)} %select_convert_fusion.8), channel_id=1, source_target_pairs={{0,8},{1,9},{2,10},{3,11},{4,12},{5,13},{6,14},{7,15},{8,0},{9,1},... | collective-permute-start | bytes 3540104 | tf_op jit(solution)/shard_map/ppermute | solution.py:16
  1275.3 25.8 %collective-permute-start.25 = (bf16[4,73752]{1,0:T(4,128)(2,1)S(1)}, bf16[4,73752]{1,0:T(4,128)(2,1)S(1)}, u32[]{:S(2)}, u32[]{:S(2)}) collective-permute-start(bf16[4,73752]{1,0:T(4,128)(2,1)S(1)} %select_convert_fusion.11), channel_id=1, source_target_pairs={{0,4},{1,5},{2,6},{3,7},{4,0},{5,1},{6,2},{7,3},{8,12},{9,13},{10,... | collective-permute-start | bytes 1770056 | tf_op jit(solution)/shard_map/ppermute | solution.py:16
  1300.5 15.3 %collective-permute-start.20 = (bf16[4,73752]{1,0:T(4,128)(2,1)S(1)}, bf16[4,73752]{1,0:T(4,128)(2,1)S(1)}, u32[]{:S(2)}, u32[]{:S(2)}) collective-permute-start(bf16[4,73752]{1,0:T(4,128)(2,1)S(1)} %select_convert_fusion.12), channel_id=1, source_target_pairs={{0,4},{1,5},{2,6},{3,7},{4,0},{5,1},{6,2},{7,3},{8,12},{9,13},{10,... | collective-permute-start | bytes 1770056 | tf_op jit(solution)/shard_map/ppermute | solution.py:16
  1302.0 28.5 %collective-permute-start.26 = (bf16[2,73752]{1,0:T(2,128)(2,1)S(1)}, bf16[2,73752]{1,0:T(2,128)(2,1)}, u32[]{:S(2)}, u32[]{:S(2)}) collective-permute-start(bf16[2,73752]{1,0:T(2,128)(2,1)S(1)} %select_convert_fusion.13), channel_id=1, source_target_pairs={{0,2},{1,3},{2,0},{3,1},{4,6},{5,7},{6,4},{7,5},{8,10},{9,11},{10,... | collective-permute-start | bytes 885032 | tf_op jit(solution)/shard_map/ppermute | solution.py:16
  1317.4 14.9 collective-permute-start.21
  1328.8 52.2 %collective-permute-start.34 = (bf16[4,2,2,73728]{3,2,1,0:T(2,128)(2,1)S(1)}, bf16[4,2,2,73728]{3,2,1,0:T(2,128)(2,1)}, u32[]{:S(2)}, u32[]{:S(2)}) collective-permute-start(bf16[4,2,2,73728]{3,2,1,0:T(2,128)(2,1)S(1)} %select_convert_fusion.5), channel_id=1, source_target_pairs={{0,2},{1,3},{2,0},{3,1},{4,6},{5,7},{6,4},{7,5},{8,10},{9,11},{10,... | collective-permute-start | bytes 7077896 | tf_op jit(solution)/shard_map/ppermute | solution.py:16
  1332.2 2.5 collective-permute-start.27
  1334.2 1.8 collective-permute-start.22
  1354.7 54.0 %collective-permute-start.29 = (bf16[8,147600]{1,0:T(8,128)(2,1)}, bf16[8,147600]{1,0:T(8,128)(2,1)}, u32[]{:S(2)}, u32[]{:S(2)}) collective-permute-start(bf16[8,147600]{1,0:T(8,128)(2,1)} %select_convert_fusion.2), channel_id=1, source_target_pairs={{0,8},{1,9},{2,10},{3,11},{4,12},{5,13},{6,14},{7,15},{8,0},{9,1},... | collective-permute-start | bytes 7084808 | tf_op jit(solution)/shard_map/ppermute | solution.py:16
  1389.9 28.0 %collective-permute-start.35 = (bf16[4,1,2,73728]{3,2,1,0:T(2,128)(2,1)S(1)}, bf16[4,1,2,73728]{3,2,1,0:T(2,128)(2,1)S(1)}, u32[]{:S(2)}, u32[]{:S(2)}) collective-permute-start(bf16[4,1,2,73728]{3,2,1,0:T(2,128)(2,1)S(1)} %select_convert_fusion.9), channel_id=1, source_target_pairs={{0,1},{1,0},{2,3},{3,2},{4,5},{5,4},{6,7},{7,6},{8,9},{9,8},{10,11... | collective-permute-start | bytes 3538952 | tf_op jit(solution)/shard_map/ppermute | solution.py:16
  1417.3 37.9 %collective-permute-start.30 = (bf16[4,147600]{1,0:T(4,128)(2,1)}, bf16[4,147600]{1,0:T(4,128)(2,1)}, u32[]{:S(2)}, u32[]{:S(2)}) collective-permute-start(bf16[4,147600]{1,0:T(4,128)(2,1)} %select_convert_fusion.6), channel_id=1, source_target_pairs={{0,4},{1,5},{2,6},{3,7},{4,0},{5,1},{6,2},{7,3},{8,12},{9,13},{10,... | collective-permute-start | bytes 3542408 | tf_op jit(solution)/shard_map/ppermute | solution.py:16
  1420.2 8.5 collective-permute-start.38
  1420.8 26.5 %collective-permute-start.37 = (bf16[2,73728]{1,0:T(2,128)(2,1)S(1)}, bf16[2,73728]{1,0:T(2,128)(2,1)S(1)}, u32[]{:S(2)}, u32[]{:S(2)}) collective-permute-start(bf16[2,73728]{1,0:T(2,128)(2,1)S(1)} %get-tuple-element.124), channel_id=1, source_target_pairs={{0,16},{1,17},{2,18},{3,19},{4,20},{5,21},{6,22},{7,23},{8,24},{9,... | collective-permute-start | bytes 884744 | tf_op jit(solution)/shard_map/ppermute | solution.py:22
  1422.1 25.5 %collective-permute-start.36 = (bf16[2,73728]{1,0:T(2,128)(2,1)S(1)}, bf16[2,73728]{1,0:T(2,128)(2,1)S(1)}, u32[]{:S(2)}, u32[]{:S(2)}) collective-permute-start(bf16[2,73728]{1,0:T(2,128)(2,1)S(1)} %get-tuple-element.122), channel_id=1, source_target_pairs={{0,8},{1,9},{2,10},{3,11},{4,12},{5,13},{6,14},{7,15},{8,16},{9,17... | collective-permute-start | bytes 884744 | tf_op jit(solution)/shard_map/ppermute | solution.py:22
  1461.0 13.9 collective-permute-start.31
  1477.0 11.3 collective-permute-start.32
  (114 other events, 806.1 us)
Sparse Core Ops, SparseCore 0:
  11.5 79.3 all-gather.17
  94.4 52.8 all-gather.19
  150.2 71.2 all-gather.13
  224.3 71.6 all-gather.15
  299.4 58.8 all-gather.21
  361.6 52.8 all-gather.23
where the time goes:
time: 1510 us; the launch traced here: 1500 us
  waiting for transfers between devices  493 us (33%)
  local copies, waits for them, and re-layouts  425 us (28%)
  other arithmetic  206 us (14%)
  matrix products  169 us (11%)
  blocking collectives  132 us (9%)
  starting transfers between devices  58.3 us (4%)
  between operations  18.2 us (1%)
    ppermute x21, waiting for transfers between devices, from_partner(): lax.ppermute(array, axis, [(i, i ^ 1 << apart) for i in range(lax.axis_si...  398 us
    unnamed x303, local copies, waits for them, and re-layouts  149 us
    unnamed x1, blocking collectives  92 us
    another operation x2, local copies, waits for them, and re-layouts, reduce_expert(): flat = jnp.stack([grad_inner.reshape(-1), grad_outer.reshape(-1)])  48 us
    ppermute x18, waiting for transfers between devices, from_behind(): return lax.ppermute(value, axis, pairs)  48 us
    dot_general x9, matrix products, cross_rows(): jnp.einsum('rd,re->de', left, right, preferred_element_type=jnp.float32)  46.9 us
    ppermute x18, starting transfers between devices, from_behind(): return lax.ppermute(value, axis, pairs)  40.6 us
    all_gather x1, blocking collectives, local(): lax.all_gather(router, 'fsdp', axis=0, tiled=True)  39.9 us
  transfers between devices with their start and end apart: 45, of which 17 were waited for; matrix products, arithmetic and copies ran while one was open for 46% of the time, Pallas kernels for 0%

commit v1 on v0

v1 whole, which is shorter than its diff:
```python
import functools

import jax
import jax.numpy as jnp
from jax import lax
from jax.experimental import pallas as pl
from jax.experimental.pallas import tpu as pltpu
from jax.sharding import PartitionSpec as P

HEADS = 12
HEAD_DIM = 64
EXPERTS = 4
CAP = 247
SLOT = 256
WIDTH = 768
HIDDEN = 3072
NORM_EPSILON = 1e-06
VMEM_BYTES = 60 << 20
F32 = jnp.float32
BF16 = jnp.bfloat16


def nn(left, right):
    return lax.dot_general(left, right, (((1,), (0,)), ((), ())), preferred_element_type=F32)


def nt(left, right):
    return lax.dot_general(left, right, (((1,), (1,)), ((), ())), preferred_element_type=F32)


def tn(left, right):
    return lax.dot_general(left, right, (((0,), (0,)), ((), ())), preferred_element_type=F32)


def tile(index, size):
    return pl.ds(pl.multiple_of(index * size, size), size)


def loop(count, body):
    pl.loop(0, count)(body)


def norm_parts(values):
    center = values - jnp.mean(values, -1, keepdims=True)
    spread = jnp.mean(center * center, -1, keepdims=True)
    scale = lax.rsqrt(spread + NORM_EPSILON)
    return center * scale, scale


def norm_rows(x_ref, gain, out_ref, block=32):
    def body(i):
        rows = tile(i, block)
        unit, _ = norm_parts(x_ref[rows, :])
        out_ref[rows, :] = (unit * gain).astype(BF16)

    loop(x_ref.shape[0] // block, body)


def norm_back(x_ref, gain, dn_ref, g_ref, dgain_ref, row, block=32):
    def body(i, total):
        rows = tile(i, block)
        unit, scale = norm_parts(x_ref[rows, :])
        dn = dn_ref[rows, :]
        scaled = dn * gain
        mean_one = jnp.mean(scaled, -1, keepdims=True)
        mean_two = jnp.mean(scaled * unit, -1, keepdims=True)
        g_ref[rows, :] = g_ref[rows, :] + scale * (scaled - mean_one - unit * mean_two)
        return total + jnp.sum((dn * unit).reshape(block // 8, 8, WIDTH), 0)

    total = lax.fori_loop(0, x_ref.shape[0] // block, body, jnp.zeros((8, WIDTH), F32))
    dgain_ref[row : row + 1, :] = jnp.sum(total, 0, keepdims=True)


def gelu_both(u):
    c = 0.7978845608
    square = u * u
    t = jnp.tanh(c * u * (1.0 + 0.044715 * square))
    half = 0.5 * (1.0 + t)
    slope = half + 0.5 * u * (1.0 - t * t) * (c + (3 * 0.044715 * c) * square)
    return u * half, slope


def halves(shape):
    lane = lax.broadcasted_iota(jnp.int32, shape, 1)
    return lane < HEAD_DIM


def head_probs(q, k, seq):
    scores = nt(q, k) * HEAD_DIM ** (-0.5)
    key = lax.broadcasted_iota(jnp.int32, scores.shape, 1)
    scores = jnp.where(key < seq, scores, -1e30)
    top = jnp.max(scores, -1, keepdims=True)
    e = jnp.exp(scores - top)
    return e / jnp.sum(e, -1, keepdims=True)


def attention_heads(qkv_ref, o_ref, images, seq):
    rows_of = qkv_ref.shape[0] // images
    for image in range(images):
        rows = pl.ds(image * rows_of, rows_of)

        def pair(p, rows=rows):
            q = qkv_ref[rows, tile(p, 128)]
            k = qkv_ref[rows, tile(p + 6, 128)]
            v = qkv_ref[rows, tile(p + 12, 128)]
            first = halves(q.shape)
            zero = jnp.zeros_like(q)
            p0 = head_probs(jnp.where(first, q, zero), k, seq).astype(BF16)
            p1 = head_probs(jnp.where(first, zero, q), k, seq).astype(BF16)
            out = nn(p0, jnp.where(first, v, zero)) + nn(p1, jnp.where(first, zero, v))
            o_ref[rows, tile(p, 128)] = out.astype(BF16)

        loop(6, pair)


def attention_forward(x_ref, gain, w_ref, xo_ref, an_ref, qkv_ref, o_ref, images, seq):
    norm_rows(x_ref, gain, an_ref)

    def project(n):
        qkv_ref[:, tile(n, 256)] = nn(an_ref[...], w_ref[:, tile(n, 256)]).astype(BF16)

    loop(9, project)
    attention_heads(qkv_ref, o_ref, images, seq)

    def outward(n):
        cols = tile(n, 256)
        xo_ref[:, cols] = x_ref[:, cols] + nn(o_ref[...], w_ref[:, tile(n + 9, 256)])

    loop(3, outward)


def attention_backward(
    g_ref, x_ref, gain, w_ref, an_ref, qkv_ref, o_ref, dw_ref, dgain_ref, row, images, seq,
    low_ref, do_ref, dqkv_ref, dn_ref,
):
    rows_of = qkv_ref.shape[0] // images
    low_ref[...] = g_ref[...].astype(BF16)

    def outward(n):
        dw_ref[:, tile(n + 9, 256)] = tn(o_ref[...], low_ref[:, tile(n, 256)]).astype(BF16)
        do_ref[:, tile(n, 256)] = nt(low_ref[...], w_ref[tile(n, 256), 2304:]).astype(BF16)

    loop(3, outward)
    for image in range(images):
        rows = pl.ds(image * rows_of, rows_of)

        def pair(p, rows=rows):
            q = qkv_ref[rows, tile(p, 128)]
            k = qkv_ref[rows, tile(p + 6, 128)]
            v = qkv_ref[rows, tile(p + 12, 128)]
            d = do_ref[rows, tile(p, 128)]
            first = halves(q.shape)
            zero = jnp.zeros_like(q)
            dq = dk = dv = None
            for mine in (first, ~first):
                qm, km, dm = (jnp.where(mine, t, zero) for t in (q, k, d))
                probs = head_probs(qm, k, seq)
                dp = nt(dm, v)
                inner = jnp.sum(dp * probs, -1, keepdims=True)
                ds = (probs * (dp - inner)).astype(BF16)
                one = (nn(ds, km), tn(ds, qm), tn(probs.astype(BF16), dm))
                dq, dk, dv = one if dq is None else (dq + one[0], dk + one[1], dv + one[2])
            scale = HEAD_DIM ** (-0.5)
            dqkv_ref[rows, tile(p, 128)] = (dq * scale).astype(BF16)
            dqkv_ref[rows, tile(p + 6, 128)] = (dk * scale).astype(BF16)
            dqkv_ref[rows, tile(p + 12, 128)] = dv.astype(BF16)

        loop(6, pair)

    def inward(n):
        dw_ref[:, tile(n, 256)] = tn(an_ref[...], dqkv_ref[:, tile(n, 256)]).astype(BF16)

    loop(9, inward)

    def normed(n):
        dn_ref[:, tile(n, 256)] = nt(dqkv_ref[...], w_ref[tile(n, 256), :2304])

    loop(3, normed)
    norm_back(x_ref, gain, dn_ref, g_ref, dgain_ref, row)


def forward_kernel(
    images, seq,
    x0_ref, g4_ref, ids_ref, small_ref, wa0_ref, wmi_ref, wmo_ref, wa1_ref,
    x1_ref, x2_ref, x3_ref, an0_ref, qkv0_ref, o0_ref, mn_ref, slope_ref, ma_ref,
    an1_ref, qkv1_ref, o1_ref, en_ref, aux_ref, g0_ref, g1_ref, rx_ref, rd_ref,
    xf_ref,
):
    rows = x0_ref.shape[0]
    xf_ref[...] = x0_ref[...].astype(F32)
    attention_forward(
        xf_ref, small_ref[0:1, :], wa0_ref, x1_ref, an0_ref, qkv0_ref, o0_ref, images, seq
    )
    norm_rows(x1_ref, small_ref[2:3, :], mn_ref)
    x2_ref[...] = x1_ref[...]

    def dense(n):
        cols = tile(n, 512)
        active, slope = gelu_both(nn(mn_ref[...], wmi_ref[:, cols]))
        slope_ref[:, cols] = slope.astype(BF16)
        active = active.astype(BF16)
        ma_ref[:, cols] = active
        x2_ref[...] += nn(active, wmo_ref[cols, :])

    loop(6, dense)
    attention_forward(
        x2_ref, small_ref[1:2, :], wa1_ref, x3_ref, an1_ref, qkv1_ref, o1_ref, images, seq
    )
    norm_rows(x3_ref, small_ref[3:4, :], en_ref)
    logits = nt(en_ref[...], small_ref[8:136, :].astype(BF16))
    lane = lax.broadcasted_iota(jnp.int32, logits.shape, 1)
    logits = jnp.where(lane < EXPERTS, logits, -1e30)
    e = jnp.exp(logits - jnp.max(logits, -1, keepdims=True))
    chances = e / jnp.sum(e, -1, keepdims=True)
    ids = ids_ref[...]
    chosen = [(ids[:, j : j + 1] == lane).astype(F32) for j in range(2)]
    row_i = lax.broadcasted_iota(jnp.int32, (rows, rows), 0)
    row_j = lax.broadcasted_iota(jnp.int32, (rows, rows), 1)
    earlier = nn((row_j < row_i).astype(BF16), (chosen[0] + chosen[1]).astype(BF16))
    place = lax.broadcasted_iota(jnp.int32, (rows, EXPERTS * SLOT), 1)
    gates = []
    for j, pick_ref in ((0, g0_ref), (1, g1_ref)):
        gates.append(jnp.sum(chances * chosen[j], -1, keepdims=True))
        inside = jnp.sum(earlier * chosen[j], -1, keepdims=True).astype(jnp.int32)
        slot = jnp.where(ids[:, j : j + 1] >= 0, ids[:, j : j + 1] * SLOT + inside, -1)
        pick_ref[...] = (slot == place).astype(BF16)
    aux = jnp.where(lane < EXPERTS, chances, 0.0)
    aux = jnp.where(lane == 8, gates[0], aux)
    aux_ref[...] = jnp.where(lane == 9, gates[1], aux)

    def fill(n):
        cols = tile(n, 256)
        both = g0_ref[:, cols] + g1_ref[:, cols]
        rx_ref[cols, :] = tn(both, en_ref[...]).astype(BF16)
        g4 = g4_ref[...].astype(F32)
        one = tn(g0_ref[:, cols], (g4 * gates[0]).astype(BF16))
        two = tn(g1_ref[:, cols], (g4 * gates[1]).astype(BF16))
        rd_ref[cols, :] = (one + two).astype(BF16)

    loop(EXPERTS, fill)


def expert_kernel(x_ref, d_ref, wi_ref, wo_ref, y_ref, dx_ref, dwi_ref, dwo_ref, yf_ref, df_ref):
    yf_ref[...] = jnp.zeros_like(yf_ref)
    df_ref[...] = jnp.zeros_like(df_ref)

    def body(n):
        cols = tile(n, 512)
        active, slope = gelu_both(nn(x_ref[...], wi_ref[:, cols]))
        active = active.astype(BF16)
        yf_ref[...] += nn(active, wo_ref[cols, :])
        dwo_ref[cols, :] = tn(active, d_ref[...]).astype(BF16)
        dh = (slope * nt(d_ref[...], wo_ref[cols, :])).astype(BF16)
        df_ref[...] += nt(dh, wi_ref[:, cols])
        dwi_ref[:, cols] = tn(x_ref[...], dh).astype(BF16)

    loop(6, body)
    y_ref[...] = yf_ref[...].astype(BF16)
    dx_ref[...] = df_ref[...].astype(BF16)


def combine_kernel(
    g4_ref, small_ref, x3_ref, en_ref, aux_ref, g0_ref, g1_ref, yr_ref, dr_ref,
    x4_ref, g_ref, ds_ref,
    dn_ref,
):
    aux = aux_ref[...]
    lane = lax.broadcasted_iota(jnp.int32, aux.shape, 1)
    g_ref[...] = g4_ref[...].astype(F32)
    x4_ref[...] = x3_ref[...]
    dgates = []
    chosen = []
    expert_of = lax.broadcasted_iota(jnp.int32, (EXPERTS * SLOT, 128), 0) // SLOT
    spread = (expert_of == lax.broadcasted_iota(jnp.int32, expert_of.shape, 1)).astype(BF16)
    for j, pick_ref in ((0, g0_ref), (1, g1_ref)):
        picked = nn(pick_ref[...], yr_ref[...])
        x4_ref[...] += aux[:, 8 + j : 9 + j] * picked
        dgates.append(jnp.sum(g_ref[...] * picked, -1, keepdims=True))
        chosen.append(nn(pick_ref[...], spread))
    dr = dgates[0] * chosen[0] + dgates[1] * chosen[1]
    chances = jnp.where(lane < EXPERTS, aux, 0.0)
    dlogits = chances * (dr - jnp.sum(chances * dr, -1, keepdims=True))
    dlogits = jnp.where(lane < EXPERTS, dlogits, 0.0).astype(BF16)
    ds_ref[...] = jnp.zeros_like(ds_ref)
    ds_ref[4:8, :] = tn(dlogits, en_ref[...])[0:4, :]
    dn_ref[...] = nn(dlogits, small_ref[8:136, :].astype(BF16)) + nn(
        g0_ref[...] + g1_ref[...], dr_ref[...]
    )
    norm_back(x3_ref, small_ref[3:4, :], dn_ref, g_ref, ds_ref, 3)


def attention_back_kernel(
    images, seq, row,
    g_in_ref, small_ref, x_ref, w_ref, an_ref, qkv_ref, o_ref,
    g_ref, dw_ref, ds_ref,
    xf_ref, low_ref, do_ref, dqkv_ref, dn_ref,
):
    g_ref[...] = g_in_ref[...]
    xf_ref[...] = x_ref[...].astype(F32)
    ds_ref[...] = jnp.zeros_like(ds_ref)
    attention_backward(
        g_ref, xf_ref, small_ref[row : row + 1, :], w_ref, an_ref, qkv_ref, o_ref, dw_ref,
        ds_ref, row, images, seq, low_ref, do_ref, dqkv_ref, dn_ref,
    )


def dense_back_kernel(
    g_in_ref, small_ref, x1_ref, wmi_ref, wmo_ref, mn_ref, slope_ref, ma_ref,
    g_ref, dwmi_ref, dwmo_ref, ds_ref,
    low_ref, dn_ref,
):
    g_ref[...] = g_in_ref[...]
    ds_ref[...] = jnp.zeros_like(ds_ref)
    low_ref[...] = g_ref[...].astype(BF16)
    dn_ref[...] = jnp.zeros_like(dn_ref)

    def dense(n):
        cols = tile(n, 512)
        dwmo_ref[cols, :] = tn(ma_ref[:, cols], low_ref[...]).astype(BF16)
        dact = nt(low_ref[...], wmo_ref[cols, :])
        dh = (slope_ref[:, cols].astype(F32) * dact).astype(BF16)
        dwmi_ref[:, cols] = tn(mn_ref[...], dh).astype(BF16)
        dn_ref[...] += nt(dh, wmi_ref[:, cols])

    loop(6, dense)
    norm_back(x1_ref, small_ref[2:3, :], dn_ref, g_ref, ds_ref, 2)


def struct(shape, dtype):
    return jax.ShapeDtypeStruct(shape, dtype)


def call(body, outs, scratch, args, flops):
    total = sum(a.size * a.dtype.itemsize for a in list(args) + list(outs))
    return pl.pallas_call(
        body,
        out_shape=outs,
        in_specs=[pl.BlockSpec(memory_space=pltpu.VMEM)] * len(args),
        out_specs=[pl.BlockSpec(memory_space=pltpu.VMEM)] * len(outs),
        scratch_shapes=scratch,
        compiler_params=pltpu.CompilerParams(vmem_limit_bytes=VMEM_BYTES),
        cost_estimate=pl.CostEstimate(flops=flops, bytes_accessed=total, transcendentals=0),
    )(*args)


def run_forward(images, seq, x0, g4, ids, small, wa0, wmi, wmo, wa1):
    rows = x0.shape[0]
    act = struct((rows, WIDTH), F32)
    low = struct((rows, WIDTH), BF16)
    qkv = struct((rows, 3 * WIDTH), BF16)
    hid = struct((rows, HIDDEN), BF16)
    pick = struct((rows, EXPERTS * SLOT), BF16)
    buf = struct((EXPERTS * SLOT, WIDTH), BF16)
    outs = [act, act, act, low, qkv, low, low, hid, hid, low, qkv, low, low,
            struct((rows, 128), F32), pick, pick, buf, buf]
    return call(
        functools.partial(forward_kernel, images, seq), outs,
        [pltpu.VMEM((rows, WIDTH), F32)],
        [x0, g4, ids, small, wa0, wmi, wmo, wa1], 8_000_000_000,
    )


def run_expert(x, d, wi, wo):
    outs = [struct(x.shape, BF16), struct(x.shape, BF16), struct(wi.shape, BF16), struct(wo.shape, BF16)]
    return call(
        expert_kernel, outs, [pltpu.VMEM(x.shape, F32), pltpu.VMEM(x.shape, F32)],
        [x, d, wi, wo], 30_000_000_000,
    )


def run_backward(images, seq, x0, g4, small, weights, saved, y_back, d_back):
    rows = x0.shape[0]
    act = struct((rows, WIDTH), F32)
    wide, tall = struct((WIDTH, HIDDEN), BF16), struct((HIDDEN, WIDTH), BF16)
    row = struct((8, WIDTH), F32)
    wa0, wmi, wmo, wa1 = weights
    x1, x2, x3, an0, qkv0, o0, mn, slope, ma, an1, qkv1, o1, en, aux, p0, p1 = saved
    full = pltpu.VMEM((rows, WIDTH), F32)
    low = pltpu.VMEM((rows, WIDTH), BF16)
    mixed = pltpu.VMEM((rows, 3 * WIDTH), BF16)
    x4, g, s0 = call(
        combine_kernel, [act, act, row], [full],
        [g4, small, x3, en, aux, p0, p1, y_back, d_back], 3_000_000_000,
    )
    g, dwa1, s1 = call(
        functools.partial(attention_back_kernel, images, seq, 1), [act, wide, row],
        [full, low, low, mixed, full], [g, small, x2, wa1, an1, qkv1, o1], 5_000_000_000,
    )
    g, dwmi, dwmo, s2 = call(
        dense_back_kernel, [act, wide, tall, row], [low, full],
        [g, small, x1, wmi, wmo, mn, slope, ma], 8_000_000_000,
    )
    g, dwa0, s3 = call(
        functools.partial(attention_back_kernel, images, seq, 0), [act, wide, row],
        [full, low, low, mixed, full], [g, small, x0, wa0, an0, qkv0, o0], 5_000_000_000,
    )
    return x4, g, dwa0, dwmi, dwmo, dwa1, s0 + s1 + s2 + s3


def gather_rows(piece):
    return lax.all_gather(piece, "fsdp", axis=0, tiled=True)


def shift(values, steps):
    count = lax.axis_size("fsdp")
    return lax.ppermute(values, "fsdp", [(s, (s + steps) % count) for s in range(count)])


def group_exchange(rows, group_size, group_id):
    out = jnp.zeros_like(rows)
    for offset in range(EXPERTS):
        piece = lax.dynamic_index_in_dim(rows, (group_id + offset) % EXPERTS, 0, keepdims=False)
        if offset:
            piece = shift(piece, offset * group_size)
        out = lax.dynamic_update_index_in_dim(out, piece, (group_id - offset) % EXPERTS, 0)
    return out


def plain_gather(smalls, wide, tall, e_in, e_out):
    n = lax.axis_size("fsdp")
    group_size = n // EXPERTS
    group = lax.axis_index("fsdp") // group_size
    small = gather_rows(smalls)
    wides = [gather_rows(w) for w in wide]
    talls = [gather_rows(w) for w in tall]
    big_in = lax.dynamic_index_in_dim(gather_rows(e_in), group, 1, keepdims=False)
    big_out = lax.dynamic_index_in_dim(gather_rows(e_out), group, 1, keepdims=False)
    return small, wides, talls, big_in, big_out


def plain_reduce(grad):
    return lax.psum_scatter(grad, "fsdp", scatter_dimension=0, tiled=True)


def plain_reduce_expert(grad):
    n = lax.axis_size("fsdp")
    group_size = n // EXPERTS
    group = lax.axis_index("fsdp") // group_size
    full = jnp.zeros((grad.shape[0], EXPERTS, grad.shape[1]), BF16)
    full = lax.dynamic_update_index_in_dim(full, grad, group, 1)
    return plain_reduce(full)

MESH_ID = pl.DeviceIdType.MESH


class Place:
    def __init__(self):
        self.me = lax.axis_index("fsdp")
        self.core = self.me % 2
        self.x = self.me // 2 % 2
        self.y = self.me // 4 % 2
        self.z = self.me // 8
        self.sibling = self.me + 1 - 2 * self.core
        self.across_x = self.me + 2 - 4 * self.x
        self.across_y = self.me + 4 - 8 * self.y
        self.across_both = self.across_x + 4 - 8 * self.y
        self.chip = self.me // 2 % 4


def remote(src, dst, send, recv, device):
    return pltpu.make_async_remote_copy(
        src_ref=src, dst_ref=dst, send_sem=send, recv_sem=recv,
        device_id=(device,), device_id_type=MESH_ID,
    )


def greet_all(place, count):
    barrier = pltpu.get_barrier_semaphore()

    def hello(i):
        pl.semaphore_signal(
            barrier, inc=1, device_id=((place.me + i) % count,), device_id_type=MESH_ID
        )

    pl.loop(1, count)(hello)
    pl.semaphore_wait(barrier, count - 1)


DENSE = ("wide", "wide", "tall", "wide")


def part(ref, kind, z, y, x, core, half):
    if kind == "wide":
        return ref.at[z, y, x, :, pl.ds(pl.multiple_of(core * 1536 + half * 768, 128), 768)]
    return ref.at[z, y, x, pl.ds(pl.multiple_of(core * 96 + half * 48, 16), 48), :]


def own_part(mine, kind, half):
    if kind == "wide":
        return mine.at[:, pl.ds(half * 768, 768)]
    return mine.at[pl.ds(half * 48, 48), :]


class Gather:
    def __init__(self, place, kind, mine, out, sems):
        self.p, self.kind, self.mine, self.out, self.sems = place, kind, mine, out, sems

    def _z(self, half, source, up):
        p = self.p
        where = part(self.out, self.kind, source, p.y, p.x, p.core, half)
        return where, 0 if up else 1

    def _slot(self, half, source):
        return half * 4 + source

    def start_own(self):
        p, s = self.p, self.sems
        for half in range(2):
            there = part(self.out, self.kind, p.z, p.y, p.x, p.core, half)
            src = own_part(self.mine, self.kind, half)
            pltpu.make_async_copy(src, there, s["own"].at[half]).start()
            self._along_z(half, p.z, src, True, True)

    def _copy_z(self, half, source, src, up):
        p, s = self.p, self.sems
        slot = self._slot(half, source)
        there = part(self.out, self.kind, source, p.y, p.x, p.core, half)
        name = "zu" if up else "zd"
        return remote(there if src is None else src, there, s[name].at[slot], s["zr"].at[slot],
                      p.me + 8 if up else p.me - 8)

    def _along_z(self, half, source, src, up, down):
        p = self.p
        if up:
            pl.when(p.z < 3)(lambda: self._copy_z(half, source, src, True).start())
        if down:
            pl.when(p.z > 0)(lambda: self._copy_z(half, source, src, False).start())

    def _first(self, half, source, src=None):
        p, s = self.p, self.sems
        slot = self._slot(half, source)
        there = part(self.out, self.kind, source, p.y, p.x, p.core, half)
        return remote(there if src is None else src, there, s["fs"].at[slot], s["fr"].at[slot],
                      p.across_y if half else p.across_x)

    def _line(self, half, source):
        p = self.p
        if self.kind == "wide":
            rows, cols = slice(None), pl.ds(pl.multiple_of(p.core * 1536 + half * 768, 128), 768)
        else:
            rows, cols = pl.ds(pl.multiple_of(p.core * 96 + half * 48, 16), 48), slice(None)
        if half:
            return self.out.at[source, :, p.x, rows, cols]
        return self.out.at[source, p.y, :, rows, cols]

    def _second(self, half, source):
        p, s = self.p, self.sems
        slot = self._slot(half, source)
        line = self._line(half, source)
        return remote(line, line, s["ss"].at[slot], s["sr"].at[slot],
                      p.across_x if half else p.across_y)

    def _hand(self, half, source):
        p, s = self.p, self.sems
        slot = self._slot(half, source)
        if self.kind == "wide":
            rows, cols = slice(None), pl.ds(pl.multiple_of(p.core * 1536 + half * 768, 128), 768)
        else:
            rows, cols = pl.ds(pl.multiple_of(p.core * 96 + half * 48, 16), 48), slice(None)
        plane = self.out.at[source, :, :, rows, cols]
        return remote(plane, plane, s["hs"].at[slot], s["hr"].at[slot], p.sibling)

    def valid(self, k):
        z = self.p.z + k
        return (z >= 0) & (z <= 3)

    def stage_one(self, half, k):
        source = self.p.z + k

        def run():
            if k == 0:
                src = own_part(self.mine, self.kind, half)
                self._first(half, source, src).start()
                there = part(self.out, self.kind, source, self.p.y, self.p.x, self.p.core, half)
                pltpu.make_async_copy(src, there, self.sems["own"].at[half]).wait()
                return
            self._copy_z(half, source, None, k < 0).wait_recv()
            self._along_z(half, source, None, k < 0, k > 0)
            self._first(half, source).start()

        pl.when(self.valid(k))(run)

    def stage_two(self, half, k):
        source = self.p.z + k

        def run():
            self._first(half, source).wait_recv()
            self._second(half, source).start()

        pl.when(self.valid(k))(run)

    def stage_three(self, half, k):
        source = self.p.z + k

        def run():
            self._second(half, source).wait_recv()
            self._hand(half, source).start()

        pl.when(self.valid(k))(run)

    def arrived(self):
        for half in range(2):
            for source in range(4):
                self._hand(half, source).wait_recv()

    def finish(self):
        p = self.p
        for half in range(2):
            for source in range(4):
                self._first(half, source).wait_send()
                self._second(half, source).wait_send()
                self._hand(half, source).wait_send()
                up = (source <= p.z) & (p.z < 3)
                down = (source >= p.z) & (p.z > 0)
                pl.when(up)(lambda: self._copy_z(half, source, None, True).wait_send())
                pl.when(down)(lambda: self._copy_z(half, source, None, False).wait_send())


GATHER_SEMS = ("zu", "zd", "zr", "fs", "fr", "ss", "sr", "hs", "hr")


def expert_block(ref, kind, z, y, core):
    if kind == "wide":
        return ref.at[z, y, :, :, pl.ds(pl.multiple_of(core * 1536, 128), 1536)]
    return ref.at[z, y, :, pl.ds(pl.multiple_of(core * 96, 16), 96), :]


def expert_piece(ref, kind, z, y, x, core):
    if kind == "wide":
        return ref.at[z, y, x, :, pl.ds(pl.multiple_of(core * 1536, 128), 1536)]
    return ref.at[z, y, x, pl.ds(pl.multiple_of(core * 96, 16), 96), :]


class ExpertGather:
    def __init__(self, place, kind, mine, out, sems):
        self.p, self.kind, self.mine, self.out, self.sems = place, kind, mine, out, sems

    def _cross(self, i):
        p, s = self.p, self.sems
        there = expert_piece(self.out, self.kind, p.z, p.y, p.x, p.core)
        device = (p.across_x, p.across_y, p.across_both)[i]
        expert = device // 2 % 4
        return remote(self.mine.at[expert], there, s["cs"].at[i], s["cr"].at[i], device)

    def _own(self):
        p = self.p
        there = expert_piece(self.out, self.kind, p.z, p.y, p.x, p.core)
        return pltpu.make_async_copy(self.mine.at[p.chip], there, self.sems["own"].at[0])

    def start_own(self):
        self._own().start()
        for i in range(3):
            self._cross(i).start()

    def _copy_z(self, y, source, up):
        p, s = self.p, self.sems
        slot = y * 4 + source
        block = expert_block(self.out, self.kind, source, y, p.core)
        return remote(block, block, s["zu" if up else "zd"].at[slot], s["zr"].at[slot],
                      p.me + 8 if up else p.me - 8)

    def _hand(self, y, source):
        p, s = self.p, self.sems
        slot = y * 4 + source
        block = expert_block(self.out, self.kind, source, y, p.core)
        return remote(block, block, s["hs"].at[slot], s["hr"].at[slot], p.sibling)

    def crossed(self):
        p = self.p
        self._own().wait()
        for i in range(3):
            self._cross(i).wait_recv()
        for y in range(2):
            pl.when(p.z < 3)(lambda: self._copy_z(y, p.z, True).start())
            pl.when(p.z > 0)(lambda: self._copy_z(y, p.z, False).start())
            self._hand(y, p.z).start()

    def stage(self, y, k):
        p = self.p
        source = p.z + k

        def run():
            self._copy_z(y, source, k < 0).wait_recv()
            if k < 0:
                pl.when(p.z < 3)(lambda: self._copy_z(y, source, True).start())
            else:
                pl.when(p.z > 0)(lambda: self._copy_z(y, source, False).start())
            self._hand(y, source).start()

        pl.when((source >= 0) & (source <= 3))(run)

    def arrived(self):
        for y in range(2):
            for source in range(4):
                self._hand(y, source).wait_recv()

    def finish(self):
        p = self.p
        for i in range(3):
            self._cross(i).wait_send()
        for y in range(2):
            for source in range(4):
                self._hand(y, source).wait_send()
                up = (source <= p.z) & (p.z < 3)
                down = (source >= p.z) & (p.z > 0)
                pl.when(up)(lambda: self._copy_z(y, source, True).wait_send())
                pl.when(down)(lambda: self._copy_z(y, source, False).wait_send())


EXPERT_SEMS = ("zu", "zd", "zr", "hs", "hr")
STEPS = (0, -1, 1, -2, 2, -3, 3)


def gather_kernel(
    small_in, wide_in, tall_in,
    small_out, wa0, wmi, wmo, wa1, ein, eout,
    wide_mine, expert_mine, from_sibling, meet, small_sems, gather_sems, own_sems, expert_sems,
    cross_sems,
):
    p = Place()
    greet_all(p, 32)
    swap = remote(wide_in.at[1 - p.core], from_sibling, meet.at[0], meet.at[1], p.sibling)
    swap.start()

    def spread(i):
        remote(small_in, small_out.at[p.me], small_sems.at[0, i], small_sems.at[1, p.me],
               (p.me + i) % 32).start()

    pl.loop(1, 32)(spread)
    small_out[p.me] = small_in[...]
    outs = (wa0, wmi, wmo, wa1)
    dense = []
    for m, kind in enumerate(DENSE):
        sems = {name: gather_sems.at[m, i] for i, name in enumerate(GATHER_SEMS)}
        sems["own"] = own_sems.at[m]
        mine = tall_in.at[0] if kind == "tall" else wide_mine.at[(0, 1, None, 2)[m]]
        dense.append(Gather(p, kind, mine, outs[m], sems))
    experts = []
    for m, kind in enumerate(("wide", "tall")):
        sems = {name: expert_sems.at[m, i] for i, name in enumerate(EXPERT_SEMS)}
        sems["cs"], sems["cr"], sems["own"] = (
            cross_sems.at[m, 0], cross_sems.at[m, 1], cross_sems.at[m, 2])
        mine = tall_in.at[pl.ds(1, 4)] if kind == "tall" else expert_mine
        experts.append(ExpertGather(p, kind, mine, (ein, eout)[m], sems))
    dense[2].start_own()
    experts[1].start_own()
    swap.wait_recv()

    def merge(m, out):
        cols = pl.ds(m * 1536, 1536)
        kept = wide_in[p.core, :, cols]
        came = from_sibling[:, cols]
        upper = jnp.where(p.core == 0, kept, came)
        lower = jnp.where(p.core == 0, came, kept)
        out[...] = jnp.concatenate([upper, lower], 0).astype(BF16)

    merge(0, wide_mine.at[0])
    dense[0].start_own()
    for e in range(4):
        merge(3 + e, expert_mine.at[e])
    experts[0].start_own()
    merge(1, wide_mine.at[1])
    dense[1].start_own()
    merge(2, wide_mine.at[2])
    dense[3].start_own()

    order = [(m, k, half) for m in (0, 1, 2, 3) for k in STEPS for half in range(2)]
    pumps = []
    for i in range(len(order) + 16):
        for stage, lag in ((0, 0), (1, 8), (2, 16)):
            if 0 <= i - lag < len(order):
                pumps.append((stage,) + order[i - lag])
    turns = [(y, k, m) for k in STEPS[1:] for m in (1, 0) for y in range(2)]
    at = {8 + j * (len(pumps) - 10) // len(turns): turn for j, turn in enumerate(turns)}
    for i, (stage, m, k, half) in enumerate(pumps):
        if i == 6:
            experts[1].crossed()
            experts[0].crossed()
        if i in at:
            y, kk, mm = at[i]
            experts[mm].stage(y, kk)
        job = dense[m]
        (job.stage_one, job.stage_two, job.stage_three)[stage](half, k)
    for job in dense + experts:
        job.arrived()
    for job in dense + experts:
        job.finish()
    swap.wait_send()

    def spread_done(i):
        remote(small_in, small_out.at[(p.me + i) % 32], small_sems.at[0, i],
               small_sems.at[1, (p.me + i) % 32], (p.me + i) % 32).wait()

    pl.loop(1, 32)(spread_done)


def run_gather(small, wide, tall):
    any_space = pl.BlockSpec(memory_space=pl.ANY)
    vmem = pl.BlockSpec(memory_space=pltpu.VMEM)
    wide_out = struct((4, 2, 2, 48, 3072), BF16)
    tall_out = struct((4, 2, 2, 192, 768), BF16)
    dma = pltpu.SemaphoreType.DMA
    return pl.pallas_call(
        gather_kernel,
        out_shape=[struct((32, 8, 128), F32), wide_out, wide_out, tall_out, wide_out,
                   wide_out, tall_out],
        in_specs=[vmem, vmem, vmem],
        out_specs=[vmem] + [any_space] * 6,
        scratch_shapes=[
            pltpu.VMEM((3, 48, 1536), BF16),
            pltpu.VMEM((4, 48, 1536), BF16),
            pltpu.VMEM((24, 7 * 1536), F32),
            dma((2,)),
            dma((2, 32)),
            dma((4, len(GATHER_SEMS), 8)),
            dma((4, 2)),
            dma((2, len(EXPERT_SEMS), 8)),
            dma((2, 3, 3)),
        ],
        compiler_params=pltpu.CompilerParams(
            collective_id=0, has_side_effects=True, vmem_limit_bytes=VMEM_BYTES),
        cost_estimate=pl.CostEstimate(flops=0, bytes_accessed=60_000_000, transcendentals=0),
    )(small, wide, tall)

KINDS = ("wide", "tall", "wide", "tall", "wide", "wide")
WIDE_AT = {2: 2, 4: 1, 5: 0}
FAR_FIRST = (-3, 3, -2, 2, -1, 1, 0)


def plane_part(ref, kind, z, core, half):
    if kind == "wide":
        return ref.at[z, :, :, :, pl.ds(pl.multiple_of(core * 1536 + half * 768, 128), 768)]
    return ref.at[z, :, :, pl.ds(pl.multiple_of(core * 96 + half * 48, 16), 48), :]


def add_into(kept, came, pieces):
    def body(i):
        rows = pl.ds(pl.multiple_of(i % 3 * 16, 16), 16)
        a, b = kept(i // 3), came(i // 3)
        a[rows, :] = (a[rows, :].astype(F32) + b[rows, :].astype(F32)).astype(BF16)

    loop(pieces * 3, body)


class Reduce:
    def __init__(self, place, m, ref, own, near, bufs, sems, sink):
        self.p, self.m, self.kind, self.ref = place, m, KINDS[m], ref
        self.own, self.near, self.bufs, self.sems, self.sink = own, near, bufs, sems, sink

    def _load(self, half, z):
        src = plane_part(self.ref, self.kind, z, self.p.core, half)
        return pltpu.make_async_copy(src, self.own.at[z, half], self.sems["load"].at[z, half])

    def _pair(self, half, z):
        p, s = self.p, self.sems
        src = plane_part(self.ref, self.kind, z, 1 - p.core, half)
        return remote(src, self.near.at[z, half], s["ps"].at[z, half], s["pr"].at[z, half], p.sibling)

    def start(self, k):
        z = self.p.z + k

        def run():
            for half in range(2):
                self._load(half, z).start()
                self._pair(half, z).start()

        pl.when(self.valid(k))(run)

    def valid(self, k):
        z = self.p.z + k
        return (z >= 0) & (z <= 3)

    def pair_sum(self, half, k):
        z = self.p.z + k
        self._load(half, z).wait()
        self._pair(half, z).wait_recv()
        own, near = self.own.at[z, half], self.near.at[z, half]
        add_into(lambda i: own.at[i // 2, i % 2], lambda i: near.at[i // 2, i % 2], 4)

    def _block(self, half, z):
        raise NotImplementedError

    def _send_z(self, half, z, up):
        p, s = self.p, self.sems
        side = 0 if up else 1
        return remote(self._block(half, z), self.bufs["z"].at[half, z, side], s["zs"].at[half, z],
                      s["zr"].at[half, z, side], p.me + 8 if up else p.me - 8)

    def _wait_z(self, half, z, up):
        p, s = self.p, self.sems
        side = 0 if up else 1
        remote(self._block(half, z), self.bufs["z"].at[half, z, side], s["zs"].at[half, z],
               s["zr"].at[half, z, side], p.me).wait_recv()

    def along_z(self, half, k):
        p = self.p
        z = p.z + k
        if k == 0:
            self.end_z(half)
            return
        up = k > 0

        def join():
            self._wait_z(half, z, up)
            self._add_z(half, z, 0 if up else 1)

        pl.when(p.z > 0 if up else p.z < 3)(join)
        self._send_z(half, z, up).start()

    def finish(self):
        p = self.p
        for half in range(2):
            for z in range(4):
                self._pair(half, z).wait_send()
                pl.when(p.z != z)(lambda: self._send_z(half, z, True).wait_send())


class DenseReduce(Reduce):
    def _block(self, half, z):
        return self.own.at[z, half, self.p.y, self.p.x]

    def _add_z(self, half, z, side):
        kept, came = self._block(half, z), self.bufs["z"].at[half, z, side]
        add_into(lambda i: kept, lambda i: came, 1)

    def _first(self, half, z):
        p, s = self.p, self.sems
        src = self.own.at[z, half, :, 1 - p.x] if half else self.own.at[z, half, 1 - p.y]
        return remote(src, self.bufs["first"].at[z, half], s["fs"].at[z, half], s["fr"].at[z, half],
                      p.across_x if half else p.across_y)

    def _second(self, half, z):
        p, s = self.p, self.sems
        src = self.own.at[z, half, 1 - p.y, p.x] if half else self.own.at[z, half, p.y, 1 - p.x]
        return remote(src, self.bufs["second"].at[z, half], s["ss"].at[z, half],
                      s["sr"].at[z, half], p.across_y if half else p.across_x)

    def stage_one(self, half, k):
        def run():
            self.pair_sum(half, k)
            self._first(half, self.p.z + k).start()

        pl.when(self.valid(k))(run)

    def stage_two(self, half, k):
        p = self.p
        z = p.z + k

        def run():
            self._first(half, z).wait_recv()
            own, came = self.own.at[z, half], self.bufs["first"].at[z, half]
            if half:
                add_into(lambda i: own.at[i, p.x], lambda i: came.at[i], 2)
            else:
                add_into(lambda i: own.at[p.y, i], lambda i: came.at[i], 2)
            self._second(half, z).start()

        pl.when(self.valid(k))(run)

    def stage_three(self, half, k):
        z = self.p.z + k

        def run():
            self._second(half, z).wait_recv()
            kept, came = self._block(half, z), self.bufs["second"].at[z, half]
            add_into(lambda i: kept, lambda i: came, 1)
            self.along_z(half, k)

        pl.when(self.valid(k))(run)

    def end_z(self, half):
        p = self.p
        kept, got = self._block(half, p.z), self.bufs["z"]
        out = self.sink(half)
        out[...] = kept[...].astype(F32)

        def join(side):
            self._wait_z(half, p.z, side == 0)
            out[...] += got[half, p.z, side].astype(F32)

        pl.when(p.z > 0)(lambda: join(0))
        pl.when(p.z < 3)(lambda: join(1))

    def finish(self):
        super().finish()
        for half in range(2):
            for z in range(4):
                self._first(half, z).wait_send()
                self._second(half, z).wait_send()


class ExpertReduce(Reduce):
    def _block(self, half, z):
        return self.own.at[z, half]

    def _add_z(self, half, z, side):
        kept, came = self._block(half, z), self.bufs["z"].at[half, z, side]
        add_into(lambda i: kept.at[i // 2, i % 2], lambda i: came.at[i // 2, i % 2], 4)

    def stage_one(self, half, k):
        def run():
            self.pair_sum(half, k)
            self.along_z(half, k)

        pl.when(self.valid(k))(run)

    def _cross(self, half, i):
        p, s = self.p, self.sems
        device = (p.across_x, p.across_y, p.across_both)[i]
        chip = device // 2 % 4
        src = self.own.at[p.z, half, chip // 2, chip % 2]
        return remote(src, self.bufs["cross"].at[half, i], s["cs"].at[half, i], s["cr"].at[half, i], device)

    def end_z(self, half):
        p = self.p
        pl.when(p.z > 0)(lambda: (self._wait_z(half, p.z, True), self._add_z(half, p.z, 0)) and None)
        pl.when(p.z < 3)(lambda: (self._wait_z(half, p.z, False), self._add_z(half, p.z, 1)) and None)
        for i in range(3):
            self._cross(half, i).start()

    def crossed(self, half):
        p = self.p
        self.sink(half, p.chip)[...] = self.own[p.z, half, p.y, p.x].astype(F32)
        for i in range(3):
            self._cross(half, i).wait_recv()
            device = (p.across_x, p.across_y, p.across_both)[i]
            self.sink(half, device // 2 % 4)[...] = self.bufs["cross"][half, i].astype(F32)

    def finish(self):
        super().finish()
        for half in range(2):
            for i in range(3):
                self._cross(half, i).wait_send()


def reduce_kernel(
    small_in, ein, eout, wa1, wmo, wmi, wa0,
    small_out, wide_out, tall_out,
    own, near, first, second, z_dense, z_expert, cross, done, small_got,
    load_sems, pair_sems, plane_sems, zs_sems, zr_sems, cross_sems, small_sems, meet,
):
    p = Place()
    greet_all(p, 32)
    jobs = []
    for m, ref in enumerate((ein, eout, wa1, wmo, wmi, wa0)):
        sems = {"load": load_sems.at[m], "ps": pair_sems.at[m, 0], "pr": pair_sems.at[m, 1],
                "zs": zs_sems.at[m], "zr": zr_sems.at[m]}
        if m < 2:
            sems.update(cs=cross_sems.at[m, 0], cr=cross_sems.at[m, 1])
            bufs = {"z": z_expert.at[m], "cross": cross.at[m]}
            if m == 0:
                def sink(half, e):
                    return done.at[3 + e, :, pl.ds(half * 768, 768)]
            else:
                def sink(half, e):
                    return tall_out.at[1 + e, pl.ds(half * 48, 48), :]
            jobs.append(ExpertReduce(p, m, ref, own.at[m], near.at[m], bufs, sems, sink))
            continue
        for i, name in enumerate(("fs", "fr", "ss", "sr")):
            sems[name] = plane_sems.at[m - 2, i]
        bufs = {"z": z_dense.at[m - 2], "first": first.at[m - 2], "second": second.at[m - 2]}
        if m in WIDE_AT:
            def sink(half, m=m):
                return done.at[WIDE_AT[m], :, pl.ds(half * 768, 768)]
        else:
            def sink(half):
                return tall_out.at[0, pl.ds(half * 48, 48), :]
        jobs.append(DenseReduce(p, m, ref, own.at[m], near.at[m], bufs, sems, sink))

    def spread(i):
        to = (p.me + i) % 32
        remote(small_in.at[to], small_got.at[p.me], small_sems.at[0, i], small_sems.at[1, p.me], to).start()

    pl.loop(1, 32)(spread)
    for k in FAR_FIRST:
        for m in (0, 2, 1, 3, 4, 5):
            jobs[m].start(k)
    experts = [("e", m, k, h) for k in FAR_FIRST for m in (0, 1) for h in range(2)]
    dense = [(m, k, h) for m in (2, 3, 4, 5) for k in FAR_FIRST for h in range(2)]
    pumps = []
    for i in range(len(dense) + 16):
        for stage, lag in ((0, 0), (1, 8), (2, 16)):
            if 0 <= i - lag < len(dense):
                pumps.append((stage,) + dense[i - lag])
    at = {j * len(pumps) // len(experts): e for j, e in enumerate(experts)}
    for i, (stage, m, k, half) in enumerate(pumps):
        if i in at:
            _, em, ek, eh = at[i]
            jobs[em].stage_one(eh, ek)
        job = jobs[m]
        (job.stage_one, job.stage_two, job.stage_three)[stage](half, k)
    for m in range(2):
        for half in range(2):
            jobs[m].crossed(half)
    swap = remote(
        done.at[:, pl.ds(pl.multiple_of((1 - p.core) * 24, 8), 24), :], wide_out.at[p.core],
        meet.at[0], meet.at[1], p.sibling)
    swap.start()
    wide_out[p.core] = done[:, pl.ds(pl.multiple_of(p.core * 24, 8), 24), :]

    def spread_done(i):
        to = (p.me + i) % 32
        remote(small_in.at[to], small_got.at[to], small_sems.at[0, i], small_sems.at[1, to], to).wait()

    pl.loop(1, 32)(spread_done)
    small_got[p.me] = small_in[p.me]
    small_out[...] = jnp.sum(small_got[...], 0)
    for job in jobs:
        job.finish()
    swap.wait()


def run_reduce(small, ein, eout, wa1, wmo, wmi, wa0):
    any_space = pl.BlockSpec(memory_space=pl.ANY)
    vmem = pl.BlockSpec(memory_space=pltpu.VMEM)
    dma = pltpu.SemaphoreType.DMA
    piece = (48, 768)
    return pl.pallas_call(
        reduce_kernel,
        out_shape=[struct((8, 128), F32), struct((2, 7, 24, 1536), F32), struct((5, 96, 768), F32)],
        in_specs=[vmem] + [any_space] * 6,
        out_specs=[vmem] * 3,
        scratch_shapes=[
            pltpu.VMEM((6, 4, 2, 2, 2) + piece, BF16),
            pltpu.VMEM((6, 4, 2, 2, 2) + piece, BF16),
            pltpu.VMEM((4, 4, 2, 2) + piece, BF16),
            pltpu.VMEM((4, 4, 2) + piece, BF16),
            pltpu.VMEM((4, 2, 4, 2) + piece, BF16),
            pltpu.VMEM((2, 2, 4, 2, 2, 2) + piece, BF16),
            pltpu.VMEM((2, 2, 3) + piece, BF16),
            pltpu.VMEM((7, 48, 1536), F32),
            pltpu.VMEM((32, 8, 128), F32),
            dma((6, 4, 2)),
            dma((6, 2, 4, 2)),
            dma((4, 4, 4, 2)),
            dma((6, 2, 4)),
            dma((6, 2, 4, 2)),
            dma((2, 2, 2, 3)),
            dma((2, 32)),
            dma((2,)),
        ],
        compiler_params=pltpu.CompilerParams(
            collective_id=1, has_side_effects=True, vmem_limit_bytes=62 << 20),
        cost_estimate=pl.CostEstimate(flops=0, bytes_accessed=60_000_000, transcendentals=0),
    )(small, ein, eout, wa1, wmo, wmi, wa0)


def fast_reduce(dsmall, de_in, de_out, d0, dmi, dmo, d1):
    small = jnp.pad(dsmall.reshape(8, 32, 24).transpose(1, 0, 2), ((0, 0), (0, 0), (0, 104)))
    w = lambda g: g.reshape(4, 2, 2, 48, HIDDEN)
    t = lambda g: g.reshape(4, 2, 2, 192, WIDTH)
    small, wide, tall = run_reduce(small, w(de_in), t(de_out), w(d1), t(dmo), w(dmi), w(d0))
    wide = wide.transpose(1, 2, 0, 3).reshape(7, 24, HIDDEN)
    return (small[:, :24].T, wide[0], wide[1], tall[0], wide[2],
            wide[3:].transpose(1, 0, 2), tall[1:].transpose(1, 0, 2))


def exchange_kernel(a, b, out_a, out_b, sems, own_sems):
    p = Place()
    greet_all(p, 32)
    copies = []
    for m, (src, dst) in enumerate(((a, out_a), (b, out_b))):
        for i, device in enumerate((p.across_x, p.across_y, p.across_both)):
            copy = remote(src.at[device // 2 % 4], dst.at[p.chip], sems.at[m, 0, i],
                          sems.at[m, 1, i], device)
            copy.start()
            copies.append(copy)
        copy = pltpu.make_async_copy(src.at[p.chip], dst.at[p.chip], own_sems.at[m])
        copy.start()
        copies.append(copy)
    for copy in copies:
        copy.wait()


def run_exchange(a, b, which):
    any_space = pl.BlockSpec(memory_space=pl.ANY)
    shape = (EXPERTS, SLOT, WIDTH)
    out = pl.pallas_call(
        exchange_kernel,
        out_shape=[struct(shape, BF16)] * 2,
        in_specs=[any_space] * 2,
        out_specs=[any_space] * 2,
        scratch_shapes=[pltpu.SemaphoreType.DMA((2, 2, 3)), pltpu.SemaphoreType.DMA((2,))],
        compiler_params=pltpu.CompilerParams(collective_id=2 + which, has_side_effects=True),
    )(a.reshape(shape), b.reshape(shape))
    return [o.reshape(EXPERTS * SLOT, WIDTH) for o in out]


def fast_gather(smalls, wide, mlp_out, expert_in, expert_out):
    width = smalls.shape[0] * 32
    small = jnp.pad(smalls.astype(F32).T, ((0, 0), (0, 128 - smalls.shape[0])))
    packed = jnp.concatenate(wide + [expert_in[:, e] for e in range(EXPERTS)], 1).astype(F32)
    packed = packed.reshape(24, 7, 2, 1536).transpose(2, 0, 1, 3).reshape(2, 24, 7 * 1536)
    tall = jnp.concatenate([mlp_out[None], expert_out.transpose(1, 0, 2)], 0)
    small, wa0, wmi, wmo, wa1, ein, eout = run_gather(small, packed, tall)
    small = small[:, :, : smalls.shape[0]].transpose(1, 0, 2).reshape(8, width)
    flat = [w.reshape(width, HIDDEN) for w in (wa0, wmi, wa1, ein)]
    return small, flat[:2] + [flat[2]], [wmo.reshape(HIDDEN, width)], flat[3], eout.reshape(HIDDEN, width)


def local(
    patches, live_count, expert_ids, attn_gain, attn_qkv, attn_out, mlp_gain, mlp_in, mlp_out,
    moe_gain, router, expert_in, expert_out, cotangent,
):
    images, seq, width = patches.shape
    padded = -(-seq // 16) * 16
    n = lax.axis_size("fsdp")
    group_size = n // EXPERTS
    group = lax.axis_index("fsdp") // group_size
    alive = jnp.arange(images, dtype=jnp.int32) < live_count[0]

    def pad(values, fill=0):
        values = values.reshape(images, seq, -1)
        values = jnp.pad(values, ((0, 0), (0, padded - seq), (0, 0)), constant_values=fill)
        return values.reshape(images * padded, -1)

    x0 = pad(patches)
    g4 = pad(jnp.where(alive[:, None, None], cotangent, jnp.zeros_like(cotangent)))
    ids = pad(expert_ids, -1)
    smalls = jnp.concatenate(
        [attn_gain, mlp_gain[:, None], moe_gain[:, None], router], 1
    )
    wide = [jnp.concatenate([attn_qkv[:, 0], attn_out[:, 0]], 1), mlp_in,
            jnp.concatenate([attn_qkv[:, 1], attn_out[:, 1]], 1)]
    if n == 32:
        small, wides, talls, w_in, w_out = fast_gather(smalls, wide, mlp_out, expert_in, expert_out)
    else:
        small, wides, talls, w_in, w_out = plain_gather(
            smalls, wide, [mlp_out], expert_in, expert_out)
        small = small.astype(F32).T
    small = jnp.concatenate(
        [small[:4], jnp.zeros((4, width), F32), small[4:], jnp.zeros((124, width), F32)], 0
    )
    weights = (wides[0], wides[1], talls[0], wides[2])
    out = run_forward(images, seq, x0, g4, ids, small, *weights)
    saved, rows_x, rows_d = out[:16], out[16], out[17]

    def exchange(first, second, which):
        if n == 32:
            return run_exchange(first, second, which)
        return exchange_one(first), exchange_one(second)

    def exchange_one(rows):
        rows = rows.reshape(EXPERTS, SLOT, width)
        return group_exchange(rows, group_size, group).reshape(EXPERTS * SLOT, width)

    y, dx, dw_in, dw_out = run_expert(*exchange(rows_x, rows_d, 0), w_in, w_out)
    x4, grad, d0, dmi, dmo, d1, dsmall = run_backward(
        images, seq, x0, g4, small, weights, saved, *exchange(y, dx, 1)
    )

    def unpad(values):
        return values.reshape(images, padded, width)[:, :seq]

    block_out = jnp.where(alive[:, None, None], unpad(x4), 0.0).astype(BF16)
    if n == 32:
        dsmall, d0, dmi, dmo, d1, de_in, de_out = fast_reduce(
            dsmall, dw_in, dw_out, d0, dmi, dmo, d1)
    else:
        d0, dmi, dmo, d1 = (plain_reduce(g).astype(F32) for g in (d0, dmi, dmo, d1))
        de_in, de_out = (plain_reduce_expert(g).astype(F32) for g in (dw_in, dw_out))
        dsmall = lax.psum_scatter(dsmall.T, "fsdp", scatter_dimension=0, tiled=True)
    return (
        block_out,
        unpad(grad),
        dsmall[:, 0:2],
        jnp.stack([d0[:, :2304], d1[:, :2304]], 1),
        jnp.stack([d0[:, 2304:], d1[:, 2304:]], 1),
        dsmall[:, 2],
        dmi,
        dmo,
        dsmall[:, 3],
        dsmall[:, 4:8],
        de_in,
        de_out,
    )


def solution(mesh):
    def lead(rank):
        return P("fsdp", *([None] * (rank - 1)))

    return jax.shard_map(
        local,
        mesh=mesh,
        in_specs=tuple(lead(r) for r in (3, 1, 2, 2, 3, 3, 1, 2, 2, 1, 2, 3, 3, 3)),
        out_specs=tuple(lead(r) for r in (3, 3, 2, 3, 3, 1, 2, 2, 1, 2, 3, 3)),
        check_vma=False,
    )
```

time: 1510 us -> 638 us (0.42)
  Pallas kernels: 0 us -> 588 us
  waiting for transfers between devices: 493 us -> 0 us
  local copies, waits for them, and re-layouts: 425 us -> 33.9 us
  other arithmetic: 206 us -> 5.87 us
  matrix products: 169 us -> 0 us
  blocking collectives: 132 us -> 0 us
  starting transfers between devices: 58.3 us -> 0 us
  between operations: 18.2 us -> 2.16 us
    pallas_call x0 -> x10, Pallas kernels: none -> 588 us  [the longest x6 199 us: call(): pl.pallas_call(body, out_shape=outs, in_specs=[pl.BlockSpec(memory_space=...]
    ppermute x39 -> x0, waiting for transfers between devices: 446 us -> none  [the longest x21 398 us: from_partner(): lax.ppermute(array, axis, [(i, i ^ 1 << apart) for i in range(lax.axis_si...]
    dot_general x41 -> x0, matrix products: 169 us -> none  [the longest x9 46.9 us: cross_rows(): jnp.einsum('rd,re->de', left, right, preferred_element_type=jnp.float32)]
    unnamed x303 -> x40, local copies, waits for them, and re-layouts: 149 us -> 8.64 us
    unnamed x1 -> x0, blocking collectives: 92 us -> none
    another operation x7 -> x2, local copies, waits for them, and re-layouts: 64.2 us -> 0.04 us  [the longest x1 0.03 us: local(): jnp.stack([d0[:, :2304], d1[:, :2304]], 1)]
    slice x19 -> x17, local copies, waits for them, and re-layouts: 70.1 us -> 8.36 us  [the longest x2 2.72 us: unpad(): return values.reshape(images, padded, width)[:, :seq]]
    ppermute x39 -> x0, starting transfers between devices: 57.8 us -> none  [the longest x18 40.6 us: from_behind(): return lax.ppermute(value, axis, pairs)]
  transfers between devices with their start and end apart: 45 -> 0, of which waited for: 17 -> 0; matrix products, arithmetic and copies ran while one was open for 46% -> 0% of each run, Pallas kernels for 0% -> 0%
where the time goes in v1:
time: 638 us; the launch traced here: 630 us
  Pallas kernels  588 us (92%)
  local copies, waits for them, and re-layouts  33.9 us (5%)
    pallas_call x6, Pallas kernels, call(): pl.pallas_call(body, out_shape=outs, in_specs=[pl.BlockSpec(memory_space=...  199 us
    pallas_call x1, Pallas kernels, run_gather(): pl.pallas_call(gather_kernel, out_shape=[struct((32, 8, 128), F32), wide_...  159 us
    pallas_call x1, Pallas kernels, run_reduce(): pl.pallas_call(reduce_kernel, out_shape=[struct((8, 128), F32), struct((2...  150 us
    pallas_call x2, Pallas kernels, run_exchange(): pl.pallas_call(exchange_kernel, out_shape=[struct(shape, BF16)] * 2, in_s...  79.6 us

profile of v1, /device:TPU:0, one launch (start us, length us, event | category | flops | bytes accessed | tf_op | source)
XLA Modules:
  0.0 629.9 jit_solution(8197033473663369620)
XLA Ops:
  1.4 0.1 pad.34.clone
  1.5 0.1 pad.32.clone
  1.6 0.7 maximum_bitcast_fusion
  2.3 0.6 pad_convert_fusion.small_in
  2.9 0.8 reshape.133
  3.6 1.1 fusion.13
  4.7 0.1 copy.59
  4.9 0.7 pad.25
  5.6 1.5 fusion.11
  7.1 0.1 copy.118
  7.2 0.9 pad_maximum_fusion.tall_in
  8.1 0.6 broadcast_select_fusion
  8.7 0.1 copy.81
  8.7 0.9 pad.21.clone
  9.6 0.1 copy.82
  9.7 0.9 pad.24.clone
  10.7 0.3 copy-done
  11.0 0.8 fusion.10
  12.1 3.1 reshape.162
  15.2 2.0 copy.117
  17.2 2.1 reshape.159.wide_in
  19.3 158.9 %shard_map.229 = (f32[32,8,128]{2,1,0:T(8,128)}, bf16[4,2,2,48,3072]{4,3,2,1,0:T(8,128)(2,1)}, bf16[4,2,2,48,3072]{4,3,2,1,0:T(8,128)(2,1)}, bf16[4,2,2,192,768]...) custom-call(f32[8,128]{1,0:T(8,128)} %pad_convert_fusion.small_in, ...), custom_call_target="tpu_custom_call" | custom-call | bytes 60000000 | tf_op jit(solution)/shard_map/pallas_call | solution.py:803
  178.2 0.9 slice_bitcast_fusion.5
  179.2 0.1 slice.106
  179.3 0.1 slice.108
  179.4 0.9 maximum_maximum_fusion.small_ref
  180.2 61.1 %shard_map.230 = (f32[416,768]{1,0:T(8,128)}, f32[416,768]{1,0:T(8,128)}, f32[416,768]{1,0:T(8,128)}, bf16[416,768]{1,0:T(8,128)(2,1)}, bf16[416,2304]{1,0:T(8,1...) custom-call(bf16[416,768]{1,0:T(8,128)(2,1)} %bitcast.133, ...), custom_call_target="tpu_custom_call" | custom-call | flops 8000000000 | bytes 42249472 | tf_op jit(solution)/shard_map/pallas_call | solution.py:335
  241.3 38.6 %shard_map.231 = (bf16[4,256,768]{2,1,0:T(8,128)(2,1)}, bf16[4,256,768]{2,1,0:T(8,128)(2,1)}) custom-call(bf16[4,256,768]{2,1,0:T(8,128)(2,1)} %bitcast.121, bf16[4,256,768]{2,1,0:T(8,128)(2,1)} %bitcast.122), custom_call_target="tpu_custom_call" | custom-call | tf_op jit(solution)/shard_map/pallas_call | solution.py:1178
  280.0 42.6 %shard_map.232 = (bf16[1024,768]{1,0:T(8,128)(2,1)}, bf16[1024,768]{1,0:T(8,128)(2,1)}, bf16[768,3072]{1,0:T(8,128)(2,1)}, bf16[3072,768]{1,0:T(8,128)(2,1)}) custom-call(bf16[1024,768]{1,0:T(8,128)(2,1)} %bitcast.156, bf16[1024,768]{1,0:T(8,128)(2,1)} %bitcast.157, bf16[768,3072]{1,0:T(8,128)(2,1)} %bitcast.152, bf16[3072,768]{1,0:T(8,128)(2,1)} %bitcast.153), custom_call_target="tpu_custom_call" | custom-call | flops 30000001024 | bytes 25165824 | tf_op jit(solution)/shard_map/pallas_call | solution.py:335
  322.6 41.0 %shard_map.233 = (bf16[4,256,768]{2,1,0:T(8,128)(2,1)}, bf16[4,256,768]{2,1,0:T(8,128)(2,1)}) custom-call(bf16[4,256,768]{2,1,0:T(8,128)(2,1)} %bitcast.123, bf16[4,256,768]{2,1,0:T(8,128)(2,1)} %bitcast.124), custom_call_target="tpu_custom_call" | custom-call | tf_op jit(solution)/shard_map/pallas_call | solution.py:1178
  363.5 12.0 %shard_map.234 = (f32[416,768]{1,0:T(8,128)}, f32[416,768]{1,0:T(8,128)}, f32[8,768]{1,0:T(8,128)}) custom-call(bf16[416,768]{1,0:T(8,128)(2,1)} %bitcast.136, f32[136,768]{1,0:T(8,128)} %maximum_maximum_fusion.small_ref, f32[416,768]{1,0:T(8,128)} %get-tuple-element.66.x3_ref, bf16[416,768]{1,0:T(8,128)(2,1)} %get-tuple-element.67.en_ref, ...), custom_call_target="tpu_custom_call" | custom-call | flops 3000000000 | bytes 10616832 | tf_op jit(solution)/shard_map/pallas_call | solution.py:335
  375.5 29.4 %shard_map.235 = (f32[416,768]{1,0:T(8,128)}, bf16[768,3072]{1,0:T(8,128)(2,1)}, f32[8,768]{1,0:T(8,128)}) custom-call(f32[416,768]{1,0:T(8,128)} %get-tuple-element.82.g_in_ref, f32[136,768]{1,0:T(8,128)} %maximum_maximum_fusion.small_ref, f32[416,768]{1,0:T(8,128)} %get-tuple-element.83.x_ref, bf16[768,3072]{1,0:T(8,128)(2,1)} %bitcast.151, ...), custom_call_target="tpu_custom_call" | custom-call | flops 5000000000 | bytes 16908288 | tf_op jit(solution)/shard_map/pallas_call | solution.py:335
  404.9 1.3 slice.129
  406.3 1.4 fusion
  407.7 24.7 %shard_map.236 = (f32[416,768]{1,0:T(8,128)}, bf16[768,3072]{1,0:T(8,128)(2,1)}, bf16[3072,768]{1,0:T(8,128)(2,1)}, f32[8,768]{1,0:T(8,128)}) custom-call(f32[416,768]{1,0:T(8,128)} %get-tuple-element.87.g_in_ref, f32[136,768]{1,0:T(8,128)} %maximum_maximum_fusion.small_ref, f32[416,768]{1,0:T(8,128)} %get-tuple-element.88.x1_ref, ...), custom_call_target="tpu_custom_call" | custom-call | flops 8000000000 | bytes 28901376 | tf_op jit(solution)/shard_map/pallas_call | solution.py:335
  432.4 0.0 copy-start.9
  432.4 29.3 %shard_map.237 = (f32[416,768]{1,0:T(8,128)}, bf16[768,3072]{1,0:T(8,128)(2,1)}, f32[8,768]{1,0:T(8,128)}) custom-call(f32[416,768]{1,0:T(8,128)} %get-tuple-element.92.g_in_ref, f32[136,768]{1,0:T(8,128)} %maximum_maximum_fusion.small_ref, bf16[416,768]{1,0:T(8,128)(2,1)} %bitcast.134, bf16[768,3072]{1,0:T(8,128)(2,1)} %bitcast.145, ...), custom_call_target="tpu_custom_call" | custom-call | flops 5000000000 | bytes 16269312 | tf_op jit(solution)/shard_map/pallas_call | solution.py:335
  461.7 0.0 copy-done.7
  461.7 0.8 add_add_fusion
  462.5 1.4 slice.130
  463.8 1.6 copy.80
  465.5 0.1 reshape.151
  465.6 0.1 copy.119
  465.7 0.7 pad.26.small_in
  466.3 150.5 %shard_map.238 = (f32[8,128]{1,0:T(8,128)}, f32[2,7,24,1536]{3,2,1,0:T(8,128)}, f32[5,96,768]{2,1,0:T(8,128)}) custom-call(f32[32,8,128]{2,1,0:T(8,128)} %pad.26.small_in, bf16[4,2,2,48,3072]{4,3,2,1,0:T(8,128)(2,1)} %bitcast.111, bf16[4,2,2,192,768]{4,3,2,1,0:T(8,128)(2,1)} %bitcast.112, bf16[4,2,2,48,3072]{4,3,2,1,0:T(8,128)(2,1)} %bitcast.113, ...), custom_call_target="tpu_custom_call" | custom-call | bytes 60000000 | tf_op jit(solution)/shard_map/pallas_call | solution.py:1118
  616.8 0.7 slice_bitcast_fusion.8
  617.5 0.6 slice.112
  618.1 0.5 slice_bitcast_fusion.9
  618.6 0.6 slice.123
  619.2 1.7 slice_bitcast_fusion.2
  620.9 1.3 slice_bitcast_fusion.1
  622.2 1.8 copy.70
  624.0 0.1 fusion.9
  624.1 0.1 slice_bitcast_fusion
  624.2 0.1 copy.83
  624.3 1.8 copy.69
  626.0 0.2 copy.65
  626.3 0.8 copy.86
  627.0 0.2 copy.64
  627.3 0.1 copy.85
  627.3 0.2 copy.63
  627.6 0.1 copy.84
  627.7 1.0 copy.67
  628.7 0.7 copy.68
  (36 shorter events, 0.4 us)
Async XLA Ops:
  0.6 6.4 %copy-start.4 = (bf16[96,4,768]{2,1,0:T(4,128)(2,1)S(1)}, bf16[96,4,768]{2,1,0:T(4,128)(2,1)}, u32[]{:S(2)}) copy-start(bf16[96,4,768]{2,1,0:T(4,128)(2,1)} %param.26) | copy-start | bytes 1769476
  0.7 6.5 %copy-start.5 = (bf16[96,768]{1,0:T(8,128)(2,1)S(1)}, bf16[96,768]{1,0:T(8,128)(2,1)}, u32[]{:S(2)}) copy-start(bf16[96,768]{1,0:T(8,128)(2,1)} %param.22) | copy-start | bytes 442372
  5.6 2.5 copy-start.2
  8.1 1.5 copy-start.3
  9.6 1.0 copy-start.6
  9.6 1.4 copy-start
  432.4 29.3 %copy-start.7 = (f32[8,768]{1,0:T(8,128)S(1)}, f32[8,768]{1,0:T(8,128)}, u32[]{:S(2)}) copy-start(f32[8,768]{1,0:T(8,128)} %get-tuple-element.97) | copy-start | bytes 73732
  432.4 29.3 %copy-start.8 = (f32[8,768]{1,0:T(8,128)S(1)}, f32[8,768]{1,0:T(8,128)}, u32[]{:S(2)}) copy-start(f32[8,768]{1,0:T(8,128)} %get-tuple-element.98) | copy-start | bytes 73732
  432.4 29.3 %copy-start.9 = (f32[8,768]{1,0:T(8,128)S(1)}, f32[8,768]{1,0:T(8,128)}, u32[]{:S(2)}) copy-start(f32[8,768]{1,0:T(8,128)} %get-tuple-element.99) | copy-start | bytes 73732
  622.2 1.8 copy-start.1

commit v2 on v1

--- a/solution.py
+++ b/solution.py
@@ -911,7 +911,8 @@
         p = self.p
         for half in range(2):
             for z in range(4):
-                self._pair(half, z).wait_send()
+                if self.m > 1:
+                    self._pair(half, z).wait_send()
                 pl.when(p.z != z)(lambda: self._send_z(half, z, True).wait_send())
 
 
@@ -990,6 +991,19 @@
 
 
 class ExpertReduce(Reduce):
+    def _load(self, half, z):
+        return pltpu.make_async_copy(
+            self.ref.at[z, half], self.own.at[z, half], self.sems["load"].at[z, half])
+
+    def start(self, k):
+        z = self.p.z + k
+
+        def run():
+            for half in range(2):
+                self._load(half, z).start()
+
+        pl.when(self.valid(k))(run)
+
     def _block(self, half, z):
         return self.own.at[z, half]
 
@@ -999,7 +1013,7 @@
 
     def stage_one(self, half, k):
         def run():
-            self.pair_sum(half, k)
+            self._load(half, self.p.z + k).wait()
             self.along_z(half, k)
 
         pl.when(self.valid(k))(run)
@@ -1034,7 +1048,7 @@
 
 
 def reduce_kernel(
-    small_in, ein, eout, wa1, wmo, wmi, wa0,
+    small_in, sums, wa1, wmo, wmi, wa0,
     small_out, wide_out, tall_out,
     own, near, first, second, z_dense, z_expert, cross, done, small_got,
     load_sems, pair_sems, plane_sems, zs_sems, zr_sems, cross_sems, small_sems, meet,
@@ -1042,7 +1056,7 @@
     p = Place()
     greet_all(p, 32)
     jobs = []
-    for m, ref in enumerate((ein, eout, wa1, wmo, wmi, wa0)):
+    for m, ref in enumerate((sums.at[0], sums.at[1], wa1, wmo, wmi, wa0)):
         sems = {"load": load_sems.at[m], "ps": pair_sems.at[m, 0], "pr": pair_sems.at[m, 1],
                 "zs": zs_sems.at[m], "zr": zr_sems.at[m]}
         if m < 2:
@@ -1054,7 +1068,7 @@
             else:
                 def sink(half, e):
                     return tall_out.at[1 + e, pl.ds(half * 48, 48), :]
-            jobs.append(ExpertReduce(p, m, ref, own.at[m], near.at[m], bufs, sems, sink))
+            jobs.append(ExpertReduce(p, m, ref, own.at[m], None, bufs, sems, sink))
             continue
         for i, name in enumerate(("fs", "fr", "ss", "sr")):
             sems[name] = plane_sems.at[m - 2, i]
@@ -1065,7 +1079,7 @@
         else:
             def sink(half):
                 return tall_out.at[0, pl.ds(half * 48, 48), :]
-        jobs.append(DenseReduce(p, m, ref, own.at[m], near.at[m], bufs, sems, sink))
+        jobs.append(DenseReduce(p, m, ref, own.at[m], near.at[m - 2], bufs, sems, sink))
 
     def spread(i):
         to = (p.me + i) % 32
@@ -1110,7 +1124,7 @@
     swap.wait()
 
 
-def run_reduce(small, ein, eout, wa1, wmo, wmi, wa0):
+def run_reduce(small, sums, wa1, wmo, wmi, wa0):
     any_space = pl.BlockSpec(memory_space=pl.ANY)
     vmem = pl.BlockSpec(memory_space=pltpu.VMEM)
     dma = pltpu.SemaphoreType.DMA
@@ -1118,11 +1132,11 @@
     return pl.pallas_call(
         reduce_kernel,
         out_shape=[struct((8, 128), F32), struct((2, 7, 24, 1536), F32), struct((5, 96, 768), F32)],
-        in_specs=[vmem] + [any_space] * 6,
+        in_specs=[vmem] + [any_space] * 5,
         out_specs=[vmem] * 3,
         scratch_shapes=[
             pltpu.VMEM((6, 4, 2, 2, 2) + piece, BF16),
-            pltpu.VMEM((6, 4, 2, 2, 2) + piece, BF16),
+            pltpu.VMEM((4, 4, 2, 2, 2) + piece, BF16),
             pltpu.VMEM((4, 4, 2, 2) + piece, BF16),
             pltpu.VMEM((4, 4, 2) + piece, BF16),
             pltpu.VMEM((4, 2, 4, 2) + piece, BF16),
@@ -1142,48 +1156,169 @@
         compiler_params=pltpu.CompilerParams(
             collective_id=1, has_side_effects=True, vmem_limit_bytes=62 << 20),
         cost_estimate=pl.CostEstimate(flops=0, bytes_accessed=60_000_000, transcendentals=0),
-    )(small, ein, eout, wa1, wmo, wmi, wa0)
-
-
-def fast_reduce(dsmall, de_in, de_out, d0, dmi, dmo, d1):
+    )(small, sums, wa1, wmo, wmi, wa0)
+
+
+def fast_reduce(dsmall, sums, d0, dmi, dmo, d1):
     small = jnp.pad(dsmall.reshape(8, 32, 24).transpose(1, 0, 2), ((0, 0), (0, 0), (0, 104)))
     w = lambda g: g.reshape(4, 2, 2, 48, HIDDEN)
     t = lambda g: g.reshape(4, 2, 2, 192, WIDTH)
-    small, wide, tall = run_reduce(small, w(de_in), t(de_out), w(d1), t(dmo), w(dmi), w(d0))
+    small, wide, tall = run_reduce(small, sums, w(d1), t(dmo), w(dmi), w(d0))
     wide = wide.transpose(1, 2, 0, 3).reshape(7, 24, HIDDEN)
     return (small[:, :24].T, wide[0], wide[1], tall[0], wide[2],
             wide[3:].transpose(1, 0, 2), tall[1:].transpose(1, 0, 2))
 
 
-def exchange_kernel(a, b, out_a, out_b, sems, own_sems):
+def expert_step(
+    rows_x, rows_d, ein, eout,
+    y_back, d_back, sums,
+    wi, wo, got_x, got_d, active, slope, y_out, d_out, acc, dwi, dwo, near,
+    load_sems, own_sems, move_sems, pair_sems, sum_sems,
+):
     p = Place()
     greet_all(p, 32)
-    copies = []
-    for m, (src, dst) in enumerate(((a, out_a), (b, out_b))):
-        for i, device in enumerate((p.across_x, p.across_y, p.across_both)):
-            copy = remote(src.at[device // 2 % 4], dst.at[p.chip], sems.at[m, 0, i],
-                          sems.at[m, 1, i], device)
-            copy.start()
-            copies.append(copy)
-        copy = pltpu.make_async_copy(src.at[p.chip], dst.at[p.chip], own_sems.at[m])
+    chips = [device // 2 % 4 for device in (p.me, p.across_x, p.across_y, p.across_both)]
+    devices = (None, p.across_x, p.across_y, p.across_both)
+    loads = [pltpu.make_async_copy(src, dst, load_sems.at[i])
+             for i, (src, dst) in enumerate(((ein, wi), (eout, wo)))]
+
+    def inward(t, i):
+        src, dst = ((rows_x, got_x), (rows_d, got_d))[t]
+        if i == 0:
+            return pltpu.make_async_copy(src.at[p.chip], dst.at[p.chip], own_sems.at[t])
+        return remote(src.at[chips[i]], dst.at[p.chip], move_sems.at[t, 0, i], move_sems.at[t, 1, i],
+                      devices[i])
+
+    def outward(t, i):
+        src, dst = ((y_out, y_back), (d_out, d_back))[t]
+        if i == 0:
+            return pltpu.make_async_copy(src.at[p.chip], dst.at[p.chip], own_sems.at[2 + t])
+        return remote(src.at[chips[i]], dst.at[p.chip], move_sems.at[2 + t, 0, i],
+                      move_sems.at[2 + t, 1, i], devices[i])
+
+    for i in range(4):
+        inward(0, i).start()
+    for copy in loads:
         copy.start()
-        copies.append(copy)
-    for copy in copies:
+    inward(1, 0).start()
+    for copy in loads:
         copy.wait()
-
-
-def run_exchange(a, b, which):
+    wide = wi.reshape(WIDTH, HIDDEN)
+    tall = wo.reshape(HIDDEN, WIDTH)
+    for i in range(4):
+        chip = chips[i]
+        if i == 0:
+            inward(0, 0).wait()
+        else:
+            inward(0, i).wait_recv()
+        if i == 1:
+            for j in range(1, 4):
+                inward(1, j).start()
+        acc[...] = jnp.zeros_like(acc)
+
+        def forward(n):
+            cols = tile(n, 512)
+            ea, sl = gelu_both(nn(got_x[chip], wide[:, cols]))
+            ea = ea.astype(BF16)
+            active[chip, :, cols] = ea
+            slope[chip, :, cols] = sl.astype(BF16)
+            acc[...] += nn(ea, tall[cols, :])
+
+        loop(6, forward)
+        y_out[chip] = acc[...].astype(BF16)
+        outward(0, i).start()
+    for i in range(4):
+        chip = chips[i]
+        if i == 0:
+            inward(1, 0).wait()
+        else:
+            inward(1, i).wait_recv()
+        acc[...] = jnp.zeros_like(acc)
+
+        def backward(n):
+            cols = tile(n, 512)
+            dh = slope[chip, :, cols].astype(F32) * nt(got_d[chip], tall[cols, :])
+            dh = dh.astype(BF16)
+            slope[chip, :, cols] = dh
+            acc[...] += nt(dh, wide[:, cols])
+
+        loop(6, backward)
+        d_out[chip] = acc[...].astype(BF16)
+        outward(1, i).start()
+    every = EXPERTS * SLOT
+    x_all, d_all = got_x.reshape(every, WIDTH), got_d.reshape(every, WIDTH)
+    ea_all, dh_all = active.reshape(every, HIDDEN), slope.reshape(every, HIDDEN)
+    dwi_all, dwo_all = dwi.reshape(WIDTH, HIDDEN), dwo.reshape(HIDDEN, WIDTH)
+
+    def weights(n):
+        cols = tile(n, 512)
+        dwo_all[cols, :] = tn(ea_all[:, cols], d_all[...]).astype(BF16)
+        dwi_all[:, cols] = tn(x_all[...], dh_all[:, cols]).astype(BF16)
+
+    loop(6, weights)
+    pairs = [(m, z, half) for z in range(4) for m in range(2) for half in range(2)]
+
+    def pair(m, z, half):
+        src = plane_part((dwi, dwo)[m], KINDS[m], z, 1 - p.core, half)
+        return remote(src, near.at[m, z, half], pair_sems.at[m, z, half, 0],
+                      pair_sems.at[m, z, half, 1], p.sibling)
+
+    def result(m, z, half):
+        return pltpu.make_async_copy(near.at[m, z, half], sums.at[m, z, half], sum_sems.at[m, z, half])
+
+    for one in pairs:
+        pair(*one).start()
+    for m, z, half in pairs:
+        pair(m, z, half).wait_recv()
+        own = plane_part((dwi, dwo)[m], KINDS[m], z, p.core, half)
+        came = near.at[m, z, half]
+        add_into(lambda i: came.at[i // 2, i % 2], lambda i: own.at[i // 2, i % 2], 4)
+        result(m, z, half).start()
+    for one in pairs:
+        result(*one).wait()
+        pair(*one).wait_send()
+    for t in range(2):
+        outward(t, 0).wait()
+        for i in range(1, 4):
+            inward(t, i).wait_send()
+            outward(t, i).wait()
+
+
+def run_expert_step(rows_x, rows_d, ein, eout):
     any_space = pl.BlockSpec(memory_space=pl.ANY)
-    shape = (EXPERTS, SLOT, WIDTH)
-    out = pl.pallas_call(
-        exchange_kernel,
-        out_shape=[struct(shape, BF16)] * 2,
-        in_specs=[any_space] * 2,
-        out_specs=[any_space] * 2,
-        scratch_shapes=[pltpu.SemaphoreType.DMA((2, 2, 3)), pltpu.SemaphoreType.DMA((2,))],
-        compiler_params=pltpu.CompilerParams(collective_id=2 + which, has_side_effects=True),
-    )(a.reshape(shape), b.reshape(shape))
-    return [o.reshape(EXPERTS * SLOT, WIDTH) for o in out]
+    dma = pltpu.SemaphoreType.DMA
+    rows = (EXPERTS, SLOT, WIDTH)
+    y, d, sums = pl.pallas_call(
+        expert_step,
+        out_shape=[struct(rows, BF16)] * 2 + [struct((2, 4, 2, 2, 2, 48, 768), BF16)],
+        in_specs=[any_space] * 4,
+        out_specs=[any_space] * 3,
+        scratch_shapes=[
+            pltpu.VMEM((4, 2, 2, 48, HIDDEN), BF16),
+            pltpu.VMEM((4, 2, 2, 192, WIDTH), BF16),
+            pltpu.VMEM(rows, BF16),
+            pltpu.VMEM(rows, BF16),
+            pltpu.VMEM((EXPERTS, SLOT, HIDDEN), BF16),
+            pltpu.VMEM((EXPERTS, SLOT, HIDDEN), BF16),
+            pltpu.VMEM(rows, BF16),
+            pltpu.VMEM(rows, BF16),
+            pltpu.VMEM((SLOT, WIDTH), F32),
+            pltpu.VMEM((4, 2, 2, 48, HIDDEN), BF16),
+            pltpu.VMEM((4, 2, 2, 192, WIDTH), BF16),
+            pltpu.VMEM((2, 4, 2, 2, 2, 48, 768), BF16),
+            dma((2,)),
+            dma((4,)),
+            dma((4, 2, 4)),
+            dma((2, 4, 2, 2)),
+            dma((2, 4, 2)),
+        ],
+        compiler_params=pltpu.CompilerParams(
+            collective_id=2, has_side_effects=True, vmem_limit_bytes=VMEM_BYTES),
+        cost_estimate=pl.CostEstimate(
+            flops=30_000_000_000, bytes_accessed=40_000_000, transcendentals=0),
+    )(rows_x.reshape(rows), rows_d.reshape(rows), ein, eout)
+    flat = (EXPERTS * SLOT, WIDTH)
+    return y.reshape(flat), d.reshape(flat), sums
 
 
 def fast_gather(smalls, wide, mlp_out, expert_in, expert_out):
@@ -1194,8 +1329,8 @@
     tall = jnp.concatenate([mlp_out[None], expert_out.transpose(1, 0, 2)], 0)
     small, wa0, wmi, wmo, wa1, ein, eout = run_gather(small, packed, tall)
     small = small[:, :, : smalls.shape[0]].transpose(1, 0, 2).reshape(8, width)
-    flat = [w.reshape(width, HIDDEN) for w in (wa0, wmi, wa1, ein)]
-    return small, flat[:2] + [flat[2]], [wmo.reshape(HIDDEN, width)], flat[3], eout.reshape(HIDDEN, width)
+    flat = [w.reshape(width, HIDDEN) for w in (wa0, wmi, wa1)]
+    return small, flat[:2] + [flat[2]], [wmo.reshape(HIDDEN, width)], ein, eout
 
 
 def local(
@@ -1235,18 +1370,17 @@
     out = run_forward(images, seq, x0, g4, ids, small, *weights)
     saved, rows_x, rows_d = out[:16], out[16], out[17]
 
-    def exchange(first, second, which):
-        if n == 32:
-            return run_exchange(first, second, which)
-        return exchange_one(first), exchange_one(second)
-
-    def exchange_one(rows):
+    def exchange(rows):
         rows = rows.reshape(EXPERTS, SLOT, width)
         return group_exchange(rows, group_size, group).reshape(EXPERTS * SLOT, width)
 
-    y, dx, dw_in, dw_out = run_expert(*exchange(rows_x, rows_d, 0), w_in, w_out)
+    if n == 32:
+        y_back, d_back, sums = run_expert_step(rows_x, rows_d, w_in, w_out)
+    else:
+        y, dx, dw_in, dw_out = run_expert(exchange(rows_x), exchange(rows_d), w_in, w_out)
+        y_back, d_back = exchange(y), exchange(dx)
     x4, grad, d0, dmi, dmo, d1, dsmall = run_backward(
-        images, seq, x0, g4, small, weights, saved, *exchange(y, dx, 1)
+        images, seq, x0, g4, small, weights, saved, y_back, d_back
     )
 
     def unpad(values):
@@ -1255,7 +1389,7 @@
     block_out = jnp.where(alive[:, None, None], unpad(x4), 0.0).astype(BF16)
     if n == 32:
         dsmall, d0, dmi, dmo, d1, de_in, de_out = fast_reduce(
-            dsmall, dw_in, dw_out, d0, dmi, dmo, d1)
+            dsmall, sums, d0, dmi, dmo, d1)
     else:
         d0, dmi, dmo, d1 = (plain_reduce(g).astype(F32) for g in (d0, dmi, dmo, d1))
         de_in, de_out = (plain_reduce_expert(g).astype(F32) for g in (dw_in, dw_out))

time: 638 us -> 586 us (0.918)
  Pallas kernels: 588 us -> 535 us
    pallas_call x6 -> x5, Pallas kernels: 199 us -> 157 us  [call(): pl.pallas_call(body, out_shape=outs, in_specs=[pl.BlockSpec(memory_space=...]
    pallas_call x2 -> x1, Pallas kernels: 79.6 us -> 73 us  [run_expert_step(): pl.pallas_call(expert_step, out_shape=[struct(rows, BF16)] * 2 + [struct(...]
where the time goes in v2:
time: 586 us; the launch traced here: 577 us
  Pallas kernels  535 us (91%)
  local copies, waits for them, and re-layouts  33.9 us (6%)
  other arithmetic  5.87 us (1%)
    pallas_call x1, Pallas kernels, run_gather(): pl.pallas_call(gather_kernel, out_shape=[struct((32, 8, 128), F32), wide_...  159 us
    pallas_call x5, Pallas kernels, call(): pl.pallas_call(body, out_shape=outs, in_specs=[pl.BlockSpec(memory_space=...  157 us
    pallas_call x1, Pallas kernels, run_reduce(): pl.pallas_call(reduce_kernel, out_shape=[struct((8, 128), F32), struct((2...  146 us
    pallas_call x1, Pallas kernels, run_expert_step(): pl.pallas_call(expert_step, out_shape=[struct(rows, BF16)] * 2 + [struct(...  73 us

profile of v2, /device:TPU:0, one launch (start us, length us, event | category | flops | bytes accessed | tf_op | source)
XLA Modules:
  0.0 576.9 jit_solution(5551571020791537348)
XLA Ops:
  0.6 0.0 copy-start.4
  1.4 0.1 pad.34.clone
  1.5 0.1 pad.32.clone
  1.6 0.7 maximum_bitcast_fusion
  2.3 0.6 pad_convert_fusion.small_in
  2.9 0.8 reshape.109
  3.6 1.1 fusion.13
  4.7 0.1 copy.59
  4.9 0.7 pad.25
  5.6 1.5 fusion.11
  7.1 0.1 copy.118
  7.2 0.0 copy-done.5
  7.2 0.9 pad_maximum_fusion.tall_in
  8.1 0.6 broadcast_select_fusion
  8.7 0.1 copy.81
  8.7 0.9 pad.21.clone
  9.6 0.1 copy.82
  9.7 0.9 pad.24.clone
  10.6 0.0 copy-done.6
  10.7 0.3 copy-done
  11.0 0.8 fusion.10
  12.1 3.1 reshape.130
  15.2 2.0 copy.117
  17.2 2.1 reshape.127.wide_in
  19.3 159.3 %shard_map.229 = (f32[32,8,128]{2,1,0:T(8,128)}, bf16[4,2,2,48,3072]{4,3,2,1,0:T(8,128)(2,1)}, bf16[4,2,2,48,3072]{4,3,2,1,0:T(8,128)(2,1)}, bf16[4,2,2,192,768]...) custom-call(f32[8,128]{1,0:T(8,128)} %pad_convert_fusion.small_in, ...), custom_call_target="tpu_custom_call" | custom-call | bytes 60000000 | tf_op jit(solution)/shard_map/pallas_call | solution.py:803
  178.6 0.9 slice_bitcast_fusion.5
  179.6 0.1 slice.106
  179.7 0.1 slice.108
  179.8 0.9 maximum_maximum_fusion.small_ref
  180.7 61.1 %shard_map.230 = (f32[416,768]{1,0:T(8,128)}, f32[416,768]{1,0:T(8,128)}, f32[416,768]{1,0:T(8,128)}, bf16[416,768]{1,0:T(8,128)(2,1)}, bf16[416,2304]{1,0:T(8,1...) custom-call(bf16[416,768]{1,0:T(8,128)(2,1)} %bitcast.119, ...), custom_call_target="tpu_custom_call" | custom-call | flops 8000000000 | bytes 42249472 | tf_op jit(solution)/shard_map/pallas_call | solution.py:335
  241.8 73.0 %shard_map.231 = (bf16[4,256,768]{2,1,0:T(8,128)(2,1)}, bf16[4,256,768]{2,1,0:T(8,128)(2,1)}, bf16[2,4,2,2,2,48,768]{6,5,4,3,2,1,0:T(8,128)(2,1)}) custom-call(bf16[4,256,768]{2,1,0:T(8,128)(2,1)} %bitcast.138, bf16[4,256,768]{2,1,0:T(8,128)(2,1)} %bitcast.139, bf16[4,2,2,48,3072]{4,3,2,1,0:T(8,128)(2,1)} %get-tuple-element.68.ein, ...), custom_call_target="tpu_custom_call" | custom-call | flops 30000001024 | bytes 40000000 | tf_op jit(solution)/shard_map/pallas_call | solution.py:1291
  314.8 12.1 %shard_map.232 = (f32[416,768]{1,0:T(8,128)}, f32[416,768]{1,0:T(8,128)}, f32[8,768]{1,0:T(8,128)}) custom-call(bf16[416,768]{1,0:T(8,128)(2,1)} %bitcast.122, f32[136,768]{1,0:T(8,128)} %maximum_maximum_fusion.small_ref, f32[416,768]{1,0:T(8,128)} %get-tuple-element.61.x3_ref, bf16[416,768]{1,0:T(8,128)(2,1)} %get-tuple-element.62.en_ref, ...), custom_call_target="tpu_custom_call" | custom-call | flops 3000000000 | bytes 10616832 | tf_op jit(solution)/shard_map/pallas_call | solution.py:335
  326.9 29.4 %shard_map.233 = (f32[416,768]{1,0:T(8,128)}, bf16[768,3072]{1,0:T(8,128)(2,1)}, f32[8,768]{1,0:T(8,128)}) custom-call(f32[416,768]{1,0:T(8,128)} %get-tuple-element.73.g_in_ref, f32[136,768]{1,0:T(8,128)} %maximum_maximum_fusion.small_ref, f32[416,768]{1,0:T(8,128)} %get-tuple-element.74.x_ref, bf16[768,3072]{1,0:T(8,128)(2,1)} %bitcast.137, ...), custom_call_target="tpu_custom_call" | custom-call | flops 5000000000 | bytes 16908288 | tf_op jit(solution)/shard_map/pallas_call | solution.py:335
  356.3 1.3 slice.129
  357.7 1.4 fusion
  359.1 24.7 %shard_map.234 = (f32[416,768]{1,0:T(8,128)}, bf16[768,3072]{1,0:T(8,128)(2,1)}, bf16[3072,768]{1,0:T(8,128)(2,1)}, f32[8,768]{1,0:T(8,128)}) custom-call(f32[416,768]{1,0:T(8,128)} %get-tuple-element.78.g_in_ref, f32[136,768]{1,0:T(8,128)} %maximum_maximum_fusion.small_ref, f32[416,768]{1,0:T(8,128)} %get-tuple-element.79.x1_ref, ...), custom_call_target="tpu_custom_call" | custom-call | flops 8000000000 | bytes 28901376 | tf_op jit(solution)/shard_map/pallas_call | solution.py:335
  383.8 29.3 %shard_map.235 = (f32[416,768]{1,0:T(8,128)}, bf16[768,3072]{1,0:T(8,128)(2,1)}, f32[8,768]{1,0:T(8,128)}) custom-call(f32[416,768]{1,0:T(8,128)} %get-tuple-element.83.g_in_ref, f32[136,768]{1,0:T(8,128)} %maximum_maximum_fusion.small_ref, bf16[416,768]{1,0:T(8,128)(2,1)} %bitcast.120, bf16[768,3072]{1,0:T(8,128)(2,1)} %bitcast.131, ...), custom_call_target="tpu_custom_call" | custom-call | flops 5000000000 | bytes 16269312 | tf_op jit(solution)/shard_map/pallas_call | solution.py:335
  413.1 0.0 copy-done.7
  413.1 0.8 add_add_fusion
  413.9 1.4 slice.130
  415.3 1.6 copy.80
  416.9 0.1 reshape.121
  417.0 0.1 copy.119
  417.1 0.7 pad.26.small_in
  417.8 146.0 %shard_map.236 = (f32[8,128]{1,0:T(8,128)}, f32[2,7,24,1536]{3,2,1,0:T(8,128)}, f32[5,96,768]{2,1,0:T(8,128)}) custom-call(f32[32,8,128]{2,1,0:T(8,128)} %pad.26.small_in, bf16[2,4,2,2,2,48,768]{6,5,4,3,2,1,0:T(8,128)(2,1)} %get-tuple-element.92.sums, bf16[4,2,2,48,3072]{4,3,2,1,0:T(8,128)(2,1)} %bitcast.104, bf16[4,2,2,192,768]{4,3,2,1,0:T(8,128)(2,1)} %bitcast.106, ...), custom_call_target="tpu_custom_call" | custom-call | bytes 60000000 | tf_op jit(solution)/shard_map/pallas_call | solution.py:1132
  563.8 0.7 slice_bitcast_fusion.8
  564.4 0.6 slice.112
  565.0 0.5 slice_bitcast_fusion.9
  565.5 0.6 slice.123
  566.1 1.7 slice_bitcast_fusion.2
  567.8 1.3 slice_bitcast_fusion.1
  569.2 1.8 copy.70
  570.9 0.1 fusion.9
  571.0 0.1 slice_bitcast_fusion
  571.1 0.1 copy.83
  571.2 1.8 copy.69
  573.0 0.2 copy.65
  573.2 0.8 copy.86
  574.0 0.2 copy.64
  574.2 0.1 copy.85
  574.3 0.2 copy.63
  574.5 0.1 copy.84
  574.7 1.0 copy.67
  575.7 0.7 copy.68
  (34 shorter events, 0.4 us)
Async XLA Ops:
  0.6 6.4 %copy-start.4 = (bf16[96,4,768]{2,1,0:T(4,128)(2,1)S(1)}, bf16[96,4,768]{2,1,0:T(4,128)(2,1)}, u32[]{:S(2)}) copy-start(bf16[96,4,768]{2,1,0:T(4,128)(2,1)} %param.26) | copy-start | bytes 1769476
  0.7 6.5 %copy-start.5 = (bf16[96,768]{1,0:T(8,128)(2,1)S(1)}, bf16[96,768]{1,0:T(8,128)(2,1)}, u32[]{:S(2)}) copy-start(bf16[96,768]{1,0:T(8,128)(2,1)} %param.22) | copy-start | bytes 442372
  5.6 2.5 copy-start.2
  8.1 1.5 copy-start.3
  9.6 1.0 copy-start.6
  9.6 1.4 copy-start
  383.8 29.3 %copy-start.7 = (f32[8,768]{1,0:T(8,128)S(1)}, f32[8,768]{1,0:T(8,128)}, u32[]{:S(2)}) copy-start(f32[8,768]{1,0:T(8,128)} %get-tuple-element.88) | copy-start | bytes 73732
  383.8 29.3 %copy-start.8 = (f32[8,768]{1,0:T(8,128)S(1)}, f32[8,768]{1,0:T(8,128)}, u32[]{:S(2)}) copy-start(f32[8,768]{1,0:T(8,128)} %get-tuple-element.89) | copy-start | bytes 73732
  383.8 29.3 %copy-start.9 = (f32[8,768]{1,0:T(8,128)S(1)}, f32[8,768]{1,0:T(8,128)}, u32[]{:S(2)}) copy-start(f32[8,768]{1,0:T(8,128)} %get-tuple-element.90) | copy-start | bytes 73732
  569.2 1.8 copy-start.1

commit v3 on v2

--- a/solution.py
+++ b/solution.py
@@ -131,16 +131,24 @@
 
 def attention_backward(
     g_ref, x_ref, gain, w_ref, an_ref, qkv_ref, o_ref, dw_ref, dgain_ref, row, images, seq,
-    low_ref, do_ref, dqkv_ref, dn_ref,
+    low_ref, do_ref, dqkv_ref, dn_ref, weights_here=lambda: None, ready=lambda: None,
+    pump=lambda: None,
 ):
     rows_of = qkv_ref.shape[0] // images
     low_ref[...] = g_ref[...].astype(BF16)
 
     def outward(n):
         dw_ref[:, tile(n + 9, 256)] = tn(o_ref[...], low_ref[:, tile(n, 256)]).astype(BF16)
+
+    loop(3, outward)
+    pump()
+    weights_here()
+
+    def outward_rows(n):
         do_ref[:, tile(n, 256)] = nt(low_ref[...], w_ref[tile(n, 256), 2304:]).astype(BF16)
 
-    loop(3, outward)
+    loop(3, outward_rows)
+    pump()
     for image in range(images):
         rows = pl.ds(image * rows_of, rows_of)
 
@@ -165,18 +173,28 @@
             dqkv_ref[rows, tile(p + 6, 128)] = (dk * scale).astype(BF16)
             dqkv_ref[rows, tile(p + 12, 128)] = dv.astype(BF16)
 
-        loop(6, pair)
-
-    def inward(n):
-        dw_ref[:, tile(n, 256)] = tn(an_ref[...], dqkv_ref[:, tile(n, 256)]).astype(BF16)
-
-    loop(9, inward)
+        loop(3, pair)
+        pump()
+        loop(3, lambda p, pair=pair: pair(p + 3))
+        pump()
+
+    for third in range(3):
+
+        def inward(n, third=third):
+            cols = tile(n + third * 3, 256)
+            dw_ref[:, cols] = tn(an_ref[...], dqkv_ref[:, cols]).astype(BF16)
+
+        loop(3, inward)
+        pump()
+    ready()
 
     def normed(n):
         dn_ref[:, tile(n, 256)] = nt(dqkv_ref[...], w_ref[tile(n, 256), :2304])
 
     loop(3, normed)
+    pump()
     norm_back(x_ref, gain, dn_ref, g_ref, dgain_ref, row)
+    pump()
 
 
 def forward_kernel(
@@ -824,7 +842,9 @@
 
 KINDS = ("wide", "tall", "wide", "tall", "wide", "wide")
 WIDE_AT = {2: 2, 4: 1, 5: 0}
-FAR_FIRST = (-3, 3, -2, 2, -1, 1, 0)
+LAG = 3
+AHEAD = 4
+PACE = ((0.65, 0), (0.65, 1.2), (0.65, 1.3), (2, 1))
 
 
 def plane_part(ref, kind, z, core, half):
@@ -835,338 +855,496 @@
 
 def add_into(kept, came, pieces):
     def body(i):
-        rows = pl.ds(pl.multiple_of(i % 3 * 16, 16), 16)
-        a, b = kept(i // 3), came(i // 3)
-        a[rows, :] = (a[rows, :].astype(F32) + b[rows, :].astype(F32)).astype(BF16)
-
-    loop(pieces * 3, body)
+        a, b = kept(i), came(i)
+        a[...] = a[...] + b[...]
+
+    if pieces == 1:
+        body(0)
+    else:
+        loop(pieces, body)
 
 
 class Reduce:
-    def __init__(self, place, m, ref, own, near, bufs, sems, sink):
+    def __init__(self, place, m, ref, bufs, sems, sink):
         self.p, self.m, self.kind, self.ref = place, m, KINDS[m], ref
-        self.own, self.near, self.bufs, self.sems, self.sink = own, near, bufs, sems, sink
-
-    def _load(self, half, z):
-        src = plane_part(self.ref, self.kind, z, self.p.core, half)
-        return pltpu.make_async_copy(src, self.own.at[z, half], self.sems["load"].at[z, half])
-
-    def _pair(self, half, z):
+        self.bufs, self.sems, self.sink = bufs, sems, sink
+
+    def goal(self, stop):
+        z = self.p.z
+        if stop == 3:
+            return z
+        table = ((3, 3, 0, 0), (2, 0, 3, 1), (1, 2, 1, 2))[stop]
+        low = jnp.where(z == 0, table[0], table[1])
+        return jnp.where(z < 2, low, jnp.where(z == 2, table[2], table[3]))
+
+    def joins(self, stop):
+        z = self.p.z
+        return (z > 0) & (z < 3) if stop < 3 else z >= 0
+
+    def _send_z(self, half, stop, src):
         p, s = self.p, self.sems
-        src = plane_part(self.ref, self.kind, z, 1 - p.core, half)
-        return remote(src, self.near.at[z, half], s["ps"].at[z, half], s["pr"].at[z, half], p.sibling)
-
-    def start(self, k):
-        z = self.p.z + k
-
-        def run():
-            for half in range(2):
-                self._load(half, z).start()
-                self._pair(half, z).start()
-
-        pl.when(self.valid(k))(run)
-
-    def valid(self, k):
-        z = self.p.z + k
-        return (z >= 0) & (z <= 3)
-
-    def pair_sum(self, half, k):
-        z = self.p.z + k
-        self._load(half, z).wait()
-        self._pair(half, z).wait_recv()
-        own, near = self.own.at[z, half], self.near.at[z, half]
+        z = self.goal(stop)
+        up = z > p.z
+        slot = jnp.where(up | (z != p.z - 1), z, 4)
+        return remote(src, self.bufs["z"].at[half, slot], s["zs"].at[half, stop],
+                      s["zr"].at[half, slot], jnp.where(up, p.me + 8, p.me - 8))
+
+    def _came(self, half, src, slot):
+        p, s = self.p, self.sems
+        came = self.bufs["z"].at[half, slot]
+        remote(src, came, s["zs"].at[half, 0], s["zr"].at[half, slot], p.sibling).wait_recv()
+        return came
+
+
+class DenseReduce(Reduce):
+    def _plane(self, half, stop):
+        return plane_part(self.ref, self.kind, self.goal(stop), self.p.core, half)
+
+    def _block(self, half, stop):
+        return self._plane(half, stop).at[self.p.y, self.p.x]
+
+    def _pair(self, half, stop):
+        p, s = self.p, self.sems
+        src = plane_part(self.ref, self.kind, self.goal(stop), 1 - p.core, half)
+        return remote(src, self.bufs["near"].at[stop, half], s["ps"].at[stop, half],
+                      s["pr"].at[stop, half], p.sibling)
+
+    def start(self):
+        for unit in range(3):
+            self._pair(unit % 2, unit // 2).start()
+
+    def _first(self, half, stop):
+        p, s = self.p, self.sems
+        plane = self._plane(half, stop)
+        src = plane.at[:, 1 - p.x] if half else plane.at[1 - p.y]
+        return remote(src, self.bufs["first"].at[stop, half], s["fs"].at[stop, half],
+                      s["fr"].at[stop, half], p.across_x if half else p.across_y)
+
+    def _second(self, half, stop):
+        p, s = self.p, self.sems
+        plane = self._plane(half, stop)
+        src = plane.at[1 - p.y, p.x] if half else plane.at[p.y, 1 - p.x]
+        return remote(src, self.bufs["second"].at[stop, half], s["ss"].at[stop, half],
+                      s["sr"].at[stop, half], p.across_y if half else p.across_x)
+
+    def stage_one(self, half, stop):
+        self._pair(half, stop).wait_recv()
+        later = stop * 2 + half + 3
+        if later < 8:
+            self._pair(later % 2, later // 2).start()
+        own, near = self._plane(half, stop), self.bufs["near"].at[stop, half]
         add_into(lambda i: own.at[i // 2, i % 2], lambda i: near.at[i // 2, i % 2], 4)
-
-    def _block(self, half, z):
-        raise NotImplementedError
-
-    def _send_z(self, half, z, up):
-        p, s = self.p, self.sems
-        side = 0 if up else 1
-        return remote(self._block(half, z), self.bufs["z"].at[half, z, side], s["zs"].at[half, z],
-                      s["zr"].at[half, z, side], p.me + 8 if up else p.me - 8)
-
-    def _wait_z(self, half, z, up):
-        p, s = self.p, self.sems
-        side = 0 if up else 1
-        remote(self._block(half, z), self.bufs["z"].at[half, z, side], s["zs"].at[half, z],
-               s["zr"].at[half, z, side], p.me).wait_recv()
-
-    def along_z(self, half, k):
+        self._first(half, stop).start()
+
+    def stage_two(self, half, stop):
         p = self.p
-        z = p.z + k
-        if k == 0:
-            self.end_z(half)
+        self._first(half, stop).wait_recv()
+        own, came = self._plane(half, stop), self.bufs["first"].at[stop, half]
+        if half:
+            add_into(lambda i: own.at[i, p.x], lambda i: came.at[i], 2)
+        else:
+            add_into(lambda i: own.at[p.y, i], lambda i: came.at[i], 2)
+        self._second(half, stop).start()
+
+    def stage_three(self, half, stop):
+        self._second(half, stop).wait_recv()
+        kept, came = self._block(half, stop), self.bufs["second"].at[stop, half]
+        add_into(lambda i: kept, lambda i: came, 1)
+
+    def stage_four(self, half, stop):
+        p = self.p
+        block = self._block(half, stop)
+        if stop < 3:
+
+            def join():
+                came = self._came(half, block, self.goal(stop))
+                add_into(lambda i: block, lambda i: came, 1)
+
+            pl.when(self.joins(stop))(join)
+            self._send_z(half, stop, block).start()
             return
-        up = k > 0
-
-        def join():
-            self._wait_z(half, z, up)
-            self._add_z(half, z, 0 if up else 1)
-
-        pl.when(p.z > 0 if up else p.z < 3)(join)
-        self._send_z(half, z, up).start()
+        out = self.sink(half)
+        out[...] = block[...].astype(F32)
+
+        def last(slot):
+            out[...] += self._came(half, block, slot)[...].astype(F32)
+
+        pl.when(p.z > 0)(lambda: last(p.z))
+        pl.when(p.z < 3)(lambda: last(4))
+
+    def z_events(self):
+        return [functools.partial(self.stage_four, half, stop)
+                for stop in range(4) for half in range(2)]
 
     def finish(self):
+        for half in range(2):
+            for stop in range(4):
+                self._pair(half, stop).wait_send()
+                self._first(half, stop).wait_send()
+                self._second(half, stop).wait_send()
+                if stop < 3:
+                    self._send_z(half, stop, self._block(half, stop)).wait_send()
+
+
+class ExpertReduce(Reduce):
+    def _source(self, half, stop):
+        return self.ref.at[self.goal(stop), half]
+
+    def _load(self, half, stop):
+        return pltpu.make_async_copy(
+            self._source(half, stop), self.bufs["own"].at[half], self.sems["load"].at[half])
+
+    def start_load(self, half, stop):
+        pl.when(self.joins(stop))(lambda: self._load(half, stop).start())
+
+    def begin(self):
+        for half in range(2):
+            self.start_load(half, 0)
+
+    def plain_send(self, half, stop):
         p = self.p
-        for half in range(2):
-            for z in range(4):
-                if self.m > 1:
-                    self._pair(half, z).wait_send()
-                pl.when(p.z != z)(lambda: self._send_z(half, z, True).wait_send())
-
-
-class DenseReduce(Reduce):
-    def _block(self, half, z):
-        return self.own.at[z, half, self.p.y, self.p.x]
-
-    def _add_z(self, half, z, side):
-        kept, came = self._block(half, z), self.bufs["z"].at[half, z, side]
-        add_into(lambda i: kept, lambda i: came, 1)
-
-    def _first(self, half, z):
-        p, s = self.p, self.sems
-        src = self.own.at[z, half, :, 1 - p.x] if half else self.own.at[z, half, 1 - p.y]
-        return remote(src, self.bufs["first"].at[z, half], s["fs"].at[z, half], s["fr"].at[z, half],
-                      p.across_x if half else p.across_y)
-
-    def _second(self, half, z):
-        p, s = self.p, self.sems
-        src = self.own.at[z, half, 1 - p.y, p.x] if half else self.own.at[z, half, p.y, 1 - p.x]
-        return remote(src, self.bufs["second"].at[z, half], s["ss"].at[z, half],
-                      s["sr"].at[z, half], p.across_y if half else p.across_x)
-
-    def stage_one(self, half, k):
-        def run():
-            self.pair_sum(half, k)
-            self._first(half, self.p.z + k).start()
-
-        pl.when(self.valid(k))(run)
-
-    def stage_two(self, half, k):
+        pl.when((p.z == 0) | (p.z == 3))(
+            lambda: self._send_z(half, stop, self._source(half, stop)).start())
+
+    def stage_one(self, half, stop):
         p = self.p
-        z = p.z + k
-
-        def run():
-            self._first(half, z).wait_recv()
-            own, came = self.own.at[z, half], self.bufs["first"].at[z, half]
-            if half:
-                add_into(lambda i: own.at[i, p.x], lambda i: came.at[i], 2)
-            else:
-                add_into(lambda i: own.at[p.y, i], lambda i: came.at[i], 2)
-            self._second(half, z).start()
-
-        pl.when(self.valid(k))(run)
-
-    def stage_three(self, half, k):
-        z = self.p.z + k
-
-        def run():
-            self._second(half, z).wait_recv()
-            kept, came = self._block(half, z), self.bufs["second"].at[z, half]
-            add_into(lambda i: kept, lambda i: came, 1)
-            self.along_z(half, k)
-
-        pl.when(self.valid(k))(run)
-
-    def end_z(self, half):
-        p = self.p
-        kept, got = self._block(half, p.z), self.bufs["z"]
-        out = self.sink(half)
-        out[...] = kept[...].astype(F32)
-
-        def join(side):
-            self._wait_z(half, p.z, side == 0)
-            out[...] += got[half, p.z, side].astype(F32)
-
-        pl.when(p.z > 0)(lambda: join(0))
-        pl.when(p.z < 3)(lambda: join(1))
-
-    def finish(self):
-        super().finish()
-        for half in range(2):
-            for z in range(4):
-                self._first(half, z).wait_send()
-                self._second(half, z).wait_send()
-
-
-class ExpertReduce(Reduce):
-    def _load(self, half, z):
-        return pltpu.make_async_copy(
-            self.ref.at[z, half], self.own.at[z, half], self.sems["load"].at[z, half])
-
-    def start(self, k):
-        z = self.p.z + k
-
-        def run():
-            for half in range(2):
-                self._load(half, z).start()
-
-        pl.when(self.valid(k))(run)
-
-    def _block(self, half, z):
-        return self.own.at[z, half]
-
-    def _add_z(self, half, z, side):
-        kept, came = self._block(half, z), self.bufs["z"].at[half, z, side]
-        add_into(lambda i: kept.at[i // 2, i % 2], lambda i: came.at[i // 2, i % 2], 4)
-
-    def stage_one(self, half, k):
-        def run():
-            self._load(half, self.p.z + k).wait()
-            self.along_z(half, k)
-
-        pl.when(self.valid(k))(run)
+        own = self.bufs["own"].at[half]
+
+        def join(slot, into_own):
+            came = self._came(half, self._source(half, stop), slot)
+            kept, added = (own, came) if into_own else (came, own)
+            add_into(lambda i: kept.at[i // 2, i % 2], lambda i: added.at[i // 2, i % 2], 4)
+
+        def middle():
+            z = self.goal(stop)
+            self._load(half, stop).wait()
+            join(z, False)
+            self._send_z(half, stop, self.bufs["z"].at[half, z]).start()
+
+        if stop < 3:
+            pl.when(self.joins(stop))(middle)
+            self.start_load(half, stop + 1)
+            return
+        self._load(half, stop).wait()
+        pl.when(p.z > 0)(lambda: join(p.z, True))
+        pl.when(p.z < 3)(lambda: join(4, True))
+        for i in range(3):
+            self._cross(half, i).start()
 
     def _cross(self, half, i):
         p, s = self.p, self.sems
         device = (p.across_x, p.across_y, p.across_both)[i]
         chip = device // 2 % 4
-        src = self.own.at[p.z, half, chip // 2, chip % 2]
+        src = self.bufs["own"].at[half, chip // 2, chip % 2]
         return remote(src, self.bufs["cross"].at[half, i], s["cs"].at[half, i], s["cr"].at[half, i], device)
-
-    def end_z(self, half):
-        p = self.p
-        pl.when(p.z > 0)(lambda: (self._wait_z(half, p.z, True), self._add_z(half, p.z, 0)) and None)
-        pl.when(p.z < 3)(lambda: (self._wait_z(half, p.z, False), self._add_z(half, p.z, 1)) and None)
-        for i in range(3):
-            self._cross(half, i).start()
 
     def crossed(self, half):
         p = self.p
-        self.sink(half, p.chip)[...] = self.own[p.z, half, p.y, p.x].astype(F32)
+        self.sink(half, p.chip)[...] = self.bufs["own"][half, p.y, p.x].astype(F32)
         for i in range(3):
             self._cross(half, i).wait_recv()
             device = (p.across_x, p.across_y, p.across_both)[i]
             self.sink(half, device // 2 % 4)[...] = self.bufs["cross"][half, i].astype(F32)
 
     def finish(self):
-        super().finish()
         for half in range(2):
             for i in range(3):
                 self._cross(half, i).wait_send()
-
-
-def reduce_kernel(
-    small_in, sums, wa1, wmo, wmi, wa0,
-    small_out, wide_out, tall_out,
-    own, near, first, second, z_dense, z_expert, cross, done, small_got,
-    load_sems, pair_sems, plane_sems, zs_sems, zr_sems, cross_sems, small_sems, meet,
+            for stop in range(3):
+                self._send_z(half, stop, self._source(half, stop)).wait_send()
+
+
+class Pump:
+    def __init__(self):
+        self.queue, self.due = [], 0.0
+
+    def add(self, events):
+        self.queue += events
+
+    def run(self, count):
+        self.due = min(self.due + count, 8.0)
+        while self.due >= 1 and self.step():
+            self.due -= 1
+
+    def step(self):
+        if self.queue:
+            self.queue.pop(0)()
+            return True
+        return False
+
+
+class Belt(Pump):
+    def __init__(self, lag, after):
+        super().__init__()
+        self.units, self.done, self.lag, self.after = [], [0, 0, 0, 0], lag, after
+
+    def add(self, job):
+        self.units += [(job, half, stop) for stop in range(4) for half in range(2)]
+
+    def step(self):
+        moved = False
+        for stage in range(4):
+            ahead = self.done[stage - 1] if stage else len(self.units)
+            mine = self.done[stage]
+            flush = ahead == len(self.units)
+            if mine < ahead and (stage == 0 or flush or ahead - mine > self.lag):
+                job, half, stop = self.units[mine]
+                self.done[stage] += 1
+                moved = True
+                if stage < 3:
+                    (job.stage_one, job.stage_two, job.stage_three)[stage](half, stop)
+                else:
+                    self.after(job, half, stop)
+        return moved
+
+
+def window(device):
+    return jnp.minimum(device * 24 // 128, 4) * 128
+
+
+def backward_step(
+    images, seq,
+    g_in, small, small_grad_in, x2, x1, x0, an1, qkv1, o1, mn, slope, ma, an0, qkv0, o0,
+    wa1, wmo, wmi, wa0, sums,
+    g_ref, small_out, wide_out, tall_out,
+    xf, low, do, dqkv, dn, an_buf, mix_buf, ds,
+    dw_wide, dw_tall, near, first, second, z_dense, own, z_expert, cross, done, small_got,
+    load_sems, expert_load_sems, pair_sems, plane_sems, zs_sems, zr_sems, cross_sems, small_sems,
+    meet, stream_sems, credit,
 ):
     p = Place()
     greet_all(p, 32)
     jobs = []
-    for m, ref in enumerate((sums.at[0], sums.at[1], wa1, wmo, wmi, wa0)):
-        sems = {"load": load_sems.at[m], "ps": pair_sems.at[m, 0], "pr": pair_sems.at[m, 1],
-                "zs": zs_sems.at[m], "zr": zr_sems.at[m]}
+    sets = {2: 0, 3: 1, 4: 2, 5: 0}
+    refs = {2: dw_wide.at[0], 3: dw_tall, 4: dw_wide.at[1], 5: dw_wide.at[2]}
+    for m in range(6):
+        sems = {"zs": zs_sems.at[m], "zr": zr_sems.at[m]}
         if m < 2:
-            sems.update(cs=cross_sems.at[m, 0], cr=cross_sems.at[m, 1])
-            bufs = {"z": z_expert.at[m], "cross": cross.at[m]}
+            sems.update(cs=cross_sems.at[m, 0], cr=cross_sems.at[m, 1], load=expert_load_sems.at[m])
+            bufs = {"z": z_expert.at[m], "cross": cross.at[m], "own": own.at[m]}
             if m == 0:
                 def sink(half, e):
                     return done.at[3 + e, :, pl.ds(half * 768, 768)]
             else:
                 def sink(half, e):
                     return tall_out.at[1 + e, pl.ds(half * 48, 48), :]
-            jobs.append(ExpertReduce(p, m, ref, own.at[m], None, bufs, sems, sink))
+            jobs.append(ExpertReduce(p, m, sums.at[m], bufs, sems, sink))
             continue
+        sems.update(ps=pair_sems.at[m - 2, 0], pr=pair_sems.at[m - 2, 1])
         for i, name in enumerate(("fs", "fr", "ss", "sr")):
             sems[name] = plane_sems.at[m - 2, i]
-        bufs = {"z": z_dense.at[m - 2], "first": first.at[m - 2], "second": second.at[m - 2]}
+        s = sets[m]
+        bufs = {"z": z_dense.at[m - 2], "first": first.at[s], "second": second.at[s], "near": near.at[s]}
         if m in WIDE_AT:
             def sink(half, m=m):
                 return done.at[WIDE_AT[m], :, pl.ds(half * 768, 768)]
         else:
             def sink(half):
                 return tall_out.at[0, pl.ds(half * 48, 48), :]
-        jobs.append(DenseReduce(p, m, ref, own.at[m], near.at[m - 2], bufs, sems, sink))
-
-    def spread(i):
-        to = (p.me + i) % 32
-        remote(small_in.at[to], small_got.at[p.me], small_sems.at[0, i], small_sems.at[1, p.me], to).start()
-
-    pl.loop(1, 32)(spread)
-    for k in FAR_FIRST:
-        for m in (0, 2, 1, 3, 4, 5):
-            jobs[m].start(k)
-    experts = [("e", m, k, h) for k in FAR_FIRST for m in (0, 1) for h in range(2)]
-    dense = [(m, k, h) for m in (2, 3, 4, 5) for k in FAR_FIRST for h in range(2)]
-    pumps = []
-    for i in range(len(dense) + 16):
-        for stage, lag in ((0, 0), (1, 8), (2, 16)):
-            if 0 <= i - lag < len(dense):
-                pumps.append((stage,) + dense[i - lag])
-    at = {j * len(pumps) // len(experts): e for j, e in enumerate(experts)}
-    for i, (stage, m, k, half) in enumerate(pumps):
-        if i in at:
-            _, em, ek, eh = at[i]
-            jobs[em].stage_one(eh, ek)
-        job = jobs[m]
-        (job.stage_one, job.stage_two, job.stage_three)[stage](half, k)
+        jobs.append(DenseReduce(p, m, refs[m], bufs, sems, sink))
     for m in range(2):
-        for half in range(2):
-            jobs[m].crossed(half)
+        jobs[m].begin()
+
+    experts = Pump()
+
+    def along(job, half, stop):
+        experts.add([functools.partial(job.stage_four, half, stop)])
+        if job.m == 2 and (half, stop) == (1, 3):
+            for device in (p.sibling, p.across_x, p.across_y):
+                pl.semaphore_signal(credit, inc=1, device_id=(device,), device_id_type=MESH_ID)
+
+    dense = Belt(LAG, along)
+    units = [(m, half, stop) for stop in range(4) for m in range(2) for half in range(2)]
+
+    def expert_event(i):
+        if i + AHEAD < 12:
+            m, half, stop = units[i + AHEAD]
+            jobs[m].plain_send(half, stop)
+        m, half, stop = units[i]
+        jobs[m].stage_one(half, stop)
+
+    for m, half, stop in units[:AHEAD]:
+        jobs[m].plain_send(half, stop)
+    experts.add([functools.partial(expert_event, i) for i in range(16)])
+    experts.add([functools.partial(jobs[m].crossed, half) for m in range(2) for half in range(2)])
+
+    def pump(e=1, d=0):
+        experts.run(e)
+        dense.run(d)
+
+    def load(pairs, sems):
+        copies = [pltpu.make_async_copy(src, dst, sems.at[i]) for i, (src, dst) in enumerate(pairs)]
+        for copy in copies:
+            copy.start()
+        return copies
+
+    def attention(w_src, x_src, an_src, qkv_src, o_src, dw, row, ready, pump):
+        def scope(w_buf):
+            qkv, o = mix_buf.at[:, pl.ds(0, 2304)], mix_buf.at[:, pl.ds(2304, 768)]
+            x_to = xf if x_src.dtype == F32 else low
+            copies = load([(x_src, x_to), (o_src, o), (an_src, an_buf), (qkv_src, qkv),
+                           (w_src.reshape(WIDTH, HIDDEN), w_buf)], load_sems)
+            for copy in copies[:2]:
+                copy.wait()
+            if x_src.dtype != F32:
+                xf[...] = low[...].astype(F32)
+
+            def weights_here():
+                for copy in copies[2:]:
+                    copy.wait()
+
+            attention_backward(
+                g_ref, xf, small[row : row + 1, :], w_buf, an_buf, qkv, o, dw, ds, row, images, seq,
+                low, do, dqkv, dn, weights_here, ready, pump,
+            )
+
+        pl.run_scoped(scope, pltpu.VMEM((WIDTH, HIDDEN), BF16))
+
+    g_ref[...] = g_in[...]
+    ds[...] = small_grad_in[...]
+    attention(wa1, x2, an1, qkv1, o1, dw_wide.at[0].reshape(WIDTH, HIDDEN), 1, jobs[2].start,
+              lambda: pump(*PACE[0]))
+    dense.add(jobs[2])
+
+    def feed_forward(wo_buf, wi_buf, slope_buf, ma_buf):
+        wo, wi = wmo.reshape(HIDDEN, WIDTH), wmi.reshape(WIDTH, HIDDEN)
+        dwo, dwi = dw_tall.reshape(HIDDEN, WIDTH), dw_wide.at[1].reshape(WIDTH, HIDDEN)
+        first_loads = load([(x1, xf), (mn, an_buf)], load_sems)
+
+        def chunk(n):
+            cols = pl.ds(n * 512, 512)
+            slot = n % 2
+            return load([(wo.at[cols, :], wo_buf.at[slot]), (wi.at[:, cols], wi_buf.at[slot]),
+                         (slope.at[:, cols], slope_buf.at[slot]), (ma.at[:, cols], ma_buf.at[slot])],
+                        stream_sems.at[slot])
+
+        coming = chunk(0)
+        low[...] = g_ref[...].astype(BF16)
+        dn[...] = jnp.zeros_like(dn)
+        for copy in first_loads:
+            copy.wait()
+        for n in range(6):
+            for copy in coming:
+                copy.wait()
+            if n < 5:
+                coming = chunk(n + 1)
+            slot = n % 2
+            cols = pl.ds(n * 512, 512)
+            dwo[cols, :] = tn(ma_buf[slot], low[...]).astype(BF16)
+            dact = nt(low[...], wo_buf[slot])
+            dh = (slope_buf[slot].astype(F32) * dact).astype(BF16)
+            dwi[:, cols] = tn(an_buf[...], dh).astype(BF16)
+            dn[...] += nt(dh, wi_buf[slot])
+            pump(*PACE[1])
+        jobs[3].start()
+        jobs[4].start()
+        norm_back(x1_buf, small[2:3, :], dn, g_ref, ds, 2)
+
+    x1_buf = xf
+    rows = g_ref.shape[0]
+    pl.run_scoped(
+        feed_forward, pltpu.VMEM((2, 512, WIDTH), BF16), pltpu.VMEM((2, WIDTH, 512), BF16),
+        pltpu.VMEM((2, rows, 512), BF16), pltpu.VMEM((2, rows, 512), BF16))
+    dense.add(jobs[3])
+    dense.add(jobs[4])
+
+    def last_ready():
+        assert dense.done[3] >= 8
+        pl.semaphore_wait(credit, 3)
+        jobs[5].start()
+
+    attention(wa0, x0, an0, qkv0, o0, dw_wide.at[2].reshape(WIDTH, HIDDEN), 0, last_ready,
+              lambda: pump(*PACE[2]))
+
+    def small_copy(to, i, source):
+        return remote(ds.at[:, pl.ds(pl.multiple_of(window(to), 128), 256)], small_got.at[source],
+                      small_sems.at[0, i], small_sems.at[1, source], to)
+
+    pl.loop(1, 32)(lambda i: small_copy((p.me + i) % 32, i, p.me).start())
+    dense.add(jobs[5])
+    while dense.done[3] < len(dense.units) or experts.queue:
+        pump(*PACE[3])
     swap = remote(
         done.at[:, pl.ds(pl.multiple_of((1 - p.core) * 24, 8), 24), :], wide_out.at[p.core],
         meet.at[0], meet.at[1], p.sibling)
     swap.start()
-    wide_out[p.core] = done[:, pl.ds(pl.multiple_of(p.core * 24, 8), 24), :]
-
-    def spread_done(i):
-        to = (p.me + i) % 32
-        remote(small_in.at[to], small_got.at[to], small_sems.at[0, i], small_sems.at[1, to], to).wait()
-
-    pl.loop(1, 32)(spread_done)
-    small_got[p.me] = small_in[p.me]
+    keep = pltpu.make_async_copy(
+        done.at[:, pl.ds(pl.multiple_of(p.core * 24, 8), 24), :], wide_out.at[p.core], meet.at[2])
+    keep.start()
+    pl.loop(1, 32)(lambda i: small_copy((p.me + i) % 32, i, (p.me + i) % 32).wait())
+    small_got[p.me] = ds[:, pl.ds(pl.multiple_of(window(p.me), 128), 256)]
     small_out[...] = jnp.sum(small_got[...], 0)
-    for job in jobs:
-        job.finish()
+    for m in range(6):
+        jobs[m].finish()
+    keep.wait()
     swap.wait()
 
 
-def run_reduce(small, sums, wa1, wmo, wmi, wa0):
+def run_backward_step(images, seq, args):
     any_space = pl.BlockSpec(memory_space=pl.ANY)
     vmem = pl.BlockSpec(memory_space=pltpu.VMEM)
     dma = pltpu.SemaphoreType.DMA
     piece = (48, 768)
+    rows = args[0].shape[0]
+    act, low = pltpu.VMEM((rows, WIDTH), F32), pltpu.VMEM((rows, WIDTH), BF16)
     return pl.pallas_call(
-        reduce_kernel,
-        out_shape=[struct((8, 128), F32), struct((2, 7, 24, 1536), F32), struct((5, 96, 768), F32)],
-        in_specs=[vmem] + [any_space] * 5,
-        out_specs=[vmem] * 3,
+        functools.partial(backward_step, images, seq),
+        out_shape=[struct((rows, WIDTH), F32), struct((8, 256), F32),
+                   struct((2, 7, 24, 1536), F32), struct((5, 96, 768), F32)],
+        in_specs=[vmem] * 3 + [any_space] * (len(args) - 3),
+        out_specs=[vmem, vmem, any_space, vmem],
         scratch_shapes=[
-            pltpu.VMEM((6, 4, 2, 2, 2) + piece, BF16),
-            pltpu.VMEM((4, 4, 2, 2, 2) + piece, BF16),
-            pltpu.VMEM((4, 4, 2, 2) + piece, BF16),
-            pltpu.VMEM((4, 4, 2) + piece, BF16),
-            pltpu.VMEM((4, 2, 4, 2) + piece, BF16),
-            pltpu.VMEM((2, 2, 4, 2, 2, 2) + piece, BF16),
+            act, low, low, pltpu.VMEM((rows, 3 * WIDTH), BF16), act, low,
+            pltpu.VMEM((rows, HIDDEN), BF16), pltpu.VMEM((8, WIDTH), F32),
+            pltpu.VMEM((3, 4, 2, 2, 48, HIDDEN), BF16),
+            pltpu.VMEM((4, 2, 2, 192, WIDTH), BF16),
+            pltpu.VMEM((3, 4, 2, 2, 2) + piece, BF16),
+            pltpu.VMEM((3, 4, 2, 2) + piece, BF16),
+            pltpu.VMEM((3, 4, 2) + piece, BF16),
+            pltpu.VMEM((4, 2, 5) + piece, BF16),
+            pltpu.VMEM((2, 2, 2, 2) + piece, BF16),
+            pltpu.VMEM((2, 2, 5, 2, 2) + piece, BF16),
             pltpu.VMEM((2, 2, 3) + piece, BF16),
             pltpu.VMEM((7, 48, 1536), F32),
-            pltpu.VMEM((32, 8, 128), F32),
-            dma((6, 4, 2)),
-            dma((6, 2, 4, 2)),
+            pltpu.VMEM((32, 8, 256), F32),
+            dma((5,)),
+            dma((2, 2)),
+            dma((4, 2, 4, 2)),
             dma((4, 4, 4, 2)),
             dma((6, 2, 4)),
-            dma((6, 2, 4, 2)),
+            dma((6, 2, 5)),
             dma((2, 2, 2, 3)),
             dma((2, 32)),
-            dma((2,)),
+            dma((3,)),
+            dma((2, 4)),
+            pltpu.SemaphoreType.REGULAR,
         ],
         compiler_params=pltpu.CompilerParams(
-            collective_id=1, has_side_effects=True, vmem_limit_bytes=62 << 20),
-        cost_estimate=pl.CostEstimate(flops=0, bytes_accessed=60_000_000, transcendentals=0),
-    )(small, sums, wa1, wmo, wmi, wa0)
-
-
-def fast_reduce(dsmall, sums, d0, dmi, dmo, d1):
-    small = jnp.pad(dsmall.reshape(8, 32, 24).transpose(1, 0, 2), ((0, 0), (0, 0), (0, 104)))
+            collective_id=1, has_side_effects=True, vmem_limit_bytes=63 << 20),
+        cost_estimate=pl.CostEstimate(
+            flops=20_000_000_000, bytes_accessed=60_000_000, transcendentals=0),
+    )(*args)
+
+
+def fast_backward(images, seq, x0, g4, small, weights, saved, y_back, d_back, sums):
+    rows = x0.shape[0]
+    act = struct((rows, WIDTH), F32)
+    wa0, wmi, wmo, wa1 = weights
+    x1, x2, x3, an0, qkv0, o0, mn, slope, ma, an1, qkv1, o1, en, aux, p0, p1 = saved
+    x4, g, ds = call(
+        combine_kernel, [act, act, struct((8, WIDTH), F32)], [pltpu.VMEM((rows, WIDTH), F32)],
+        [g4, small, x3, en, aux, p0, p1, y_back, d_back], 3_000_000_000,
+    )
     w = lambda g: g.reshape(4, 2, 2, 48, HIDDEN)
     t = lambda g: g.reshape(4, 2, 2, 192, WIDTH)
-    small, wide, tall = run_reduce(small, sums, w(d1), t(dmo), w(dmi), w(d0))
+    g, dsmall, wide, tall = run_backward_step(images, seq, [
+        g, small, ds, x2, x1, x0, an1, qkv1, o1, mn, slope, ma, an0, qkv0, o0,
+        w(wa1), t(wmo), w(wmi), w(wa0), sums])
+    me = lax.axis_index("fsdp")
+    dsmall = lax.dynamic_slice(dsmall, (0, me * 24 - window(me)), (8, 24))
     wide = wide.transpose(1, 2, 0, 3).reshape(7, 24, HIDDEN)
-    return (small[:, :24].T, wide[0], wide[1], tall[0], wide[2],
-            wide[3:].transpose(1, 0, 2), tall[1:].transpose(1, 0, 2))
+    return x4, g, (dsmall.T, wide[0], wide[1], tall[0], wide[2],
+                   wide[3:].transpose(1, 0, 2), tall[1:].transpose(1, 0, 2))
 
 
 def expert_step(
@@ -1376,24 +1554,22 @@
 
     if n == 32:
         y_back, d_back, sums = run_expert_step(rows_x, rows_d, w_in, w_out)
+        x4, grad, shards = fast_backward(
+            images, seq, x0, g4, small, weights, saved, y_back, d_back, sums)
+        dsmall, d0, dmi, dmo, d1, de_in, de_out = shards
     else:
         y, dx, dw_in, dw_out = run_expert(exchange(rows_x), exchange(rows_d), w_in, w_out)
-        y_back, d_back = exchange(y), exchange(dx)
-    x4, grad, d0, dmi, dmo, d1, dsmall = run_backward(
-        images, seq, x0, g4, small, weights, saved, y_back, d_back
-    )
-
-    def unpad(values):
-        return values.reshape(images, padded, width)[:, :seq]
-
-    block_out = jnp.where(alive[:, None, None], unpad(x4), 0.0).astype(BF16)
-    if n == 32:
-        dsmall, d0, dmi, dmo, d1, de_in, de_out = fast_reduce(
-            dsmall, sums, d0, dmi, dmo, d1)
-    else:
+        x4, grad, d0, dmi, dmo, d1, dsmall = run_backward(
+            images, seq, x0, g4, small, weights, saved, exchange(y), exchange(dx)
+        )
         d0, dmi, dmo, d1 = (plain_reduce(g).astype(F32) for g in (d0, dmi, dmo, d1))
         de_in, de_out = (plain_reduce_expert(g).astype(F32) for g in (dw_in, dw_out))
         dsmall = lax.psum_scatter(dsmall.T, "fsdp", scatter_dimension=0, tiled=True)
+
+    def unpad(values):
+        return values.reshape(images, padded, width)[:, :seq]
+
+    block_out = jnp.where(alive[:, None, None], unpad(x4), 0.0).astype(BF16)
     return (
         block_out,
         unpad(grad),

time: 586 us -> 511 us (0.87)
  Pallas kernels: 535 us -> 471 us
    pallas_call x5 -> x2, Pallas kernels: 157 us -> 73.2 us  [call(): pl.pallas_call(body, out_shape=outs, in_specs=[pl.BlockSpec(memory_space=...]
    pallas_call x1, Pallas kernels: 146 us -> 165 us  [run_backward_step(): pl.pallas_call(functools.partial(backward_step, images, seq), out_shape=[...]
where the time goes in v3:
time: 511 us; the launch traced here: 506 us
  Pallas kernels  471 us (92%)
  local copies, waits for them, and re-layouts  29.1 us (6%)
    pallas_call x1, Pallas kernels, run_backward_step(): pl.pallas_call(functools.partial(backward_step, images, seq), out_shape=[...  165 us
    pallas_call x1, Pallas kernels, run_gather(): pl.pallas_call(gather_kernel, out_shape=[struct((32, 8, 128), F32), wide_...  159 us
    pallas_call x2, Pallas kernels, call(): pl.pallas_call(body, out_shape=outs, in_specs=[pl.BlockSpec(memory_space=...  73.2 us
    pallas_call x1, Pallas kernels, run_expert_step(): pl.pallas_call(expert_step, out_shape=[struct(rows, BF16)] * 2 + [struct(...  73 us

profile of v3, /device:TPU:0, one launch (start us, length us, event | category | flops | bytes accessed | tf_op | source)
XLA Modules:
  0.0 506.0 jit_solution(13553184434025696902)
XLA Ops:
  0.6 0.0 copy-start.8
  0.7 1.5 fusion.11
  2.2 1.1 fusion.13
  3.4 0.8 fusion.10
  4.5 3.1 reshape.110
  7.6 2.0 copy.115
  9.6 0.0 copy-start.6
  9.6 0.0 copy-start.7
  9.7 2.1 reshape.107.wide_in
  11.7 0.0 copy-done.6
  11.7 0.0 copy-start.14
  11.7 0.1 copy.116
  11.8 0.9 pad_maximum_fusion.tall_in
  12.8 0.0 copy-done.11
  12.8 0.0 copy-done.13
  12.8 0.6 pad_convert_fusion.small_in
  13.4 159.4 %shard_map.229 = (f32[32,8,128]{2,1,0:T(8,128)}, bf16[4,2,2,48,3072]{4,3,2,1,0:T(8,128)(2,1)}, bf16[4,2,2,48,3072]{4,3,2,1,0:T(8,128)(2,1)}, bf16[4,2,2,192,768]...) custom-call(f32[8,128]{1,0:T(8,128)} %pad_convert_fusion.small_in, ...), custom_call_target="tpu_custom_call" | custom-call | bytes 60000000 | tf_op jit(solution)/shard_map/pallas_call | solution.py:821
  172.8 0.9 slice_bitcast_fusion.5
  173.8 0.1 slice.103
  173.9 0.1 slice.105
  174.0 0.1 pad.27.clone
  174.1 0.1 pad.29.clone
  174.2 0.9 maximum_maximum_fusion.small_ref.small
  175.7 0.0 copy-done.4
  175.7 0.0 copy-start.5
  175.7 0.6 broadcast_select_fusion
  176.3 0.1 copy.80
  176.3 0.0 copy-start.9
  176.4 0.9 pad.17.clone
  177.2 0.1 copy.81
  177.3 0.9 pad.20.clone
  178.2 0.1 reshape.94
  178.3 0.1 copy.59
  178.4 0.7 pad.21
  179.1 61.1 %shard_map.230 = (f32[416,768]{1,0:T(8,128)}, f32[416,768]{1,0:T(8,128)}, f32[416,768]{1,0:T(8,128)}, bf16[416,768]{1,0:T(8,128)(2,1)}, bf16[416,2304]{1,0:T(8,1...) custom-call(bf16[416,768]{1,0:T(8,128)(2,1)} %bitcast.108, ...), custom_call_target="tpu_custom_call" | custom-call | flops 8000000000 | bytes 42249472 | tf_op jit(solution)/shard_map/pallas_call | solution.py:353
  240.3 73.0 %shard_map.231 = (bf16[4,256,768]{2,1,0:T(8,128)(2,1)}, bf16[4,256,768]{2,1,0:T(8,128)(2,1)}, bf16[2,4,2,2,2,48,768]{6,5,4,3,2,1,0:T(8,128)(2,1)}) custom-call(bf16[4,256,768]{2,1,0:T(8,128)(2,1)} %bitcast.122, bf16[4,256,768]{2,1,0:T(8,128)(2,1)} %bitcast.123, bf16[4,2,2,48,3072]{4,3,2,1,0:T(8,128)(2,1)} %get-tuple-element.59.ein, ...), custom_call_target="tpu_custom_call" | custom-call | flops 30000001024 | bytes 40000000 | tf_op jit(solution)/shard_map/pallas_call | solution.py:1469
  313.3 12.1 %shard_map.232 = (f32[416,768]{1,0:T(8,128)}, f32[416,768]{1,0:T(8,128)}, f32[8,768]{1,0:T(8,128)}) custom-call(bf16[416,768]{1,0:T(8,128)(2,1)} %bitcast.111, f32[136,768]{1,0:T(8,128)} %maximum_maximum_fusion.small_ref.small, f32[416,768]{1,0:T(8,128)} %get-tuple-element.52.x3_ref, bf16[416,768]{1,0:T(8,128)(2,1)} %get-tuple-element.53.en_ref, ...), custom_call_target="tpu_custom_call" | custom-call | flops 3000000000 | bytes 10616832 | tf_op jit(solution)/shard_map/pallas_call | solution.py:353
  325.3 165.0 %shard_map.233 = (f32[416,768]{1,0:T(8,128)}, f32[8,256]{1,0:T(8,128)}, f32[2,7,24,1536]{3,2,1,0:T(8,128)}, f32[5,96,768]{2,1,0:T(8,128)}) custom-call(f32[416,768]{1,0:T(8,128)} %get-tuple-element.64.g_in, f32[136,768]{1,0:T(8,128)} %maximum_maximum_fusion.small_ref.small, f32[8,768]{1,0:T(8,128)} %get-tuple-element.65.small_grad_in, ...), custom_call_target="tpu_custom_call" | custom-call | flops 20000000000 | bytes 60000000 | tf_op jit(solution)/shard_map/pallas_call | solution.py:1290
  490.4 1.2 fusion.9
  491.6 0.2 copy.62
  491.8 0.1 copy.83
  491.9 0.2 copy.63
  492.1 0.1 copy.84
  492.2 0.7 copy.67
  493.0 1.0 copy.66
  494.0 0.0 copy-done.1
  494.0 0.1 slice_bitcast_fusion
  494.1 0.1 copy.82
  494.2 0.0 copy-start.3
  494.2 1.8 copy.68
  496.0 0.1 slice.126
  496.1 1.6 copy.79
  497.7 0.1 slice_bitcast_fusion.1
  497.8 0.0 copy-start.10
  497.8 1.8 copy.69
  499.6 0.2 copy.64
  499.8 0.8 copy.85
  500.6 0.7 slice_bitcast_fusion.2
  501.3 0.1 dynamic-slice_bitcast_fusion
  501.4 0.6 slice.119
  502.0 0.5 slice_bitcast_fusion.8
  502.5 0.6 slice.108
  503.1 1.3 slice.125
  504.4 1.4 fusion
  (37 shorter events, 0.5 us)
Async XLA Ops:
  0.6 2.7 copy-start.8
  0.7 2.7 copy-start
  9.6 2.1 copy-start.6
  9.6 2.2 copy-start.7
  11.7 1.0 copy-start.11
  11.7 1.0 copy-start.12
  11.7 1.0 copy-start.13
  11.7 1.0 copy-start.14
  13.4 162.3 %copy-start.4 = (bf16[2,197,768]{2,0,1:T(2,128)(2,1)S(1)}, bf16[2,197,768]{2,0,1:T(2,128)(2,1)}, u32[]{:S(2)}) copy-start(bf16[2,197,768]{2,0,1:T(2,128)(2,1)} %param.27) | copy-start | bytes 1815556
  175.7 1.5 copy-start.5
  176.3 1.9 copy-start.9
  492.2 1.8 copy-start.1
  494.2 1.8 copy-start.3
  496.1 1.7 copy-start.2
  497.8 3.5 copy-start.10

commit v4 on v3

--- a/solution.py
+++ b/solution.py
@@ -197,34 +197,8 @@
     pump()
 
 
-def forward_kernel(
-    images, seq,
-    x0_ref, g4_ref, ids_ref, small_ref, wa0_ref, wmi_ref, wmo_ref, wa1_ref,
-    x1_ref, x2_ref, x3_ref, an0_ref, qkv0_ref, o0_ref, mn_ref, slope_ref, ma_ref,
-    an1_ref, qkv1_ref, o1_ref, en_ref, aux_ref, g0_ref, g1_ref, rx_ref, rd_ref,
-    xf_ref,
-):
-    rows = x0_ref.shape[0]
-    xf_ref[...] = x0_ref[...].astype(F32)
-    attention_forward(
-        xf_ref, small_ref[0:1, :], wa0_ref, x1_ref, an0_ref, qkv0_ref, o0_ref, images, seq
-    )
-    norm_rows(x1_ref, small_ref[2:3, :], mn_ref)
-    x2_ref[...] = x1_ref[...]
-
-    def dense(n):
-        cols = tile(n, 512)
-        active, slope = gelu_both(nn(mn_ref[...], wmi_ref[:, cols]))
-        slope_ref[:, cols] = slope.astype(BF16)
-        active = active.astype(BF16)
-        ma_ref[:, cols] = active
-        x2_ref[...] += nn(active, wmo_ref[cols, :])
-
-    loop(6, dense)
-    attention_forward(
-        x2_ref, small_ref[1:2, :], wa1_ref, x3_ref, an1_ref, qkv1_ref, o1_ref, images, seq
-    )
-    norm_rows(x3_ref, small_ref[3:4, :], en_ref)
+def route_rows(g4_ref, ids_ref, small_ref, en_ref, aux_ref, g0_ref, g1_ref, rx_ref, rd_ref, pump):
+    rows = en_ref.shape[0]
     logits = nt(en_ref[...], small_ref[8:136, :].astype(BF16))
     lane = lax.broadcasted_iota(jnp.int32, logits.shape, 1)
     logits = jnp.where(lane < EXPERTS, logits, -1e30)
@@ -255,7 +229,43 @@
         two = tn(g1_ref[:, cols], (g4 * gates[1]).astype(BF16))
         rd_ref[cols, :] = (one + two).astype(BF16)
 
-    loop(EXPERTS, fill)
+    pump()
+    loop(2, fill)
+    pump()
+    loop(2, lambda n: fill(n + 2))
+    pump()
+
+
+def forward_kernel(
+    images, seq,
+    x0_ref, g4_ref, ids_ref, small_ref, wa0_ref, wmi_ref, wmo_ref, wa1_ref,
+    x1_ref, x2_ref, x3_ref, an0_ref, qkv0_ref, o0_ref, mn_ref, slope_ref, ma_ref,
+    an1_ref, qkv1_ref, o1_ref, en_ref, aux_ref, g0_ref, g1_ref, rx_ref, rd_ref,
+    xf_ref,
+):
+    xf_ref[...] = x0_ref[...].astype(F32)
+    attention_forward(
+        xf_ref, small_ref[0:1, :], wa0_ref, x1_ref, an0_ref, qkv0_ref, o0_ref, images, seq
+    )
+    norm_rows(x1_ref, small_ref[2:3, :], mn_ref)
+    x2_ref[...] = x1_ref[...]
+
+    def dense(n):
+        cols = tile(n, 512)
+        active, slope = gelu_both(nn(mn_ref[...], wmi_ref[:, cols]))
+        slope_ref[:, cols] = slope.astype(BF16)
+        active = active.astype(BF16)
+        ma_ref[:, cols] = active
+        x2_ref[...] += nn(active, wmo_ref[cols, :])
+
+    loop(6, dense)
+    attention_forward(
+        x2_ref, small_ref[1:2, :], wa1_ref, x3_ref, an1_ref, qkv1_ref, o1_ref, images, seq
+    )
+    norm_rows(x3_ref, small_ref[3:4, :], en_ref)
+    route_rows(
+        g4_ref, ids_ref, small_ref, en_ref, aux_ref, g0_ref, g1_ref, rx_ref, rd_ref, lambda: None
+    )
 
 
 def expert_kernel(x_ref, d_ref, wi_ref, wo_ref, y_ref, dx_ref, dwi_ref, dwo_ref, yf_ref, df_ref):
@@ -728,40 +738,43 @@
 EXPERT_SEMS = ("zu", "zd", "zr", "hs", "hr")
 STEPS = (0, -1, 1, -2, 2, -3, 3)
 
-
-def gather_kernel(
-    small_in, wide_in, tall_in,
-    small_out, wa0, wmi, wmo, wa1, ein, eout,
-    wide_mine, expert_mine, from_sibling, meet, small_sems, gather_sems, own_sems, expert_sems,
-    cross_sems,
+FRONT = (0.05, (0.3, 4.7), (0.4, 7), (0.4, 14), 1)
+
+
+def front_kernel(
+    images, seq,
+    small_in, wide_in, tall_in, x0_ref, g4_ref, ids_ref,
+    small, wa0, wmi, wmo, wa1, ein, eout, *rest,
 ):
+    outs, mine, tools = rest[:18], rest[18:36], rest[36:]
+    (x1, x2, x3, an0, qkv0, o0, mn, slope, ma, an1, qkv1, o1, en, aux_ref, pick0, pick1, rx, rd) = mine
+    (xf, va0, vmi, vmo, va1, wide_mine, expert_mine, from_sibling, small_got,
+     meet, small_sems, gather_sems, own_sems, expert_sems, cross_sems, out_sems, weight_sems) = tools
     p = Place()
     greet_all(p, 32)
     swap = remote(wide_in.at[1 - p.core], from_sibling, meet.at[0], meet.at[1], p.sibling)
     swap.start()
 
-    def spread(i):
-        remote(small_in, small_out.at[p.me], small_sems.at[0, i], small_sems.at[1, p.me],
-               (p.me + i) % 32).start()
-
-    pl.loop(1, 32)(spread)
-    small_out[p.me] = small_in[...]
-    outs = (wa0, wmi, wmo, wa1)
-    dense = []
+    def small_copy(to, i, source):
+        return remote(small_in, small_got.at[source], small_sems.at[0, i], small_sems.at[1, source], to)
+
+    pl.loop(1, 32)(lambda i: small_copy((p.me + i) % 32, i, p.me).start())
+    small_got[p.me] = small_in[...]
+    landing, weights = (va0, vmi, vmo, va1), (wa0, wmi, wmo, wa1)
+    jobs = []
     for m, kind in enumerate(DENSE):
         sems = {name: gather_sems.at[m, i] for i, name in enumerate(GATHER_SEMS)}
         sems["own"] = own_sems.at[m]
-        mine = tall_in.at[0] if kind == "tall" else wide_mine.at[(0, 1, None, 2)[m]]
-        dense.append(Gather(p, kind, mine, outs[m], sems))
-    experts = []
+        piece = tall_in.at[0] if kind == "tall" else wide_mine.at[(0, 1, None, 2)[m]]
+        jobs.append(Gather(p, kind, piece, landing[m], sems))
+    big = []
     for m, kind in enumerate(("wide", "tall")):
         sems = {name: expert_sems.at[m, i] for i, name in enumerate(EXPERT_SEMS)}
         sems["cs"], sems["cr"], sems["own"] = (
             cross_sems.at[m, 0], cross_sems.at[m, 1], cross_sems.at[m, 2])
-        mine = tall_in.at[pl.ds(1, 4)] if kind == "tall" else expert_mine
-        experts.append(ExpertGather(p, kind, mine, (ein, eout)[m], sems))
-    dense[2].start_own()
-    experts[1].start_own()
+        piece = tall_in.at[pl.ds(1, 4)] if kind == "tall" else expert_mine
+        big.append(ExpertGather(p, kind, piece, (ein, eout)[m], sems))
+    jobs[2].start_own()
     swap.wait_recv()
 
     def merge(m, out):
@@ -773,72 +786,193 @@
         out[...] = jnp.concatenate([upper, lower], 0).astype(BF16)
 
     merge(0, wide_mine.at[0])
-    dense[0].start_own()
+    jobs[0].start_own()
+    big[1].start_own()
     for e in range(4):
         merge(3 + e, expert_mine.at[e])
-    experts[0].start_own()
+    big[0].start_own()
     merge(1, wide_mine.at[1])
-    dense[1].start_own()
+    jobs[1].start_own()
     merge(2, wide_mine.at[2])
-    dense[3].start_own()
-
-    order = [(m, k, half) for m in (0, 1, 2, 3) for k in STEPS for half in range(2)]
-    pumps = []
-    for i in range(len(order) + 16):
-        for stage, lag in ((0, 0), (1, 8), (2, 16)):
+    jobs[3].start_own()
+
+    dense, experts = Pump(), Pump()
+    order = [(m, k, half) for m in range(4) for k in STEPS for half in range(2)]
+    done_at = {}
+    for i in range(len(order) + 24):
+        for stage, lag in ((0, 0), (1, 12), (2, 24)):
             if 0 <= i - lag < len(order):
-                pumps.append((stage,) + order[i - lag])
-    turns = [(y, k, m) for k in STEPS[1:] for m in (1, 0) for y in range(2)]
-    at = {8 + j * (len(pumps) - 10) // len(turns): turn for j, turn in enumerate(turns)}
-    for i, (stage, m, k, half) in enumerate(pumps):
-        if i == 6:
-            experts[1].crossed()
-            experts[0].crossed()
-        if i in at:
-            y, kk, mm = at[i]
-            experts[mm].stage(y, kk)
-        job = dense[m]
-        (job.stage_one, job.stage_two, job.stage_three)[stage](half, k)
-    for job in dense + experts:
+                m, k, half = order[i - lag]
+                name = ("stage_one", "stage_two", "stage_three")[stage]
+                dense.add([functools.partial(getattr(jobs[m], name), half, k)])
+                if stage == 2:
+                    done_at[m] = len(dense.queue)
+    total = len(dense.queue)
+
+    def crossed():
+        big[1].crossed()
+        big[0].crossed()
+
+    experts.add([crossed])
+    experts.add([functools.partial(big[m].stage, y, k) for k in STEPS[1:] for m in (1, 0) for y in range(2)])
+
+    def pump(pace=(0, 0)):
+        experts.run(pace[0])
+        dense.run(pace[1])
+
+    def arrive(m):
+        while total - len(dense.queue) < done_at[m]:
+            pump((FRONT[0], 1))
+        jobs[m].arrived()
+        pltpu.make_async_copy(landing[m], weights[m], weight_sems.at[m]).start()
+
+    copies = []
+
+    def emit(i):
+        copy = pltpu.make_async_copy(mine[i], outs[i], out_sems.at[i])
+        copy.start()
+        copies.append(copy)
+
+    def attention(x, row, w_ref, xo, an, qkv, o, pace):
+        norm_rows(x, small[row : row + 1, :], an)
+        pump(pace)
+        for third in range(3):
+
+            def project(n, third=third):
+                cols = tile(n + third * 3, 256)
+                qkv[:, cols] = nn(an[...], w_ref[:, cols]).astype(BF16)
+
+            loop(3, project)
+            pump(pace)
+        rows_of = qkv.shape[0] // images
+        for image in range(images):
+            rows = pl.ds(image * rows_of, rows_of)
+
+            def pair(i, rows=rows):
+                q = qkv[rows, tile(i, 128)]
+                k = qkv[rows, tile(i + 6, 128)]
+                v = qkv[rows, tile(i + 12, 128)]
+                first = halves(q.shape)
+                zero = jnp.zeros_like(q)
+                p0 = head_probs(jnp.where(first, q, zero), k, seq).astype(BF16)
+                p1 = head_probs(jnp.where(first, zero, q), k, seq).astype(BF16)
+                out = nn(p0, jnp.where(first, v, zero)) + nn(p1, jnp.where(first, zero, v))
+                o[rows, tile(i, 128)] = out.astype(BF16)
+
+            for part in range(2):
+                loop(3, lambda i, pair=pair, part=part: pair(i + 3 * part))
+                pump(pace)
+
+        def outward(n):
+            cols = tile(n, 256)
+            xo[:, cols] = x[:, cols] + nn(o[...], w_ref[:, tile(n + 9, 256)])
+
+        loop(3, outward)
+        pump(pace)
+
+    xf[...] = x0_ref[...].astype(F32)
+    arrive(0)
+    pl.loop(1, 32)(lambda i: small_copy((p.me + i) % 32, i, (p.me + i) % 32).wait())
+    small[...] = jnp.zeros_like(small)
+    for d in range(32):
+        lanes = slice(24 * d, 24 * d + 24)
+        small[0:4, lanes] = small_got[d, 0:4, 0:24]
+        small[8:12, lanes] = small_got[d, 4:8, 0:24]
+    attention(xf, 0, va0.reshape(WIDTH, HIDDEN), x1, an0, qkv0, o0, FRONT[1])
+    for i in (0, 3, 4, 5):
+        emit(i)
+    norm_rows(x1, small[2:3, :], mn)
+    emit(6)
+    arrive(1)
+    wi = vmi.reshape(WIDTH, HIDDEN)
+    for n in range(6):
+        cols = pl.ds(n * 512, 512)
+        active, bend = gelu_both(nn(mn[...], wi[:, cols]))
+        slope[:, cols] = bend.astype(BF16)
+        ma[:, cols] = active.astype(BF16)
+        pump(FRONT[2])
+    emit(7)
+    emit(8)
+    arrive(2)
+    wo = vmo.reshape(HIDDEN, WIDTH)
+    for n in range(3):
+        cols = pl.ds(n * 256, 256)
+        x2[:, cols] = x1[:, cols] + nn(ma[...], wo[:, cols])
+        pump(FRONT[3])
+    emit(1)
+    arrive(3)
+    attention(x2, 1, va1.reshape(WIDTH, HIDDEN), x3, an1, qkv1, o1, (FRONT[4], 0))
+    for i in (2, 9, 10, 11):
+        emit(i)
+    norm_rows(x3, small[3:4, :], en)
+    route_rows(g4_ref, ids_ref, small, en, aux_ref, pick0, pick1, rx, rd, lambda: pump((FRONT[4], 0)))
+    for i in range(12, 18):
+        emit(i)
+    while experts.step():
+        pass
+    for job in big:
         job.arrived()
-    for job in dense + experts:
+    for job in jobs + big:
         job.finish()
     swap.wait_send()
-
-    def spread_done(i):
-        remote(small_in, small_out.at[(p.me + i) % 32], small_sems.at[0, i],
-               small_sems.at[1, (p.me + i) % 32], (p.me + i) % 32).wait()
-
-    pl.loop(1, 32)(spread_done)
-
-
-def run_gather(small, wide, tall):
+    for m in range(4):
+        pltpu.make_async_copy(landing[m], weights[m], weight_sems.at[m]).wait()
+    for copy in copies:
+        copy.wait()
+
+
+def run_front(images, seq, small, wide, tall, x0, g4, ids):
     any_space = pl.BlockSpec(memory_space=pl.ANY)
     vmem = pl.BlockSpec(memory_space=pltpu.VMEM)
-    wide_out = struct((4, 2, 2, 48, 3072), BF16)
-    tall_out = struct((4, 2, 2, 192, 768), BF16)
+    wide_out = struct((4, 2, 2, 48, HIDDEN), BF16)
+    tall_out = struct((4, 2, 2, 192, WIDTH), BF16)
     dma = pltpu.SemaphoreType.DMA
+    rows = x0.shape[0]
+    act, low = struct((rows, WIDTH), F32), struct((rows, WIDTH), BF16)
+    qkv, hid = struct((rows, 3 * WIDTH), BF16), struct((rows, HIDDEN), BF16)
+    pick, buf = struct((rows, EXPERTS * SLOT), BF16), struct((EXPERTS * SLOT, WIDTH), BF16)
+    kept = [act, act, act, low, qkv, low, low, hid, hid, low, qkv, low, low,
+            struct((rows, 128), F32), pick, pick, buf, buf]
+
+    def scratch(one):
+        return pltpu.VMEM(one.shape, one.dtype)
+
     return pl.pallas_call(
-        gather_kernel,
-        out_shape=[struct((32, 8, 128), F32), wide_out, wide_out, tall_out, wide_out,
-                   wide_out, tall_out],
-        in_specs=[vmem, vmem, vmem],
-        out_specs=[vmem] + [any_space] * 6,
-        scratch_shapes=[
+        functools.partial(front_kernel, images, seq),
+        out_shape=[struct((136, WIDTH), F32), wide_out, wide_out, tall_out, wide_out, wide_out,
+                   tall_out] + kept,
+        in_specs=[vmem] * 6,
+        out_specs=[vmem] + [any_space] * 24,
+        scratch_shapes=[scratch(one) for one in kept] + [
+            scratch(act), scratch(wide_out), scratch(wide_out), scratch(tall_out), scratch(wide_out),
             pltpu.VMEM((3, 48, 1536), BF16),
             pltpu.VMEM((4, 48, 1536), BF16),
             pltpu.VMEM((24, 7 * 1536), F32),
+            pltpu.VMEM((32, 8, 128), F32),
             dma((2,)),
             dma((2, 32)),
             dma((4, len(GATHER_SEMS), 8)),
             dma((4, 2)),
             dma((2, len(EXPERT_SEMS), 8)),
             dma((2, 3, 3)),
+            dma((18,)),
+            dma((4,)),
         ],
         compiler_params=pltpu.CompilerParams(
-            collective_id=0, has_side_effects=True, vmem_limit_bytes=VMEM_BYTES),
-        cost_estimate=pl.CostEstimate(flops=0, bytes_accessed=60_000_000, transcendentals=0),
-    )(small, wide, tall)
+            collective_id=0, has_side_effects=True, vmem_limit_bytes=63 << 20),
+        cost_estimate=pl.CostEstimate(
+            flops=9_000_000_000, bytes_accessed=60_000_000, transcendentals=0),
+    )(small, wide, tall, x0, g4, ids)
+
+
+def fast_front(images, seq, smalls, wide, mlp_out, expert_in, expert_out, x0, g4, ids):
+    small = jnp.pad(smalls.astype(F32).T, ((0, 0), (0, 128 - smalls.shape[0])))
+    packed = jnp.concatenate(wide + [expert_in[:, e] for e in range(EXPERTS)], 1).astype(F32)
+    packed = packed.reshape(24, 7, 2, 1536).transpose(2, 0, 1, 3).reshape(2, 24, 7 * 1536)
+    tall = jnp.concatenate([mlp_out[None], expert_out.transpose(1, 0, 2)], 0)
+    out = run_front(images, seq, small, packed, tall, x0, g4, ids)
+    small, wa0, wmi, wmo, wa1, ein, eout = out[:7]
+    return small, (wa0, wmi, wmo, wa1), ein, eout, out[7:23], out[23], out[24]
 
 KINDS = ("wide", "tall", "wide", "tall", "wide", "wide")
 WIDE_AT = {2: 2, 4: 1, 5: 0}
@@ -1062,7 +1196,7 @@
         self.queue += events
 
     def run(self, count):
-        self.due = min(self.due + count, 8.0)
+        self.due = min(self.due + count, count + 4.0)
         while self.due >= 1 and self.step():
             self.due -= 1
 
@@ -1499,18 +1633,6 @@
     return y.reshape(flat), d.reshape(flat), sums
 
 
-def fast_gather(smalls, wide, mlp_out, expert_in, expert_out):
-    width = smalls.shape[0] * 32
-    small = jnp.pad(smalls.astype(F32).T, ((0, 0), (0, 128 - smalls.shape[0])))
-    packed = jnp.concatenate(wide + [expert_in[:, e] for e in range(EXPERTS)], 1).astype(F32)
-    packed = packed.reshape(24, 7, 2, 1536).transpose(2, 0, 1, 3).reshape(2, 24, 7 * 1536)
-    tall = jnp.concatenate([mlp_out[None], expert_out.transpose(1, 0, 2)], 0)
-    small, wa0, wmi, wmo, wa1, ein, eout = run_gather(small, packed, tall)
-    small = small[:, :, : smalls.shape[0]].transpose(1, 0, 2).reshape(8, width)
-    flat = [w.reshape(width, HIDDEN) for w in (wa0, wmi, wa1)]
-    return small, flat[:2] + [flat[2]], [wmo.reshape(HIDDEN, width)], ein, eout
-
-
 def local(
     patches, live_count, expert_ids, attn_gain, attn_qkv, attn_out, mlp_gain, mlp_in, mlp_out,
     moe_gain, router, expert_in, expert_out, cotangent,
@@ -1536,17 +1658,18 @@
     wide = [jnp.concatenate([attn_qkv[:, 0], attn_out[:, 0]], 1), mlp_in,
             jnp.concatenate([attn_qkv[:, 1], attn_out[:, 1]], 1)]
     if n == 32:
-        small, wides, talls, w_in, w_out = fast_gather(smalls, wide, mlp_out, expert_in, expert_out)
+        small, weights, w_in, w_out, saved, rows_x, rows_d = fast_front(
+            images, seq, smalls, wide, mlp_out, expert_in, expert_out, x0, g4, ids)
     else:
         small, wides, talls, w_in, w_out = plain_gather(
             smalls, wide, [mlp_out], expert_in, expert_out)
         small = small.astype(F32).T
-    small = jnp.concatenate(
-        [small[:4], jnp.zeros((4, width), F32), small[4:], jnp.zeros((124, width), F32)], 0
-    )
-    weights = (wides[0], wides[1], talls[0], wides[2])
-    out = run_forward(images, seq, x0, g4, ids, small, *weights)
-    saved, rows_x, rows_d = out[:16], out[16], out[17]
+        small = jnp.concatenate(
+            [small[:4], jnp.zeros((4, width), F32), small[4:], jnp.zeros((124, width), F32)], 0
+        )
+        weights = (wides[0], wides[1], talls[0], wides[2])
+        out = run_forward(images, seq, x0, g4, ids, small, *weights)
+        saved, rows_x, rows_d = out[:16], out[16], out[17]
 
     def exchange(rows):
         rows = rows.reshape(EXPERTS, SLOT, width)

time: 511 us -> 444 us (0.87)
  Pallas kernels: 471 us -> 402 us
    pallas_call x2 -> x1, Pallas kernels: 73.2 us -> 12 us  [call(): pl.pallas_call(body, out_shape=outs, in_specs=[pl.BlockSpec(memory_space=...]
    pallas_call x1, Pallas kernels: 159 us -> 154 us  [run_front(): pl.pallas_call(functools.partial(front_kernel, images, seq), out_shape=[s...]
where the time goes in v4:
time: 444 us; the launch traced here: 436 us
  Pallas kernels  402 us (91%)
  local copies, waits for them, and re-layouts  27.7 us (6%)
    pallas_call x1, Pallas kernels, run_backward_step(): pl.pallas_call(functools.partial(backward_step, images, seq), out_shape=[...  163 us
    pallas_call x1, Pallas kernels, run_front(): pl.pallas_call(functools.partial(front_kernel, images, seq), out_shape=[s...  154 us
    pallas_call x1, Pallas kernels, run_expert_step(): pl.pallas_call(expert_step, out_shape=[struct(rows, BF16)] * 2 + [struct(...  73.2 us
    pallas_call x1, Pallas kernels, call(): pl.pallas_call(body, out_shape=outs, in_specs=[pl.BlockSpec(memory_space=...  12 us

profile of v4, /device:TPU:0, one launch (start us, length us, event | category | flops | bytes accessed | tf_op | source)
XLA Modules:
  0.0 435.8 jit_solution(17589430510208442028)
XLA Ops:
  0.6 0.0 copy-start.8
  0.7 0.0 copy-start
  0.7 1.5 fusion.11
  2.2 1.1 fusion.12
  3.3 0.0 copy-done.8
  3.4 0.0 copy-done
  3.4 0.8 fusion.10
  4.5 3.1 reshape.91
  7.6 2.0 copy.111
  9.6 0.0 copy-start.4
  9.6 2.1 reshape.88.wide_in
  12.4 0.0 copy-done.4
  12.4 0.0 copy-start.5
  12.4 0.6 broadcast_select_fusion
  12.9 0.1 copy.76
  13.0 0.0 copy-start.6
  13.0 0.9 pad.17.clone
  13.9 0.0 copy-done.5
  13.9 0.1 copy.77
  14.0 0.9 pad.20.clone
  14.8 0.0 copy-done.6
  14.9 0.0 copy-start.13
  14.9 0.0 copy-start.14
  14.9 0.1 copy.112
  15.0 0.0 copy-done.7
  15.0 0.9 pad_maximum_fusion.tall_in
  15.9 0.0 copy-done.9
  15.9 0.1 reshape.79
  16.0 0.1 copy.55
  16.1 0.7 pad.21
  16.8 0.0 copy-done.11
  16.8 0.0 copy-done.12
  16.8 0.0 copy-done.13
  16.8 0.0 copy-done.14
  16.9 0.6 pad_convert_fusion.small_in
  17.5 153.8 %shard_map.229 = (f32[136,768]{1,0:T(8,128)}, bf16[4,2,2,48,3072]{4,3,2,1,0:T(8,128)(2,1)}, bf16[4,2,2,48,3072]{4,3,2,1,0:T(8,128)(2,1)}, bf16[4,2,2,192,768]{4,...) custom-call(f32[8,128]{1,0:T(8,128)} %pad_convert_fusion.small_in, ...), custom_call_target="tpu_custom_call" | custom-call | flops 8999999488 | bytes 60000000 | tf_op jit(solution)/shard_map/pallas_call | solution.py:940
  171.3 73.2 %shard_map.230 = (bf16[4,256,768]{2,1,0:T(8,128)(2,1)}, bf16[4,256,768]{2,1,0:T(8,128)(2,1)}, bf16[2,4,2,2,2,48,768]{6,5,4,3,2,1,0:T(8,128)(2,1)}) custom-call(bf16[4,256,768]{2,1,0:T(8,128)(2,1)} %bitcast.112, bf16[4,256,768]{2,1,0:T(8,128)(2,1)} %bitcast.113, bf16[4,2,2,48,3072]{4,3,2,1,0:T(8,128)(2,1)} %get-tuple-element.55.ein, ...), custom_call_target="tpu_custom_call" | custom-call | flops 30000001024 | bytes 40000000 | tf_op jit(solution)/shard_map/pallas_call | solution.py:1603
  244.6 12.0 %shard_map.231 = (f32[416,768]{1,0:T(8,128)}, f32[416,768]{1,0:T(8,128)}, f32[8,768]{1,0:T(8,128)}) custom-call(bf16[416,768]{1,0:T(8,128)(2,1)} %bitcast.105, f32[136,768]{1,0:T(8,128)} %get-tuple-element.47.small_ref.small, f32[416,768]{1,0:T(8,128)} %get-tuple-element.48.x3_ref, bf16[416,768]{1,0:T(8,128)(2,1)} %get-tuple-element.49.en_ref, ...), custom_call_target="tpu_custom_call" | custom-call | flops 3000000000 | bytes 10616832 | tf_op jit(solution)/shard_map/pallas_call | solution.py:363
  256.6 163.3 %shard_map.232 = (f32[416,768]{1,0:T(8,128)}, f32[8,256]{1,0:T(8,128)}, f32[2,7,24,1536]{3,2,1,0:T(8,128)}, f32[5,96,768]{2,1,0:T(8,128)}) custom-call(f32[416,768]{1,0:T(8,128)} %get-tuple-element.60.g_in, f32[136,768]{1,0:T(8,128)} %get-tuple-element.47.small_ref.small, f32[8,768]{1,0:T(8,128)} %get-tuple-element.61.small_grad_in, ...), custom_call_target="tpu_custom_call" | custom-call | flops 20000000000 | bytes 60000000 | tf_op jit(solution)/shard_map/pallas_call | solution.py:1424
  419.9 1.2 fusion.9
  421.1 0.2 copy.58
  421.3 0.1 copy.79
  421.4 0.2 copy.59
  421.6 0.1 copy.80
  421.7 0.7 copy.63
  422.6 1.0 copy.62
  423.6 0.1 slice_bitcast_fusion
  423.6 0.1 copy.78
  423.7 1.8 copy.64
  425.5 0.0 copy-done.3
  425.5 0.1 slice.104
  425.6 1.6 copy.75
  427.3 0.0 copy-done.2
  427.3 0.1 slice_bitcast_fusion.1
  427.4 1.8 copy.65
  429.1 0.2 copy.60
  429.4 0.8 copy.81
  430.1 0.7 slice_bitcast_fusion.2
  430.9 0.1 dynamic-slice_bitcast_fusion
  430.9 0.6 slice.99
  431.5 0.5 slice_bitcast_fusion.7
  432.0 0.6 slice.88
  432.6 1.3 slice.103
  434.0 1.4 fusion
  (25 shorter events, 0.4 us)
Async XLA Ops:
  0.6 2.7 copy-start.8
  0.7 2.7 copy-start
  9.6 2.7 copy-start.4
  12.4 1.5 copy-start.5
  13.0 1.8 copy-start.6
  13.9 1.1 copy-start.7
  14.8 1.0 copy-start.9
  14.9 2.0 copy-start.11
  14.9 2.0 copy-start.12
  14.9 2.0 copy-start.13
  14.9 2.0 copy-start.14
  421.7 1.8 copy-start.1
  423.7 1.8 copy-start.3
  425.6 1.7 copy-start.2
  427.4 3.5 copy-start.10

commit v5 on v4

--- a/solution.py
+++ b/solution.py
@@ -967,8 +967,12 @@
 
 def fast_front(images, seq, smalls, wide, mlp_out, expert_in, expert_out, x0, g4, ids):
     small = jnp.pad(smalls.astype(F32).T, ((0, 0), (0, 128 - smalls.shape[0])))
-    packed = jnp.concatenate(wide + [expert_in[:, e] for e in range(EXPERTS)], 1).astype(F32)
-    packed = packed.reshape(24, 7, 2, 1536).transpose(2, 0, 1, 3).reshape(2, 24, 7 * 1536)
+    mixed = [wide[0], wide[2]]
+    one = [mixed[0][0][:, :1536], wide[1][:, :1536], mixed[1][0][:, :1536]]
+    two = [mixed[0][0][:, 1536:], mixed[0][1], wide[1][:, 1536:], mixed[1][0][:, 1536:], mixed[1][1]]
+    one += [expert_in[:, e, :1536] for e in range(EXPERTS)]
+    two += [expert_in[:, e, 1536:] for e in range(EXPERTS)]
+    packed = jnp.stack([jnp.concatenate(one, 1), jnp.concatenate(two, 1)]).astype(F32)
     tall = jnp.concatenate([mlp_out[None], expert_out.transpose(1, 0, 2)], 0)
     out = run_front(images, seq, small, packed, tall, x0, g4, ids)
     small, wa0, wmi, wmo, wa1, ein, eout = out[:7]
@@ -1238,13 +1242,13 @@
 
 def backward_step(
     images, seq,
-    g_in, small, small_grad_in, x2, x1, x0, an1, qkv1, o1, mn, slope, ma, an0, qkv0, o0,
+    g4, small, x3, en_src, aux_src, p0_src, p1_src, y_src, d_src, x2, x1, x0, an1, qkv1, o1, mn, slope, ma, an0, qkv0, o0,
     wa1, wmo, wmi, wa0, sums,
-    g_ref, small_out, wide_out, tall_out,
+    x4_ref, g_ref, small_out, wide_out, tall_out,
     xf, low, do, dqkv, dn, an_buf, mix_buf, ds,
     dw_wide, dw_tall, near, first, second, z_dense, own, z_expert, cross, done, small_got,
     load_sems, expert_load_sems, pair_sems, plane_sems, zs_sems, zr_sems, cross_sems, small_sems,
-    meet, stream_sems, credit,
+    meet, stream_sems, combine_sems, credit,
 ):
     p = Place()
     greet_all(p, 32)
@@ -1334,8 +1338,39 @@
 
         pl.run_scoped(scope, pltpu.VMEM((WIDTH, HIDDEN), BF16))
 
-    g_ref[...] = g_in[...]
-    ds[...] = small_grad_in[...]
+    def combine(en, aux_ref, p0, p1, y, d):
+        copies = load([(y_src, y), (p0_src, p0), (p1_src, p1), (x3, xf), (aux_src, aux_ref),
+                       (en_src, en), (d_src, d)], combine_sems)
+        g_ref[...] = g4[...].astype(F32)
+        ds[...] = jnp.zeros_like(ds)
+        expert_of = lax.broadcasted_iota(jnp.int32, (EXPERTS * SLOT, 128), 0) // SLOT
+        spread = (expert_of == lax.broadcasted_iota(jnp.int32, expert_of.shape, 1)).astype(BF16)
+        for copy in copies:
+            copy.wait()
+        aux = aux_ref[...]
+        lane = lax.broadcasted_iota(jnp.int32, aux.shape, 1)
+        dr = jnp.zeros(aux.shape, F32)
+        dn[...] = xf[...]
+        for j, pick in ((0, p0), (1, p1)):
+            picked = nn(pick[...], y[...])
+            dn[...] += aux[:, 8 + j : 9 + j] * picked
+            dr += jnp.sum(g_ref[...] * picked, -1, keepdims=True) * nn(pick[...], spread)
+            pump(*PACE[0])
+        x4_ref[...] = dn[...].astype(BF16)
+        chances = jnp.where(lane < EXPERTS, aux, 0.0)
+        dlogits = chances * (dr - jnp.sum(chances * dr, -1, keepdims=True))
+        dlogits = jnp.where(lane < EXPERTS, dlogits, 0.0).astype(BF16)
+        ds[4:8, :] = tn(dlogits, en[...])[0:4, :]
+        dn[...] = nn(dlogits, small[8:136, :].astype(BF16)) + nn(p0[...] + p1[...], d[...])
+        pump(*PACE[0])
+        norm_back(xf, small[3:4, :], dn, g_ref, ds, 3)
+        pump(*PACE[0])
+
+    rows = g_ref.shape[0]
+    pl.run_scoped(
+        combine, pltpu.VMEM((rows, WIDTH), BF16), pltpu.VMEM((rows, 128), F32),
+        pltpu.VMEM((rows, EXPERTS * SLOT), BF16), pltpu.VMEM((rows, EXPERTS * SLOT), BF16),
+        pltpu.VMEM((EXPERTS * SLOT, WIDTH), BF16), pltpu.VMEM((EXPERTS * SLOT, WIDTH), BF16))
     attention(wa1, x2, an1, qkv1, o1, dw_wide.at[0].reshape(WIDTH, HIDDEN), 1, jobs[2].start,
               lambda: pump(*PACE[0]))
     dense.add(jobs[2])
@@ -1375,7 +1410,6 @@
         norm_back(x1_buf, small[2:3, :], dn, g_ref, ds, 2)
 
     x1_buf = xf
-    rows = g_ref.shape[0]
     pl.run_scoped(
         feed_forward, pltpu.VMEM((2, 512, WIDTH), BF16), pltpu.VMEM((2, WIDTH, 512), BF16),
         pltpu.VMEM((2, rows, 512), BF16), pltpu.VMEM((2, rows, 512), BF16))
@@ -1398,12 +1432,14 @@
     dense.add(jobs[5])
     while dense.done[3] < len(dense.units) or experts.queue:
         pump(*PACE[3])
+    mine = pl.ds(pl.multiple_of(p.core * 1536, 128), 1536)
     swap = remote(
-        done.at[:, pl.ds(pl.multiple_of((1 - p.core) * 24, 8), 24), :], wide_out.at[p.core],
+        done.at[:, pl.ds(pl.multiple_of((1 - p.core) * 24, 8), 24), :], wide_out.at[:, :, mine],
         meet.at[0], meet.at[1], p.sibling)
     swap.start()
     keep = pltpu.make_async_copy(
-        done.at[:, pl.ds(pl.multiple_of(p.core * 24, 8), 24), :], wide_out.at[p.core], meet.at[2])
+        done.at[:, pl.ds(pl.multiple_of(p.core * 24, 8), 24), :], wide_out.at[:, :, mine],
+        meet.at[2])
     keep.start()
     pl.loop(1, 32)(lambda i: small_copy((p.me + i) % 32, i, (p.me + i) % 32).wait())
     small_got[p.me] = ds[:, pl.ds(pl.multiple_of(window(p.me), 128), 256)]
@@ -1423,10 +1459,10 @@
     act, low = pltpu.VMEM((rows, WIDTH), F32), pltpu.VMEM((rows, WIDTH), BF16)
     return pl.pallas_call(
         functools.partial(backward_step, images, seq),
-        out_shape=[struct((rows, WIDTH), F32), struct((8, 256), F32),
-                   struct((2, 7, 24, 1536), F32), struct((5, 96, 768), F32)],
-        in_specs=[vmem] * 3 + [any_space] * (len(args) - 3),
-        out_specs=[vmem, vmem, any_space, vmem],
+        out_shape=[struct((rows, WIDTH), BF16), struct((rows, WIDTH), F32), struct((8, 256), F32),
+                   struct((7, 24, HIDDEN), F32), struct((5, 96, 768), F32)],
+        in_specs=[vmem] * 2 + [any_space] * (len(args) - 2),
+        out_specs=[vmem, vmem, vmem, any_space, vmem],
         scratch_shapes=[
             act, low, low, pltpu.VMEM((rows, 3 * WIDTH), BF16), act, low,
             pltpu.VMEM((rows, HIDDEN), BF16), pltpu.VMEM((8, WIDTH), F32),
@@ -1451,6 +1487,7 @@
             dma((2, 32)),
             dma((3,)),
             dma((2, 4)),
+            dma((7,)),
             pltpu.SemaphoreType.REGULAR,
         ],
         compiler_params=pltpu.CompilerParams(
@@ -1461,22 +1498,13 @@
 
 
 def fast_backward(images, seq, x0, g4, small, weights, saved, y_back, d_back, sums):
-    rows = x0.shape[0]
-    act = struct((rows, WIDTH), F32)
     wa0, wmi, wmo, wa1 = weights
     x1, x2, x3, an0, qkv0, o0, mn, slope, ma, an1, qkv1, o1, en, aux, p0, p1 = saved
-    x4, g, ds = call(
-        combine_kernel, [act, act, struct((8, WIDTH), F32)], [pltpu.VMEM((rows, WIDTH), F32)],
-        [g4, small, x3, en, aux, p0, p1, y_back, d_back], 3_000_000_000,
-    )
-    w = lambda g: g.reshape(4, 2, 2, 48, HIDDEN)
-    t = lambda g: g.reshape(4, 2, 2, 192, WIDTH)
-    g, dsmall, wide, tall = run_backward_step(images, seq, [
-        g, small, ds, x2, x1, x0, an1, qkv1, o1, mn, slope, ma, an0, qkv0, o0,
-        w(wa1), t(wmo), w(wmi), w(wa0), sums])
+    x4, g, dsmall, wide, tall = run_backward_step(images, seq, [
+        g4, small, x3, en, aux, p0, p1, y_back, d_back, x2, x1, x0, an1, qkv1, o1, mn, slope, ma,
+        an0, qkv0, o0, wa1, wmo, wmi, wa0, sums])
     me = lax.axis_index("fsdp")
     dsmall = lax.dynamic_slice(dsmall, (0, me * 24 - window(me)), (8, 24))
-    wide = wide.transpose(1, 2, 0, 3).reshape(7, 24, HIDDEN)
     return x4, g, (dsmall.T, wide[0], wide[1], tall[0], wide[2],
                    wide[3:].transpose(1, 0, 2), tall[1:].transpose(1, 0, 2))
 
@@ -1655,14 +1683,14 @@
     smalls = jnp.concatenate(
         [attn_gain, mlp_gain[:, None], moe_gain[:, None], router], 1
     )
-    wide = [jnp.concatenate([attn_qkv[:, 0], attn_out[:, 0]], 1), mlp_in,
-            jnp.concatenate([attn_qkv[:, 1], attn_out[:, 1]], 1)]
+    wide = [(attn_qkv[:, 0], attn_out[:, 0]), mlp_in, (attn_qkv[:, 1], attn_out[:, 1])]
     if n == 32:
         small, weights, w_in, w_out, saved, rows_x, rows_d = fast_front(
             images, seq, smalls, wide, mlp_out, expert_in, expert_out, x0, g4, ids)
     else:
         small, wides, talls, w_in, w_out = plain_gather(
-            smalls, wide, [mlp_out], expert_in, expert_out)
+            smalls, [jnp.concatenate(wide[0], 1), mlp_in, jnp.concatenate(wide[2], 1)],
+            [mlp_out], expert_in, expert_out)
         small = small.astype(F32).T
         small = jnp.concatenate(
             [small[:4], jnp.zeros((4, width), F32), small[4:], jnp.zeros((124, width), F32)], 0

time: 444 us -> 430 us (0.968)
  local copies, waits for them, and re-layouts: 27.7 us -> 17.3 us
  Pallas kernels: 402 us -> 397 us
    pallas_call x1 -> x0, Pallas kernels: 12 us -> none  [call(): pl.pallas_call(body, out_shape=outs, in_specs=[pl.BlockSpec(memory_space=...]
    reshape x3 -> x0, local copies, waits for them, and re-layouts: 7.22 us -> none  [fast_front(): packed.reshape(24, 7, 2, 1536).transpose(2, 0, 1, 3)]
    pallas_call x1, Pallas kernels: 163 us -> 170 us  [run_backward_step(): pl.pallas_call(functools.partial(backward_step, images, seq), out_shape=[...]
where the time goes in v5:
time: 430 us; the launch traced here: 421 us
  Pallas kernels  397 us (92%)
  local copies, waits for them, and re-layouts  17.3 us (4%)
  other arithmetic  5.08 us (1%)
    pallas_call x1, Pallas kernels, run_backward_step(): pl.pallas_call(functools.partial(backward_step, images, seq), out_shape=[...  170 us
    pallas_call x1, Pallas kernels, run_front(): pl.pallas_call(functools.partial(front_kernel, images, seq), out_shape=[s...  154 us
    pallas_call x1, Pallas kernels, run_expert_step(): pl.pallas_call(expert_step, out_shape=[struct(rows, BF16)] * 2 + [struct(...  72.8 us

profile of v5, /device:TPU:0, one launch (start us, length us, event | category | flops | bytes accessed | tf_op | source)
XLA Modules:
  0.0 421.5 jit_solution(5378307842095171767)
XLA Ops:
  0.6 0.0 copy-start.8
  0.7 0.0 copy-start.10
  0.7 0.0 copy-start
  0.7 1.5 fusion.11
  2.2 0.0 copy-done.8
  2.2 0.1 fusion.12
  2.4 0.0 copy-done.10
  2.4 0.0 copy-done
  2.4 0.9 fusion.10
  3.5 0.0 copy-start.4
  3.5 1.4 maximum_convert_fusion.wide_in
  5.6 0.0 copy-done.4
  5.6 0.0 copy-start.5
  5.7 0.6 broadcast_select_fusion.1
  6.2 0.1 copy.62
  6.3 0.0 copy-start.7
  6.3 0.9 pad.17.clone
  7.2 0.0 copy-done.5
  7.2 0.0 copy-start.9
  7.2 0.1 copy.63
  7.3 0.9 pad.20.clone
  8.1 0.0 copy-start.11
  8.1 0.0 copy-done.7
  8.1 0.0 copy-start.15
  8.2 0.0 copy-start.16
  8.2 0.1 copy.98
  8.2 0.0 copy-done.9
  8.2 0.9 pad_maximum_fusion.tall_in
  9.2 0.0 copy-done.11
  9.2 0.1 reshape.60
  9.3 0.1 copy.41
  9.4 0.7 pad.21
  10.1 0.0 copy-done.13
  10.1 0.0 copy-done.14
  10.1 0.0 copy-done.15
  10.1 0.0 copy-done.16
  10.1 0.6 pad_convert_fusion.small_in
  10.7 153.9 %shard_map.229 = (f32[136,768]{1,0:T(8,128)}, bf16[4,2,2,48,3072]{4,3,2,1,0:T(8,128)(2,1)}, bf16[4,2,2,48,3072]{4,3,2,1,0:T(8,128)(2,1)}, bf16[4,2,2,192,768]{4,...) custom-call(f32[8,128]{1,0:T(8,128)} %pad_convert_fusion.small_in, ...), custom_call_target="tpu_custom_call" | custom-call | flops 8999999488 | bytes 60000000 | tf_op jit(solution)/shard_map/pallas_call | solution.py:940
  164.6 72.8 %shard_map.230 = (bf16[4,256,768]{2,1,0:T(8,128)(2,1)}, bf16[4,256,768]{2,1,0:T(8,128)(2,1)}, bf16[2,4,2,2,2,48,768]{6,5,4,3,2,1,0:T(8,128)(2,1)}) custom-call(bf16[4,256,768]{2,1,0:T(8,128)(2,1)} %bitcast.108, bf16[4,256,768]{2,1,0:T(8,128)(2,1)} %bitcast.109, bf16[4,2,2,48,3072]{4,3,2,1,0:T(8,128)(2,1)} %get-tuple-element.53.ein, ...), custom_call_target="tpu_custom_call" | custom-call | flops 30000001024 | bytes 40000000 | tf_op jit(solution)/shard_map/pallas_call | solution.py:1631
  237.4 170.3 %shard_map.231 = (bf16[416,768]{1,0:T(8,128)(2,1)}, f32[416,768]{1,0:T(8,128)}, f32[8,256]{1,0:T(8,128)}, f32[7,24,3072]{2,1,0:T(8,128)}, f32[5,96,768]{2,1,0:T(8,128)}) custom-call(bf16[416,768]{1,0:T(8,128)(2,1)} %bitcast.97, f32[136,768]{1,0:T(8,128)} %get-tuple-element.45.small, f32[416,768]{1,0:T(8,128)} %get-tuple-element.46.x3, ...), custom_call_target="tpu_custom_call" | custom-call | flops 20000000000 | bytes 60000000 | tf_op jit(solution)/shard_map/pallas_call | solution.py:1460
  407.8 1.9 slice_bitcast_fusion.3
  409.7 0.0 copy-start.3
  409.7 0.7 copy.45
  410.6 1.0 copy.44
  411.6 0.0 copy-done.3
  411.6 0.1 slice.141
  411.6 0.0 copy-start.1
  411.7 1.6 copy.61
  413.3 0.0 copy-done.1
  413.3 0.1 slice_bitcast_fusion.1
  413.4 0.0 copy-start.2
  413.4 1.8 copy.46
  415.2 0.0 copy-done.2
  415.2 0.1 slice_bitcast_fusion
  415.3 0.0 copy-start.6
  415.3 1.8 copy.47
  417.1 0.0 copy-done.6
  417.1 1.5 broadcast_select_fusion
  418.6 0.7 slice_bitcast_fusion.2
  419.3 0.0 copy-done.12
  419.3 0.1 dynamic-slice_bitcast_fusion
  419.4 0.6 slice.133
  420.0 0.5 slice_bitcast_fusion.10
  420.5 0.6 slice.122
  (28 shorter events, 0.4 us)
Async XLA Ops:
  0.6 1.6 copy-start.8
  0.7 1.7 copy-start.10
  0.7 1.8 copy-start
  3.5 2.1 copy-start.4
  5.6 1.5 copy-start.5
  6.3 1.8 copy-start.7
  7.2 1.1 copy-start.9
  8.1 1.0 copy-start.11
  8.1 2.0 copy-start.13
  8.1 2.0 copy-start.14
  8.1 2.0 copy-start.15
  8.2 2.0 copy-start.16
  409.7 1.9 copy-start.3
  411.6 1.7 copy-start.1
  413.4 1.8 copy-start.2
  415.3 1.8 copy-start.6
  417.1 2.3 copy-start.12
